TPU v7x, 128 devices: a whole 4x4x4 slice. The times are simulated.
128 devices in a mesh: dp: 8 (over z_lo, y), ctx: 16 (over x, z_hi, core).
Axes of the slice: x: 4, y: 4, z: 4 (z_hi: 2, z_lo: 2; z = z_hi * 2 + z_lo), core: 2. Of those that a mesh axis runs over, the one named last changes fastest.
Arguments:
- tokens: bfloat16 [32, 4096, 768], P('dp', 'ctx'), may hold values from -6 to 6
- w_qkv: bfloat16 [768, 2304], replicated, may hold values from -0.21650635 to 0.21650635
- w_out: bfloat16 [768, 768], replicated, may hold values from -0.21875 to 0.21875
- ln_gain: float32 [768], replicated, may hold values from 0.25 to 1.75
- cache: bfloat16 [16384, 768], P(('dp', 'ctx')), may hold values from -0.5051815 to 0.5051815
- positive: int32 [32], replicated, may hold values from 0 to 16383
- lengths: int32 [32], P('dp'), may hold values from 2048 to 4096, as said below
Outputs:
- hidden: bfloat16 [32, 4096, 768], P('dp', 'ctx')
- loss: float32 [], replicated
- grad_out: float32 [768, 768], P(('dp', 'ctx'))
Inputs may be any that keep to these rules, and one draw needn't show every extreme that they name: `lengths`: some document has exactly 4096 valid tokens in every draw.
All inputs are finite; a program needn't handle non-finite values.
Results may differ from a plain program's by a relative error of at most 0.003.
The roundings to bfloat16 on the way count: a program that leaves them out, or rounds other values in their place, can miss the bound.
Values may be sent and summed in bfloat16 or wider, within the bound.
No kernel may reach another device: no remote copies, remote signals or barrier semaphores. Data moves between devices by JAX's collectives and lax.ppermute only.
A program may use at most 128 MiB of HBM per device.

v0:
```python
import functools
import math

import jax
import jax.numpy as jnp
from jax import lax
from jax.experimental import pallas as pl
from jax.experimental.pallas import tpu as pltpu
from jax.sharding import PartitionSpec as P

H = 12
WIN = 256
TAU = 0.02
FAR = 1e32
CHUNK = 2
NT = (((1,), (1,)), ((), ()))
TN = (((0,), (0,)), ((), ()))
HIGHEST = lax.Precision.HIGHEST
VMEM = pl.BlockSpec(memory_space=pltpu.VMEM)
SMEM = pl.BlockSpec(memory_space=pltpu.SMEM)
ANY = pl.BlockSpec(memory_space=pl.ANY)


def swap(value, axis, bits):
    return lax.ppermute(value, axis, [(i, i ^ bits) for i in range(lax.axis_size(axis))])


def from_x(value, k):
    size = lax.axis_size("ctx")
    return lax.ppermute(value, "ctx", [((c + 4 * k) % size, c) for c in range(size)])


def from_y(value, k):
    return lax.ppermute(value, "dp", [((d & 4) | ((d + k) & 3), d) for d in range(lax.axis_size("dp"))])


def from_z(value, k):
    n_dp, n_ctx = lax.axis_size("dp"), lax.axis_size("ctx")
    pairs = []
    for d in range(n_dp):
        for c in range(n_ctx):
            z = ((c & 2) + (d >> 2) + k) & 3
            pairs.append((((z & 1) * 4 + (d & 3)) * n_ctx + (c & ~2) + (z & 2), d * n_ctx + c))
    return lax.ppermute(value, ("dp", "ctx"), pairs)


def around(value, fetch):
    return [value] + [fetch(value, k) for k in (1, 2, 3)]


def call(kernel, out_shape, in_specs, out_specs, limit=24, flops=0, moved=0, **keywords):
    return pl.pallas_call(
        kernel,
        out_shape=out_shape,
        in_specs=in_specs,
        out_specs=out_specs,
        compiler_params=pltpu.CompilerParams(vmem_limit_bytes=limit * 2**20),
        cost_estimate=pl.CostEstimate(flops=flops, bytes_accessed=moved, transcendentals=0),
        **keywords,
    )


def f32(*shape):
    return jax.ShapeDtypeStruct(shape, jnp.float32)


def bf16(*shape):
    return jax.ShapeDtypeStruct(shape, jnp.bfloat16)


def slopes_of(heads):
    largest = 2 ** int(math.floor(math.log2(heads)))
    listed = [2.0 ** (-8.0 * (h + 1) / largest) for h in range(largest)]
    return listed + [2.0 ** (-4.0 * (2 * m + 1) / largest) for m in range(heads - largest)]


def thirds(value):
    high = value.astype(jnp.bfloat16)
    rest = value - high.astype(jnp.float32)
    middle = rest.astype(jnp.bfloat16)
    low = (rest - middle.astype(jnp.float32)).astype(jnp.bfloat16)
    parts = [p.astype(jnp.float32) for p in (high, middle, low)]
    return jnp.concatenate(parts, axis=0).astype(jnp.bfloat16)


def folded(products):
    rows = products.shape[0] // 3
    return products[0:rows] + products[rows : 2 * rows] + products[2 * rows :]


def attend_kernel(
    first, me, lengths, tok, left, right, qk, v_turned, w_k, w_v_turned, w_out, gain, *refs
):
    hidden, mixed, normed, rstd_out, pool, keys, values, dist = refs[-8:]
    tb, width = tok.shape[1:]
    ext = tb + 2 * WIN
    start, length = me[1] * tb, lengths[first + pl.program_id(0)]
    rows = jnp.concatenate([left[0], right[0]], axis=0)
    new = jnp.dot(rows, w_k[...], preferred_element_type=jnp.float32).astype(jnp.bfloat16)
    keys[0:WIN] = new[0:WIN]
    keys[WIN : WIN + tb] = qk[0, :, width:]
    keys[WIN + tb :] = new[WIN:]
    new = lax.dot_general(w_v_turned[...], rows, NT, preferred_element_type=jnp.float32).astype(jnp.bfloat16)
    values[:, 0:WIN] = new[:, 0:WIN]
    values[:, WIN : WIN + tb] = v_turned[...]
    values[:, WIN + tb :] = new[:, WIN:]
    j = lax.broadcasted_iota(jnp.int32, (ext, tb), 0) - WIN
    away = jnp.abs(lax.broadcasted_iota(jnp.int32, (ext, tb), 1) - j)
    kpos = start + j
    seen = (away <= WIN) & (((kpos >= 0) & (kpos < length)) | (away == 0))
    dist[...] = jnp.where(seen, away.astype(jnp.float32), FAR)
    half = lax.broadcasted_iota(jnp.int32, (tb, 128), 1) < 64
    slopes = slopes_of(H)
    lanes = 128
    span = lanes + 2 * WIN
    for pair in range(H // 2):
        cols = pl.ds(pair * 128, 128)
        query = qk[0, :, cols] * jnp.bfloat16(0.125)
        zero = jnp.bfloat16(0)
        both = jnp.concatenate([jnp.where(half, query, zero), jnp.where(half, zero, query)], axis=0)
        scores = lax.dot_general(keys[:, cols], both, NT, preferred_element_type=jnp.float32)
        for part in range(2):
            columns = []
            for low in range(0, tb, lanes):
                score = scores[low : low + span, part * tb + low : part * tb + low + lanes]
                score = score - slopes[2 * pair + part] * dist[pl.ds(low, span), pl.ds(low, lanes)]
                expo = jnp.exp(score - jnp.max(score, axis=0, keepdims=True))
                weights = (expo * (1.0 / jnp.sum(expo, axis=0, keepdims=True))).astype(jnp.bfloat16)
                above, below = low, ext - span - low
                pieces = [weights]
                if above:
                    pieces = [jnp.zeros((above, lanes), jnp.bfloat16)] + pieces
                if below:
                    pieces = pieces + [jnp.zeros((below, lanes), jnp.bfloat16)]
                columns.append(jnp.concatenate(pieces, axis=0))
            weights = jnp.concatenate(columns, axis=1)
            head = pl.ds(pair * 128 + part * 64, 64)
            mixed[head, :] = jnp.dot(values[head, :], weights, preferred_element_type=jnp.float32).astype(jnp.bfloat16)
    summed = tok[0].astype(jnp.float32) + lax.dot_general(mixed[...], w_out[...], TN, preferred_element_type=jnp.float32)
    centred = summed - jnp.mean(summed, axis=1, keepdims=True)
    rstd = lax.rsqrt(jnp.mean(centred * centred, axis=1, keepdims=True) + 1e-05)
    unit = centred * rstd
    hidden_f = unit * gain[...]
    hidden[0] = hidden_f.astype(jnp.bfloat16)
    normed[0] = unit.astype(jnp.bfloat16)
    rstd_out[0] = jnp.broadcast_to(rstd, rstd_out.shape[1:])
    keep = start + lax.broadcasted_iota(jnp.int32, (tb, 1), 0) < length
    pool[0] = jnp.sum(jnp.where(keep, hidden_f, 0.0), axis=0, keepdims=True)


def attend(first, before, me, lengths, tokens, left, right, qk, v_turned, w_qkv, w_v_turned, w_out, gain):
    docs, tb, width = tokens.shape
    ext = tb + 2 * WIN
    here = lambda *s: pl.BlockSpec((1,) + s, lambda i: (first + i, 0, 0))
    chunk = lambda *s: pl.BlockSpec((1,) + s, lambda i: (i, 0, 0))
    column = pl.BlockSpec((width, tb), lambda i: (0, first + i))
    fixed = lambda s, at=(0, 0): pl.BlockSpec(s, lambda i: at, pipeline_mode=pl.Buffered(1))
    out_shape = (bf16(docs, tb, width), bf16(width, docs * tb), bf16(docs, tb, width), f32(docs, tb, 128), f32(docs, 1, width))
    in_specs = [
        SMEM, SMEM, here(tb, width), chunk(WIN, width), chunk(WIN, width), here(tb, 2 * width), column,
        fixed((width, width), (0, 1)), fixed((width, width)), fixed((width, width)), fixed((1, width)),
    ]
    operands = [me, lengths, tokens, left, right, qk, v_turned, w_qkv, w_v_turned, w_out, gain]
    aliases = {}
    if before is not None:
        aliases = {len(operands) + k: k for k in range(len(out_shape))}
        operands = operands + list(before)
        in_specs = in_specs + [ANY] * len(out_shape)
    return call(
        functools.partial(attend_kernel, first),
        out_shape,
        in_specs,
        (here(tb, width), column, here(tb, width), here(tb, 128), here(1, width)),
        limit=32,
        flops=CHUNK * 5 * 2 * tb * ext * width,
        moved=8 * 2**20,
        grid=(CHUNK,),
        scratch_shapes=[
            pltpu.VMEM((ext, width), jnp.bfloat16),
            pltpu.VMEM((width, ext), jnp.bfloat16),
            pltpu.VMEM((ext, tb), jnp.float32),
        ],
        input_output_aliases=aliases,
        name="attend",
    )(*operands)


def row_ids(me, k, rows, shape, dim):
    place = lax.broadcasted_iota(jnp.int32, shape, dim)
    y, z_lo = (me[0] + k) & 3, me[0] >> 2
    other = (place >= rows).astype(jnp.int32)
    owner = (z_lo + other - 2 * z_lo * other) * 4 + y
    return (owner * 16 + me[1]) * rows + place - other * rows


def target_kernel(docs, me, positive, *refs):
    pieces, out = refs[:4], refs[4]
    total = jnp.zeros(out.shape, jnp.float32)
    for k, piece in enumerate(pieces):
        rows = piece.shape[0]
        ids = row_ids(me, k, rows // 2, (8, rows), 1)
        doc = lax.broadcasted_iota(jnp.int32, (8, rows), 0)
        wanted = jnp.full((8, rows), -1, jnp.int32)
        for d in range(docs):
            wanted = jnp.where(doc == d, positive[me[0] * docs + d], wanted)
        hit = (ids == wanted).astype(jnp.float32).astype(jnp.bfloat16)
        total = total + jnp.dot(hit, piece[...], preferred_element_type=jnp.float32)[0:docs]
    out[...] = total


def norm_kernel(lengths, mine, other, emb_out, rinv_out, target_out):
    docs = emb_out.shape[0]
    both = mine[...] + other[...]
    row = lax.broadcasted_iota(jnp.int32, (docs, 128), 0)
    count = jnp.zeros((docs, 128), jnp.float32)
    for d in range(docs):
        count = jnp.where(row == d, lengths[d].astype(jnp.float32), count)
    pooled = both[0:docs] / count[:, 0:1]
    rinv = lax.rsqrt(jnp.sum(pooled * pooled, axis=1, keepdims=True) + 1e-06)
    emb_out[...] = pooled * rinv
    rinv_out[...] = jnp.broadcast_to(rinv, rinv_out.shape)
    target_out[...] = both[docs:]


def as_row(column):
    size = column.shape[0]
    same = lax.broadcasted_iota(jnp.int32, (size, size), 0) == lax.broadcasted_iota(jnp.int32, (size, size), 1)
    return jnp.sum(jnp.where(same, column, 0.0), axis=0, keepdims=True)


def score_kernel(docs, me, positive, e0, e1, e2, e3, t0, t1, t2, t3, everyone, state, expos):
    all_docs, width = everyone.shape
    y, z_lo = me[0] & 3, me[0] >> 2
    for k, piece in enumerate((e0, e1, e2, e3)):
        value = piece[...]
        turned = jnp.concatenate([value[docs:], value[0:docs]], axis=0)
        place = pl.multiple_of(((y + k) & 3) * 2 * docs, 2 * docs)
        everyone[pl.ds(place, 2 * docs), :] = jnp.where(z_lo == 1, turned, value)
    tables = (t0, t1, t2, t3)
    rows = t0.shape[0]
    emb = thirds(everyone[...])
    scores = [folded(lax.dot_general(emb, t[...], NT, preferred_element_type=jnp.float32)) / TAU for t in tables]
    tops = [jnp.max(s, axis=1, keepdims=True) for s in scores]
    top = jnp.maximum(jnp.maximum(tops[0], tops[2]), jnp.maximum(tops[1], tops[3]))
    totals, found = [], jnp.zeros((all_docs, 1), jnp.float32)
    for k, s in enumerate(scores):
        expo = jnp.exp(s - top)
        expos[:, k * rows : (k + 1) * rows] = expo
        halves = [jnp.sum(expo[:, h : h + rows // 2], axis=1, keepdims=True) for h in (0, rows // 2)]
        totals.append(halves[0] + halves[1])
        hit = row_ids(me, k, rows // 2, (all_docs, rows), 1) == positive[...]
        found = found + jnp.sum(jnp.where(hit, s, 0.0), axis=1, keepdims=True)
    total = (totals[0] + totals[2]) + (totals[1] + totals[3])
    place = pl.multiple_of(y * 2 * docs, 2 * docs)
    mine = thirds(expos[pl.ds(place, 2 * docs), :])
    mix = jnp.zeros((2 * docs, width), jnp.float32)
    for k, t in enumerate(tables):
        mix = mix + folded(jnp.dot(mine[:, k * rows : (k + 1) * rows], t[...], preferred_element_type=jnp.float32))
    column = lax.broadcasted_iota(jnp.int32, (docs, all_docs), 1)
    own = column == lax.broadcasted_iota(jnp.int32, (docs, all_docs), 0) + y * 2 * docs + z_lo * docs
    total_row, top_row, found_row = as_row(total), as_row(top), as_row(found)
    state[...] = jnp.zeros_like(state)
    state[0:docs, 0:width] = jnp.where(z_lo == 1, mix[docs:], mix[0:docs])
    for place, row in ((width, total_row), (width + 128, top_row)):
        value = jnp.sum(jnp.where(own, row, 0.0), axis=1, keepdims=True)
        state[0:docs, place : place + 128] = jnp.broadcast_to(value, (docs, 128))
    for index, row in enumerate((total_row, top_row, found_row)):
        state[docs + index : docs + index + 1, 0:all_docs] = row


def merge(docs, width, states):
    row = lax.broadcasted_iota(jnp.int32, states[0].shape, 0)
    column = lax.broadcasted_iota(jnp.int32, states[0].shape, 1)
    place = width + 128
    by_row = [s[:, place : place + 1] for s in states]
    by_lane = [s[docs + 1 : docs + 2, :] for s in states]
    top_row = functools.reduce(jnp.maximum, by_row)
    top_lane = functools.reduce(jnp.maximum, by_lane)
    terms = [
        s * jnp.exp(jnp.where(row == docs, b - top_lane, a - top_row)) for s, a, b in zip(states, by_row, by_lane)
    ]
    if len(terms) == 4:
        terms = [terms[0] + terms[2], terms[1] + terms[3]]
    joined = jnp.where((row < docs) & (column >= place), top_row, terms[0] + terms[1])
    return jnp.where(row == docs + 1, top_lane, joined)


def batch_kernel(docs, me, emb, everyone, product_out, stats):
    everything = everyone[...]
    all_docs = everything.shape[0]
    own = lax.dot_general(emb[...], everything, NT, precision=HIGHEST, preferred_element_type=jnp.float32) / TAU
    product = lax.dot_general(everything, everything, NT, precision=HIGHEST, preferred_element_type=jnp.float32) / TAU
    wide = (all_docs, all_docs)
    same = lax.broadcasted_iota(jnp.int32, wide, 0) == lax.broadcasted_iota(jnp.int32, wide, 1)
    product = jnp.where(same, -1e30, product)
    top = jnp.max(product, axis=0, keepdims=True)
    total = jnp.sum(jnp.exp(product - top), axis=0, keepdims=True)
    product_out[...] = own
    stats[...] = jnp.concatenate([top, total] * 4, axis=0)


def grad_kernel(
    me, lengths, state, emb, rinv, everyone, target, product, stats, gain, normed, rstd, turned,
    keep_out, send_out, loss_out, d_summed,
):
    docs, width = emb.shape
    all_docs = everyone.shape[0]
    y, z_lo = me[0] & 3, me[0] >> 2
    own, others, now = emb[...], everyone[...], state[...]
    total, top, found = (now[docs + k : docs + k + 1, 0:all_docs] for k in range(3))
    batch_top, batch_total = stats[0:1], stats[1:2]
    peak = jnp.maximum(top, batch_top)
    lse_row = peak + jnp.log(total * jnp.exp(top - peak) + batch_total * jnp.exp(batch_top - peak))
    loss_out[...] = jnp.broadcast_to(jnp.sum(lse_row - found, axis=1, keepdims=True) / all_docs, loss_out.shape)
    column = lax.broadcasted_iota(jnp.int32, (docs, all_docs), 1)
    same = column == lax.broadcasted_iota(jnp.int32, (docs, all_docs), 0) + y * 2 * docs + z_lo * docs
    lse = jnp.sum(jnp.where(same, lse_row, 0.0), axis=1, keepdims=True)
    scores = product[...]
    g_batch = jnp.where(same, 0.0, jnp.exp(scores - lse) + jnp.exp(scores - lse_row)) / all_docs
    mix = now[0:docs, 0:width] * jnp.exp(now[0:docs, width + 128 : width + 129] - lse)
    from_batch = jnp.dot(g_batch, others, precision=HIGHEST, preferred_element_type=jnp.float32)
    d_emb = ((mix - target[...]) / all_docs + from_batch) / TAU
    d_pooled = (d_emb - own * jnp.sum(own * d_emb, axis=1, keepdims=True)) * rinv[:, 0:1]
    tb = normed.shape[1]
    for doc in range(docs):
        dy = d_pooled[doc : doc + 1] / lengths[doc].astype(jnp.float32) * gain[...]
        level = dy - jnp.mean(dy, axis=1, keepdims=True)
        unit = normed[doc].astype(jnp.float32)
        along = jnp.mean(unit * dy, axis=1, keepdims=True)
        keep = me[1] * tb + lax.broadcasted_iota(jnp.int32, (tb, 1), 0) < lengths[doc]
        scale = jnp.where(keep, rstd[doc, :, 0:1], 0.0)
        d_summed[doc * tb : (doc + 1) * tb, :] = (scale * (level - unit * along)).astype(jnp.bfloat16)
    half = width // 2
    send_out[...] = jnp.dot(turned[half:], d_summed[...], preferred_element_type=jnp.float32)
    keep_out[...] = jnp.dot(turned[0:half], d_summed[...], preferred_element_type=jnp.float32)


def sum_kernel(count, *refs):
    terms, outs = refs[:count], refs[count:]
    total = terms[0][...].astype(jnp.float32)
    for term in terms[1:]:
        total = total + term[...].astype(jnp.float32)
    rows = outs[0].shape[0]
    for index, out in enumerate(outs):
        out[...] = total[index * rows : (index + 1) * rows].astype(out.dtype)


def sum_and_split(terms, kind):
    rows, width = terms[0].shape
    piece = (rows // 4, width)
    shapes = (f32(*piece),) + (jax.ShapeDtypeStruct(piece, kind),) * 3
    return call(
        functools.partial(sum_kernel, len(terms)), shapes, [VMEM] * len(terms), (VMEM,) * 4, limit=8, name="sum_split"
    )(*terms)


def shards(tokens, w_qkv, w_out, ln_gain, cache, positive, lengths):
    docs, tb, width = tokens.shape
    n_ctx, n_dp = lax.axis_size("ctx"), lax.axis_size("dp")
    devices = n_dp * n_ctx
    dp, ctx = lax.axis_index("dp"), lax.axis_index("ctx")
    me = jnp.stack([dp, ctx]).astype(jnp.int32)
    all_docs = n_dp * docs
    halos = []
    for first in range(0, docs, CHUNK):
        part = tokens[first : first + CHUNK]
        left = lax.ppermute(part, "ctx", [(i, i + 1) for i in range(n_ctx - 1)])
        right = lax.ppermute(part, "ctx", [(i + 1, i) for i in range(n_ctx - 1)])
        halos.append((left, right))
    tables = around(jnp.concatenate([cache, swap(cache, "dp", 4)], axis=0), from_y)
    target = call(
        functools.partial(target_kernel, docs), f32(docs, width), [SMEM, SMEM] + [VMEM] * 4, VMEM, name="target"
    )(me, positive, *tables)

    gain = ln_gain.reshape(1, width)
    flat = tokens.reshape(docs * tb, width)
    w_v_turned = w_qkv[:, 2 * width :].T
    qk = jnp.dot(flat, w_qkv[:, : 2 * width], preferred_element_type=jnp.float32).astype(jnp.bfloat16)
    v_turned = lax.dot_general(w_v_turned, flat, NT, preferred_element_type=jnp.float32).astype(jnp.bfloat16)
    qk = qk.reshape(docs, tb, 2 * width)
    done = None
    for index, (left, right) in enumerate(halos):
        done = attend(
            index * CHUNK, done, me, lengths, tokens, left, right, qk, v_turned, w_qkv, w_v_turned, w_out, gain
        )
    hidden, mixed, normed, rstd, pool = done

    place = jnp.arange(width, dtype=jnp.int32)
    each = width // devices
    core = (ctx & 1) ^ (place // (64 * each))
    y = ((dp & 3) + place // (16 * each) % 4) & 3
    x = ((ctx >> 2) + place // (4 * each) % 4) & 3
    z = ((ctx & 2) + (dp >> 2) + place // each % 4) & 3
    block = ((z & 1) * 4 + y) * n_ctx + x * 4 + (z >> 1) * 2 + core
    chosen = ((block * each + place % each)[:, None] == place[None, :]).astype(jnp.bfloat16)
    turned = jnp.dot(chosen, mixed, preferred_element_type=jnp.float32).astype(jnp.bfloat16)

    sums = jnp.concatenate([pool.reshape(docs, width), target], axis=0)
    sums = sums + swap(sums, "ctx", 1)
    terms = around(sums, from_x)
    sums = (terms[0] + terms[2]) + (terms[1] + terms[3])
    emb, rinv, target = call(
        norm_kernel,
        (f32(docs, width), f32(docs, 128), f32(docs, width)),
        [SMEM, VMEM, VMEM],
        (VMEM,) * 3,
        limit=4,
        name="norm",
    )(lengths, sums, swap(sums, "ctx", 2))
    embs = around(jnp.concatenate([emb, swap(emb, "dp", 4)], axis=0), from_y)
    wanted = positive.reshape(2, 4, docs).transpose(1, 0, 2).reshape(all_docs, 1)
    everyone, state = call(
        functools.partial(score_kernel, docs),
        (f32(all_docs, width), f32(2 * docs, width + 256)),
        [SMEM] + [VMEM] * 9,
        (VMEM, VMEM),
        moved=2 * 2**20,
        scratch_shapes=[pltpu.VMEM((all_docs, n_dp * cache.shape[0]), jnp.float32)],
        name="score",
    )(me, wanted, *embs, *tables)
    product, stats = call(
        functools.partial(batch_kernel, docs),
        (f32(docs, all_docs), f32(8, all_docs)),
        [SMEM, VMEM, VMEM],
        (VMEM, VMEM),
        limit=4,
        name="batch",
    )(me, emb, everyone)
    state = merge(docs, width, [state, swap(state, "ctx", 1)])
    state = merge(docs, width, around(state, from_x))
    state = merge(docs, width, [state, swap(state, "ctx", 2)])
    half = width // 2
    keep, send, loss = call(
        grad_kernel,
        (f32(half, width), f32(half, width), f32(8, 128)),
        [SMEM, SMEM] + [VMEM] * 11,
        (VMEM,) * 3,
        flops=2 * docs * tb * width * width,
        moved=8 * 2**20,
        scratch_shapes=[pltpu.VMEM((docs * tb, width), jnp.bfloat16)],
        name="grad",
    )(me, lengths, state, emb, rinv, everyone, target, product, stats, gain, normed, rstd, turned)
    keep, *sends = sum_and_split([keep, swap(send, "ctx", 1)], jnp.bfloat16)
    got = [from_y(piece, -(k + 1)) for k, piece in enumerate(sends)]
    keep, *sends = sum_and_split([keep] + got, jnp.float32)
    got = [from_x(piece, -(k + 1)) for k, piece in enumerate(sends)]
    keep, *sends = sum_and_split([keep] + got, jnp.float32)
    got = [from_z(piece, -(k + 1)) for k, piece in enumerate(sends)]
    return (hidden, loss[0, 0], keep + got[0] + got[1] + got[2])


def solution(mesh):
    placed = (P("dp", "ctx", None), P(), P(), P(), P(("dp", "ctx"), None), P(), P("dp"))
    return jax.shard_map(
        shards,
        mesh=mesh,
        in_specs=placed,
        out_specs=(P("dp", "ctx", None), P(), P(("dp", "ctx"), None)),
        check_vma=False,
    )
```

profile of v0, /device:TPU:0, one launch (start us, length us, event | category | flops | bytes accessed | tf_op | source)
XLA Modules:
  0.0 164.6 jit_solution(75869411271088663)
XLA Ops:
  0.6 2.1 %collective-permute-start.4 = (bf16[128,768]{1,0:T(8,128)(2,1)}, bf16[128,768]{1,0:T(8,128)(2,1)S(1)}, u32[]{:S(2)}, u32[]{:S(2)}) collective-permute-start(bf16[128,768]{1,0:T(8,128)(2,1)} %param.11), channel_id=1, source_target_pairs={{0,64},{16,80},{32,96},{48,112},{64,0},{80,16},{96,32},{112,48},{1... | collective-permute-start | bytes 589832 | tf_op jit(solution)/shard_map/ppermute | solution.py:25
  2.7 1.7 %constant_dynamic-update-slice_fusion.1 = bf16[256,768]{1,0:T(8,128)(2,1)} fusion(bf16[128,768]{1,0:T(8,128)(2,1)} %param.11), kind=kLoop, calls=%fused_computation.26 | loop fusion | bytes 393216
  4.4 3.4 %collective-permute-done.4 = bf16[128,768]{1,0:T(8,128)(2,1)S(1)} collective-permute-done((bf16[128,768]{1,0:T(8,128)(2,1)}, bf16[128,768]{1,0:T(8,128)(2,1)S(1)}, u32[]{:S(2)}, u32[]{:S(2)}) %collective-permute-start.4) | collective-permute-done | bytes 196640 | tf_op jit(solution)/shard_map/ppermute | solution.py:25
  8.5 3.0 %collective-permute-start.5 = (bf16[256,768]{1,0:T(8,128)(2,1)}, bf16[256,768]{1,0:T(8,128)(2,1)S(1)}, u32[]{:S(2)}, u32[]{:S(2)}) collective-permute-start(bf16[256,768]{1,0:T(8,128)(2,1)} %constant_dynamic-update-slice_fusion.refs_0_.t0), channel_id=1, source_target_pairs={{16,0},{32,16},{48,32},{0,48},{80,64},{96,80},{112,96},{64,112},{1... | collective-permute-start | bytes 1179656 | tf_op jit(solution)/shard_map/ppermute | solution.py:34
  11.5 2.8 %fusion.43 = (bf16[2,256,768]{2,1,0:T(8,128)(2,1)}, bf16[2,256,768]{2,1,0:T(8,128)(2,1)}) fusion(bf16[4,256,768]{2,1,0:T(8,128)(2,1)} %tok.3), kind=kLoop, calls=%fused_computation.105 | loop fusion | bytes 3145728 | tf_op jit(solution)/shard_map/slice | solution.py:366
  14.3 2.2 %collective-permute-start.2 = (bf16[2,256,768]{2,1,0:T(8,128)(2,1)}, bf16[2,256,768]{2,1,0:T(8,128)(2,1)}, u32[]{:S(2)}, u32[]{:S(2)}) collective-permute-start(bf16[2,256,768]{2,1,0:T(8,128)(2,1)} %get-tuple-element.84), channel_id=1, source_target_pairs={{0,1},{1,2},{2,3},{3,4},{4,5},{5,6},{6,7},{7,8},{8,9},{9,10},{10,1... | collective-permute-start | bytes 2359304 | tf_op jit(solution)/shard_map/ppermute | solution.py:367
  16.5 1.3 collective-permute-start.3
  17.8 7.0 %collective-permute-start = (bf16[2,256,768]{2,1,0:T(8,128)(2,1)}, bf16[2,256,768]{2,1,0:T(8,128)(2,1)}, u32[]{:S(2)}, u32[]{:S(2)}) collective-permute-start(bf16[2,256,768]{2,1,0:T(8,128)(2,1)} %get-tuple-element.85), channel_id=1, source_target_pairs={{0,1},{1,2},{2,3},{3,4},{4,5},{5,6},{6,7},{7,8},{8,9},{9,10},{10,1... | collective-permute-start | bytes 2359304 | tf_op jit(solution)/shard_map/ppermute | solution.py:367
  24.8 1.3 collective-permute-start.1
  27.4 5.4 %convolution_convert_fusion = bf16[1024,1536]{1,0:T(8,128)(2,1)} fusion(bf16[1024,768]{1,0:T(8,128)(2,1)} %bitcast.24, bf16[768,2304]{1,0:T(8,128)(2,1)S(1)} %copy-done), kind=kOutput, calls=%fused_computation | convolution fusion | flops 2417491968 | bytes 7077888 | tf_op jit(solution)/shard_map/dot_general | solution.py:378
  32.9 5.7 %collective-permute-done.6.refs_2_.t2 = bf16[256,768]{1,0:T(8,128)(2,1)} collective-permute-done((bf16[256,768]{1,0:T(8,128)(2,1)}, bf16[256,768]{1,0:T(8,128)(2,1)}, u32[]{:S(2)}, u32[]{:S(2)}) %collective-permute-start.6) | collective-permute-done | bytes 393248 | tf_op jit(solution)/shard_map/ppermute | solution.py:34
  38.6 1.1 slice.65
  39.7 2.4 %copy.22 = bf16[768,768]{0,1:T(8,128)(2,1)} copy(bf16[768,768]{1,0:T(8,128)(2,1)} %slice.65) | data formatting | bytes 2359296
  42.1 3.0 %convolution_convert_fusion.1.v_turned = bf16[768,1024]{1,0:T(8,128)(2,1)S(1)} fusion(bf16[1024,768]{1,0:T(8,128)(2,1)} %bitcast.25, bf16[768,2304]{1,0:T(8,128)(2,1)S(1)} %copy-done), kind=kOutput, calls=%fused_computation.5 | convolution fusion | flops 1208745984 | bytes 4325376 | tf_op jit(solution)/shard_map/dot_general | solution.py:379
  45.1 6.0 %collective-permute-done.7.refs_3_.t3 = bf16[256,768]{1,0:T(8,128)(2,1)} collective-permute-done((bf16[256,768]{1,0:T(8,128)(2,1)}, bf16[256,768]{1,0:T(8,128)(2,1)}, u32[]{:S(2)}, u32[]{:S(2)}) %collective-permute-start.7) | collective-permute-done | bytes 393248 | tf_op jit(solution)/shard_map/ppermute | solution.py:34
  51.1 1.5 target.1
  52.7 13.9 %attend.2 = (bf16[4,256,768]{2,1,0:T(8,128)(2,1)}, bf16[768,1024]{1,0:T(8,128)(2,1)S(1)}, bf16[4,256,768]{2,1,0:T(8,128)(2,1)S(1)}, f32[4,256,128]{2,1,0:T(8,128)S(1)}, f32[4,1,768]{2,1,0:T(1,128)S(1)}) custom-call(s32[2]{0:T(128)S(1)} %pad_add_fusion.me, s32[4]{0:T(128)S(1)} %copy-done.14, bf16[4,256,768]{2,1,0:T(8,128)(2,1)S(1)} %copy-done.1, ...), custom_call_target="tpu_custom_call" | custom-call | flops 3019898880 | bytes 8388608 | tf_op jit(solution)/shard_map/attend/pallas_call | solution.py:169
  66.7 14.1 %attend.3 = (bf16[4,256,768]{2,1,0:T(8,128)(2,1)}, bf16[768,1024]{1,0:T(8,128)(2,1)S(1)}, bf16[4,256,768]{2,1,0:T(8,128)(2,1)S(1)}, f32[4,256,128]{2,1,0:T(8,128)S(1)}, f32[4,1,768]{2,1,0:T(1,128)S(1)}) custom-call(s32[2]{0:T(128)S(1)} %pad_add_fusion.me, ...), custom_call_target="tpu_custom_call", output_to_operand_aliasing={{0}: (11, {}), {1}: (12, {}), {2}: (13, {}), {3}: (14, {}),... | custom-call | flops 3019898880 | bytes 8388608 | tf_op jit(solution)/shard_map/attend/pallas_call | solution.py:169
  80.8 1.2 copy-done.8
  82.0 1.2 copy-done.10
  85.7 4.4 %collective-permute-start.10 = (f32[8,768]{1,0:T(8,128)S(1)}, f32[8,768]{1,0:T(8,128)S(1)}, u32[]{:S(2)}, u32[]{:S(2)}) collective-permute-start(f32[8,768]{1,0:T(8,128)S(1)} %fusion.40), channel_id=1, source_target_pairs={{4,0},{5,1},{6,2},{7,3},{8,4},{9,5},{10,6},{11,7},{12,8},{13,9},{1... | collective-permute-start | bytes 73736 | tf_op jit(solution)/shard_map/ppermute | solution.py:30
  90.0 2.3 %collective-permute-start.9 = (f32[8,768]{1,0:T(8,128)S(1)}, f32[8,768]{1,0:T(8,128)S(1)}, u32[]{:S(2)}, u32[]{:S(2)}) collective-permute-start(f32[8,768]{1,0:T(8,128)S(1)} %fusion.40), channel_id=1, source_target_pairs={{8,0},{9,1},{10,2},{11,3},{12,4},{13,5},{14,6},{15,7},{0,8},{1,9},... | collective-permute-start | bytes 73736 | tf_op jit(solution)/shard_map/ppermute | solution.py:30
  92.3 2.7 %collective-permute-done.11 = f32[8,768]{1,0:T(8,128)S(1)} collective-permute-done((f32[8,768]{1,0:T(8,128)S(1)}, f32[8,768]{1,0:T(8,128)S(1)}, u32[]{:S(2)}, u32[]{:S(2)}) %collective-permute-start.11) | collective-permute-done | bytes 24608 | tf_op jit(solution)/shard_map/ppermute | solution.py:30
  96.1 4.7 %collective-permute-done.12.other = f32[8,768]{1,0:T(8,128)S(1)} collective-permute-done((f32[8,768]{1,0:T(8,128)S(1)}, f32[8,768]{1,0:T(8,128)S(1)}, u32[]{:S(2)}, u32[]{:S(2)}) %collective-permute-start.12) | collective-permute-done | bytes 24608 | tf_op jit(solution)/shard_map/ppermute | solution.py:25
  101.8 3.4 %collective-permute-done.13 = f32[4,768]{1,0:T(4,128)S(1)} collective-permute-done((f32[4,768]{1,0:T(4,128)S(1)}, f32[4,768]{1,0:T(4,128)S(1)}, u32[]{:S(2)}, u32[]{:S(2)}) %collective-permute-start.13) | collective-permute-done | bytes 12320 | tf_op jit(solution)/shard_map/ppermute | solution.py:25
  105.2 1.1 collective-permute-start.15
  107.4 1.6 collective-permute-done.14.e1
  109.1 1.6 collective-permute-done.15.e2
  110.7 1.1 collective-permute-done.16.e3
  111.7 1.0 copy-done.7
  112.7 2.6 %score.1 = (f32[32,768]{1,0:T(8,128)S(1)}, f32[8,1024]{1,0:T(8,128)S(1)}) custom-call(s32[2]{0:T(128)S(1)} %pad_add_fusion.me, s32[32,1]{1,0:T(8,128)S(1)} %reshape.123.positive, f32[8,768]{1,0:T(8,128)S(1)} %pad_maximum_fusion.1.e0, f32[8,768]{1,0:T(8,128)S(1)} %collective-permute-done.14.e1, f32[8,768]{1,0:T(8,128)S(1)} %collective-permute-done.15.e2, ...), custom_call_target="tpu_custom_call" | custom-call | bytes 2097152 | tf_op jit(solution)/shard_map/score/pallas_call | solution.py:412
  115.4 1.2 collective-permute-done.17
  116.9 3.3 %collective-permute-start.18 = (f32[8,1024]{1,0:T(8,128)S(1)}, f32[8,1024]{1,0:T(8,128)S(1)}, u32[]{:S(2)}, u32[]{:S(2)}) collective-permute-start(f32[8,1024]{1,0:T(8,128)S(1)} %fusion.4), channel_id=1, source_target_pairs={{4,0},{5,1},{6,2},{7,3},{8,4},{9,5},{10,6},{11,7},{12,8},{13,9},{1... | collective-permute-start | bytes 98312 | tf_op jit(solution)/shard_map/ppermute | solution.py:30
  120.2 0.9 collective-permute-start.20
  121.8 3.9 %collective-permute-done.19 = f32[8,1024]{1,0:T(8,128)S(1)} collective-permute-done((f32[8,1024]{1,0:T(8,128)S(1)}, f32[8,1024]{1,0:T(8,128)S(1)}, u32[]{:S(2)}, u32[]{:S(2)}) %collective-permute-start.19) | collective-permute-done | bytes 32800 | tf_op jit(solution)/shard_map/ppermute | solution.py:30
  126.0 2.0 %collective-permute-start.21 = (f32[8,1024]{1,0:T(8,128)S(1)}, f32[8,1024]{1,0:T(8,128)S(1)}, u32[]{:S(2)}, u32[]{:S(2)}) collective-permute-start(f32[8,1024]{1,0:T(8,128)S(1)} %fusion.5), channel_id=1, source_target_pairs={{0,2},{1,3},{2,0},{3,1},{4,6},{5,7},{6,4},{7,5},{8,10},{9,11},{10,... | collective-permute-start | bytes 98312 | tf_op jit(solution)/shard_map/ppermute | solution.py:25
  128.0 1.4 fusion.2.turned
  130.3 1.4 collective-permute-done.21
  132.0 2.9 %grad.1 = (f32[384,768]{1,0:T(8,128)S(1)}, f32[384,768]{1,0:T(8,128)S(1)}, f32[8,128]{1,0:T(8,128)S(1)}) custom-call(s32[2]{0:T(128)S(1)} %pad_add_fusion.me, s32[4]{0:T(128)S(1)} %copy-done.14, f32[8,1024]{1,0:T(8,128)S(1)} %fusion.6.state, f32[4,768]{1,0:T(4,128)S(1)} %get-tuple-element.42.emb, f32[4,128]{1,0:T(4,128)S(1)} %get-tuple-element.44.rinv, ...), custom_call_target="tpu_custom_call" | custom-call | flops 1207959552 | bytes 8388608 | tf_op jit(solution)/shard_map/grad/pallas_call | solution.py:433
  135.0 2.8 %collective-permute-done.22.refs_1_ = f32[384,768]{1,0:T(8,128)S(1)} collective-permute-done((f32[384,768]{1,0:T(8,128)S(1)}, f32[384,768]{1,0:T(8,128)S(1)}, u32[]{:S(2)}, u32[]{:S(2)}) %collective-permute-start.22) | collective-permute-done | bytes 1179680 | tf_op jit(solution)/shard_map/ppermute | solution.py:25
  139.0 2.6 %collective-permute-start.24 = (bf16[96,768]{1,0:T(8,128)(2,1)S(1)}, bf16[96,768]{1,0:T(8,128)(2,1)S(1)}, u32[]{:S(2)}, u32[]{:S(2)}) collective-permute-start(bf16[96,768]{1,0:T(8,128)(2,1)S(1)} %get-tuple-element.57), channel_id=1, source_target_pairs={{32,0},{48,16},{0,32},{16,48},{96,64},{112,80},{64,96},{80,112},{3... | collective-permute-start | bytes 442376 | tf_op jit(solution)/shard_map/ppermute | solution.py:34
  141.9 3.8 %collective-permute-done.23.refs_1_ = bf16[96,768]{1,0:T(8,128)(2,1)S(1)} collective-permute-done((bf16[96,768]{1,0:T(8,128)(2,1)S(1)}, bf16[96,768]{1,0:T(8,128)(2,1)S(1)}, u32[]{:S(2)}, u32[]{:S(2)}) %collective-permute-start.23) | collective-permute-done | bytes 147488 | tf_op jit(solution)/shard_map/ppermute | solution.py:34
  145.7 2.9 %collective-permute-done.24.refs_2_ = bf16[96,768]{1,0:T(8,128)(2,1)S(1)} collective-permute-done((bf16[96,768]{1,0:T(8,128)(2,1)S(1)}, bf16[96,768]{1,0:T(8,128)(2,1)S(1)}, u32[]{:S(2)}, u32[]{:S(2)}) %collective-permute-start.24) | collective-permute-done | bytes 147488 | tf_op jit(solution)/shard_map/ppermute | solution.py:34
  149.1 2.3 %collective-permute-start.27 = (f32[24,768]{1,0:T(8,128)S(1)}, f32[24,768]{1,0:T(8,128)S(1)}, u32[]{:S(2)}, u32[]{:S(2)}) collective-permute-start(f32[24,768]{1,0:T(8,128)S(1)} %get-tuple-element.61), channel_id=1, source_target_pairs={{8,0},{9,1},{10,2},{11,3},{12,4},{13,5},{14,6},{15,7},{0,8},{1,9},... | collective-permute-start | bytes 221192 | tf_op jit(solution)/shard_map/ppermute | solution.py:30
  151.4 2.3 %collective-permute-start.28 = (f32[24,768]{1,0:T(8,128)S(1)}, f32[24,768]{1,0:T(8,128)S(1)}, u32[]{:S(2)}, u32[]{:S(2)}) collective-permute-start(f32[24,768]{1,0:T(8,128)S(1)} %get-tuple-element.62), channel_id=1, source_target_pairs={{4,0},{5,1},{6,2},{7,3},{8,4},{9,5},{10,6},{11,7},{12,8},{13,9},{1... | collective-permute-start | bytes 221192 | tf_op jit(solution)/shard_map/ppermute | solution.py:30
  153.7 1.8 %collective-permute-done.26.refs_1_ = f32[24,768]{1,0:T(8,128)S(1)} collective-permute-done((f32[24,768]{1,0:T(8,128)S(1)}, f32[24,768]{1,0:T(8,128)S(1)}, u32[]{:S(2)}, u32[]{:S(2)}) %collective-permute-start.26) | collective-permute-done | bytes 73760 | tf_op jit(solution)/shard_map/ppermute | solution.py:30
  156.7 3.4 %collective-permute-start.30 = (f32[6,768]{1,0:T(8,128)S(1)}, f32[6,768]{1,0:T(8,128)S(1)}, u32[]{:S(2)}, u32[]{:S(2)}) collective-permute-start(f32[6,768]{1,0:T(8,128)S(1)} %get-tuple-element.65), channel_id=1, source_target_pairs={{2,0},{3,1},{0,2},{1,3},{6,4},{7,5},{4,6},{5,7},{10,8},{11,9},{8,1... | collective-permute-start | bytes 55304 | tf_op jit(solution)/shard_map/ppermute | solution.py:44
  162.2 1.8 %collective-permute-done.31 = f32[6,768]{1,0:T(8,128)S(1)} collective-permute-done((f32[6,768]{1,0:T(8,128)S(1)}, f32[6,768]{1,0:T(8,128)S(1)}, u32[]{:S(2)}, u32[]{:S(2)}) %collective-permute-start.31) | collective-permute-done | bytes 18464 | tf_op jit(solution)/shard_map/ppermute | solution.py:44
  (96 shorter events, 16.3 us)
Async XLA Ops:
  0.6 7.2 %collective-permute-start.4 = (bf16[128,768]{1,0:T(8,128)(2,1)}, bf16[128,768]{1,0:T(8,128)(2,1)S(1)}, u32[]{:S(2)}, u32[]{:S(2)}) collective-permute-start(bf16[128,768]{1,0:T(8,128)(2,1)} %param.11), channel_id=1, source_target_pairs={{0,64},{16,80},{32,96},{48,112},{64,0},{80,16},{96,32},{112,48},{1... | collective-permute-start | bytes 589832 | tf_op jit(solution)/shard_map/ppermute | solution.py:25
  7.8 19.6 %copy-start = (bf16[768,2304]{1,0:T(8,128)(2,1)S(1)}, bf16[768,2304]{1,0:T(8,128)(2,1)}, u32[]{:S(2)}) copy-start(bf16[768,2304]{1,0:T(8,128)(2,1)} %w_k.3) | copy-start | bytes 10616836
  8.5 17.5 %collective-permute-start.5 = (bf16[256,768]{1,0:T(8,128)(2,1)}, bf16[256,768]{1,0:T(8,128)(2,1)S(1)}, u32[]{:S(2)}, u32[]{:S(2)}) collective-permute-start(bf16[256,768]{1,0:T(8,128)(2,1)} %constant_dynamic-update-slice_fusion.refs_0_.t0), channel_id=1, source_target_pairs={{16,0},{32,16},{48,32},{0,48},{80,64},{96,80},{112,96},{64,112},{1... | collective-permute-start | bytes 1179656 | tf_op jit(solution)/shard_map/ppermute | solution.py:34
  14.3 38.3 %collective-permute-start.2 = (bf16[2,256,768]{2,1,0:T(8,128)(2,1)}, bf16[2,256,768]{2,1,0:T(8,128)(2,1)}, u32[]{:S(2)}, u32[]{:S(2)}) collective-permute-start(bf16[2,256,768]{2,1,0:T(8,128)(2,1)} %get-tuple-element.84), channel_id=1, source_target_pairs={{0,1},{1,2},{2,3},{3,4},{4,5},{5,6},{6,7},{7,8},{8,9},{9,10},{10,1... | collective-permute-start | bytes 2359304 | tf_op jit(solution)/shard_map/ppermute | solution.py:367
  16.5 36.2 %collective-permute-start.3 = (bf16[2,256,768]{2,1,0:T(8,128)(2,1)}, bf16[2,256,768]{2,1,0:T(8,128)(2,1)}, u32[]{:S(2)}, u32[]{:S(2)}) collective-permute-start(bf16[2,256,768]{2,1,0:T(8,128)(2,1)} %get-tuple-element.84), channel_id=1, source_target_pairs={{1,0},{2,1},{3,2},{4,3},{5,4},{6,5},{7,6},{8,7},{9,8},{10,9},{11,1... | collective-permute-start | bytes 2359304 | tf_op jit(solution)/shard_map/ppermute | solution.py:368
  17.8 48.9 %collective-permute-start = (bf16[2,256,768]{2,1,0:T(8,128)(2,1)}, bf16[2,256,768]{2,1,0:T(8,128)(2,1)}, u32[]{:S(2)}, u32[]{:S(2)}) collective-permute-start(bf16[2,256,768]{2,1,0:T(8,128)(2,1)} %get-tuple-element.85), channel_id=1, source_target_pairs={{0,1},{1,2},{2,3},{3,4},{4,5},{5,6},{6,7},{7,8},{8,9},{9,10},{10,1... | collective-permute-start | bytes 2359304 | tf_op jit(solution)/shard_map/ppermute | solution.py:367
  24.8 41.9 %collective-permute-start.1 = (bf16[2,256,768]{2,1,0:T(8,128)(2,1)}, bf16[2,256,768]{2,1,0:T(8,128)(2,1)}, u32[]{:S(2)}, u32[]{:S(2)}) collective-permute-start(bf16[2,256,768]{2,1,0:T(8,128)(2,1)} %get-tuple-element.85), channel_id=1, source_target_pairs={{1,0},{2,1},{3,2},{4,3},{5,4},{6,5},{7,6},{8,7},{9,8},{10,9},{11,1... | collective-permute-start | bytes 2359304 | tf_op jit(solution)/shard_map/ppermute | solution.py:368
  26.8 11.7 %collective-permute-start.6 = (bf16[256,768]{1,0:T(8,128)(2,1)}, bf16[256,768]{1,0:T(8,128)(2,1)}, u32[]{:S(2)}, u32[]{:S(2)}) collective-permute-start(bf16[256,768]{1,0:T(8,128)(2,1)} %constant_dynamic-update-slice_fusion.refs_0_.t0), channel_id=1, source_target_pairs={{32,0},{48,16},{0,32},{16,48},{96,64},{112,80},{64,96},{80,112},{3... | collective-permute-start | bytes 1179656 | tf_op jit(solution)/shard_map/ppermute | solution.py:34
  32.9 6.8 %copy-start.16 = (f32[768]{0:T(1024)S(1)}, f32[768]{0:T(1024)}, u32[]{:S(2)}) copy-start(f32[768]{0:T(1024)} %param.10) | copy-start | bytes 9220
  38.5 12.6 %collective-permute-start.7 = (bf16[256,768]{1,0:T(8,128)(2,1)}, bf16[256,768]{1,0:T(8,128)(2,1)}, u32[]{:S(2)}, u32[]{:S(2)}) collective-permute-start(bf16[256,768]{1,0:T(8,128)(2,1)} %constant_dynamic-update-slice_fusion.refs_0_.t0), channel_id=1, source_target_pairs={{48,0},{0,16},{16,32},{32,48},{112,64},{64,80},{80,96},{96,112},{4... | collective-permute-start | bytes 1179656 | tf_op jit(solution)/shard_map/ppermute | solution.py:34
  42.1 9.0 %copy-start.6 = (bf16[256,768]{1,0:T(8,128)(2,1)S(1)}, bf16[256,768]{1,0:T(8,128)(2,1)}, u32[]{:S(2)}) copy-start(bf16[256,768]{1,0:T(8,128)(2,1)} %copy-done.5) | copy-start | bytes 1179652
  42.1 9.0 %copy-start.15 = (s32[32]{0:T(128)S(1)}, s32[32]{0:T(128)}, u32[]{:S(2)}) copy-start(s32[32]{0:T(128)} %positive.1) | copy-start | bytes 388
  42.1 10.6 %copy-start.2 = (bf16[1024,1536]{1,0:T(8,128)(2,1)S(1)}, bf16[1024,1536]{1,0:T(8,128)(2,1)}, u32[]{:S(2)}) copy-start(bf16[1024,1536]{1,0:T(8,128)(2,1)} %convolution_convert_fusion) | copy-start | bytes 9437188
  42.1 10.6 %copy-start.3 = (bf16[768,768]{0,1:T(8,128)(2,1)S(1)}, bf16[768,768]{0,1:T(8,128)(2,1)}, u32[]{:S(2)}) copy-start(bf16[768,768]{0,1:T(8,128)(2,1)} %copy.22) | copy-start | bytes 3538948
  42.1 10.6 %copy-start.4 = (bf16[768,768]{1,0:T(8,128)(2,1)S(1)}, bf16[768,768]{1,0:T(8,128)(2,1)}, u32[]{:S(2)}) copy-start(bf16[768,768]{1,0:T(8,128)(2,1)} %w_out.3) | copy-start | bytes 3538948
  45.1 7.6 %copy-start.1 = (bf16[4,256,768]{2,1,0:T(8,128)(2,1)S(1)}, bf16[4,256,768]{2,1,0:T(8,128)(2,1)}, u32[]{:S(2)}) copy-start(bf16[4,256,768]{2,1,0:T(8,128)(2,1)} %tok.3) | copy-start | bytes 4718596
  45.1 7.6 %copy-start.14 = (s32[4]{0:T(128)S(1)}, s32[4]{0:T(128)}, u32[]{:S(2)}) copy-start(s32[4]{0:T(128)} %lengths.7) | copy-start | bytes 52
  80.8 1.2 copy-start.8
  82.0 1.2 copy-start.10
  83.2 0.8 copy-start.12
  84.0 1.7 %collective-permute-start.8 = (f32[8,768]{1,0:T(8,128)S(1)}, f32[8,768]{1,0:T(8,128)S(1)}, u32[]{:S(2)}, u32[]{:S(2)}) collective-permute-start(f32[8,768]{1,0:T(8,128)S(1)} %pad_maximum_fusion), channel_id=1, source_target_pairs={{0,1},{1,0},{2,3},{3,2},{4,5},{5,4},{6,7},{7,6},{8,9},{9,8},{10,11... | collective-permute-start | bytes 73736 | tf_op jit(solution)/shard_map/ppermute | solution.py:25
  85.7 6.7 %collective-permute-start.10 = (f32[8,768]{1,0:T(8,128)S(1)}, f32[8,768]{1,0:T(8,128)S(1)}, u32[]{:S(2)}, u32[]{:S(2)}) collective-permute-start(f32[8,768]{1,0:T(8,128)S(1)} %fusion.40), channel_id=1, source_target_pairs={{4,0},{5,1},{6,2},{7,3},{8,4},{9,5},{10,6},{11,7},{12,8},{13,9},{1... | collective-permute-start | bytes 73736 | tf_op jit(solution)/shard_map/ppermute | solution.py:30
  90.0 5.0 %collective-permute-start.11 = (f32[8,768]{1,0:T(8,128)S(1)}, f32[8,768]{1,0:T(8,128)S(1)}, u32[]{:S(2)}, u32[]{:S(2)}) collective-permute-start(f32[8,768]{1,0:T(8,128)S(1)} %fusion.40), channel_id=1, source_target_pairs={{12,0},{13,1},{14,2},{15,3},{0,4},{1,5},{2,6},{3,7},{4,8},{5,9},{6... | collective-permute-start | bytes 73736 | tf_op jit(solution)/shard_map/ppermute | solution.py:30
  90.0 5.3 %collective-permute-start.9 = (f32[8,768]{1,0:T(8,128)S(1)}, f32[8,768]{1,0:T(8,128)S(1)}, u32[]{:S(2)}, u32[]{:S(2)}) collective-permute-start(f32[8,768]{1,0:T(8,128)S(1)} %fusion.40), channel_id=1, source_target_pairs={{8,0},{9,1},{10,2},{11,3},{12,4},{13,5},{14,6},{15,7},{0,8},{1,9},... | collective-permute-start | bytes 73736 | tf_op jit(solution)/shard_map/ppermute | solution.py:30
  95.4 5.4 %collective-permute-start.12 = (f32[8,768]{1,0:T(8,128)S(1)}, f32[8,768]{1,0:T(8,128)S(1)}, u32[]{:S(2)}, u32[]{:S(2)}) collective-permute-start(f32[8,768]{1,0:T(8,128)S(1)} %add_add_fusion.1.mine), channel_id=1, source_target_pairs={{0,2},{1,3},{2,0},{3,1},{4,6},{5,7},{6,4},{7,5},{8,10},{9,11},{10,... | collective-permute-start | bytes 73736 | tf_op jit(solution)/shard_map/ppermute | solution.py:25
  101.4 3.7 %collective-permute-start.13 = (f32[4,768]{1,0:T(4,128)S(1)}, f32[4,768]{1,0:T(4,128)S(1)}, u32[]{:S(2)}, u32[]{:S(2)}) collective-permute-start(f32[4,768]{1,0:T(4,128)S(1)} %get-tuple-element.42.emb), channel_id=1, source_target_pairs={{0,64},{16,80},{32,96},{48,112},{64,0},{80,16},{96,32},{112,48},{1... | collective-permute-start | bytes 36872 | tf_op jit(solution)/shard_map/ppermute | solution.py:25
  105.2 3.9 %collective-permute-start.14 = (f32[8,768]{1,0:T(8,128)S(1)}, f32[8,768]{1,0:T(8,128)S(1)}, u32[]{:S(2)}, u32[]{:S(2)}) collective-permute-start(f32[8,768]{1,0:T(8,128)S(1)} %pad_maximum_fusion.1.e0), channel_id=1, source_target_pairs={{16,0},{32,16},{48,32},{0,48},{80,64},{96,80},{112,96},{64,112},{1... | collective-permute-start | bytes 73736 | tf_op jit(solution)/shard_map/ppermute | solution.py:34
  105.2 5.4 %collective-permute-start.15 = (f32[8,768]{1,0:T(8,128)S(1)}, f32[8,768]{1,0:T(8,128)S(1)}, u32[]{:S(2)}, u32[]{:S(2)}) collective-permute-start(f32[8,768]{1,0:T(8,128)S(1)} %pad_maximum_fusion.1.e0), channel_id=1, source_target_pairs={{32,0},{48,16},{0,32},{16,48},{96,64},{112,80},{64,96},{80,112},{3... | collective-permute-start | bytes 73736 | tf_op jit(solution)/shard_map/ppermute | solution.py:34
  106.4 5.4 %collective-permute-start.16 = (f32[8,768]{1,0:T(8,128)S(1)}, f32[8,768]{1,0:T(8,128)S(1)}, u32[]{:S(2)}, u32[]{:S(2)}) collective-permute-start(f32[8,768]{1,0:T(8,128)S(1)} %pad_maximum_fusion.1.e0), channel_id=1, source_target_pairs={{48,0},{0,16},{16,32},{32,48},{112,64},{64,80},{80,96},{96,112},{4... | collective-permute-start | bytes 73736 | tf_op jit(solution)/shard_map/ppermute | solution.py:34
  111.7 1.0 copy-start.7
  112.7 15.3 %copy-start.9 = (bf16[768,1024]{1,0:T(8,128)(2,1)S(1)}, bf16[768,1024]{1,0:T(8,128)(2,1)}, u32[]{:S(2)}) copy-start(bf16[768,1024]{1,0:T(8,128)(2,1)} %copy-done.8) | copy-start | bytes 4718596
  115.3 1.3 collective-permute-start.17
  116.9 4.9 %collective-permute-start.18 = (f32[8,1024]{1,0:T(8,128)S(1)}, f32[8,1024]{1,0:T(8,128)S(1)}, u32[]{:S(2)}, u32[]{:S(2)}) collective-permute-start(f32[8,1024]{1,0:T(8,128)S(1)} %fusion.4), channel_id=1, source_target_pairs={{4,0},{5,1},{6,2},{7,3},{8,4},{9,5},{10,6},{11,7},{12,8},{13,9},{1... | collective-permute-start | bytes 98312 | tf_op jit(solution)/shard_map/ppermute | solution.py:30
  120.2 5.5 %collective-permute-start.19 = (f32[8,1024]{1,0:T(8,128)S(1)}, f32[8,1024]{1,0:T(8,128)S(1)}, u32[]{:S(2)}, u32[]{:S(2)}) collective-permute-start(f32[8,1024]{1,0:T(8,128)S(1)} %fusion.4), channel_id=1, source_target_pairs={{8,0},{9,1},{10,2},{11,3},{12,4},{13,5},{14,6},{15,7},{0,8},{1,9},... | collective-permute-start | bytes 98312 | tf_op jit(solution)/shard_map/ppermute | solution.py:30
  120.2 5.5 %collective-permute-start.20 = (f32[8,1024]{1,0:T(8,128)S(1)}, f32[8,1024]{1,0:T(8,128)S(1)}, u32[]{:S(2)}, u32[]{:S(2)}) collective-permute-start(f32[8,1024]{1,0:T(8,128)S(1)} %fusion.4), channel_id=1, source_target_pairs={{12,0},{13,1},{14,2},{15,3},{0,4},{1,5},{2,6},{3,7},{4,8},{5,9},{6... | collective-permute-start | bytes 98312 | tf_op jit(solution)/shard_map/ppermute | solution.py:30
  126.0 5.7 %collective-permute-start.21 = (f32[8,1024]{1,0:T(8,128)S(1)}, f32[8,1024]{1,0:T(8,128)S(1)}, u32[]{:S(2)}, u32[]{:S(2)}) collective-permute-start(f32[8,1024]{1,0:T(8,128)S(1)} %fusion.5), channel_id=1, source_target_pairs={{0,2},{1,3},{2,0},{3,1},{4,6},{5,7},{6,4},{7,5},{8,10},{9,11},{10,... | collective-permute-start | bytes 98312 | tf_op jit(solution)/shard_map/ppermute | solution.py:25
  128.0 4.0 %copy-start.11 = (bf16[4,256,768]{2,1,0:T(8,128)(2,1)S(1)}, bf16[4,256,768]{2,1,0:T(8,128)(2,1)}, u32[]{:S(2)}) copy-start(bf16[4,256,768]{2,1,0:T(8,128)(2,1)} %copy-done.10) | copy-start | bytes 4718596
  128.0 4.0 %copy-start.13 = (f32[4,256,128]{2,1,0:T(8,128)S(1)}, f32[4,256,128]{2,1,0:T(8,128)}, u32[]{:S(2)}) copy-start(f32[4,256,128]{2,1,0:T(8,128)} %copy-done.12) | copy-start | bytes 1572868
  134.9 2.9 %collective-permute-start.22 = (f32[384,768]{1,0:T(8,128)S(1)}, f32[384,768]{1,0:T(8,128)S(1)}, u32[]{:S(2)}, u32[]{:S(2)}) collective-permute-start(f32[384,768]{1,0:T(8,128)S(1)} %get-tuple-element.54), channel_id=1, source_target_pairs={{0,1},{1,0},{2,3},{3,2},{4,5},{5,4},{6,7},{7,6},{8,9},{9,8},{10,11... | collective-permute-start | bytes 3538952 | tf_op jit(solution)/shard_map/ppermute | solution.py:25
  138.0 7.7 %collective-permute-start.23 = (bf16[96,768]{1,0:T(8,128)(2,1)S(1)}, bf16[96,768]{1,0:T(8,128)(2,1)S(1)}, u32[]{:S(2)}, u32[]{:S(2)}) collective-permute-start(bf16[96,768]{1,0:T(8,128)(2,1)S(1)} %get-tuple-element.56), channel_id=1, source_target_pairs={{48,0},{0,16},{16,32},{32,48},{112,64},{64,80},{80,96},{96,112},{4... | collective-permute-start | bytes 442376 | tf_op jit(solution)/shard_map/ppermute | solution.py:34
  139.0 9.6 %collective-permute-start.24 = (bf16[96,768]{1,0:T(8,128)(2,1)S(1)}, bf16[96,768]{1,0:T(8,128)(2,1)S(1)}, u32[]{:S(2)}, u32[]{:S(2)}) collective-permute-start(bf16[96,768]{1,0:T(8,128)(2,1)S(1)} %get-tuple-element.57), channel_id=1, source_target_pairs={{32,0},{48,16},{0,32},{16,48},{96,64},{112,80},{64,96},{80,112},{3... | collective-permute-start | bytes 442376 | tf_op jit(solution)/shard_map/ppermute | solution.py:34
  141.6 7.4 %collective-permute-start.25 = (bf16[96,768]{1,0:T(8,128)(2,1)S(1)}, bf16[96,768]{1,0:T(8,128)(2,1)S(1)}, u32[]{:S(2)}, u32[]{:S(2)}) collective-permute-start(bf16[96,768]{1,0:T(8,128)(2,1)S(1)} %get-tuple-element.58), channel_id=1, source_target_pairs={{16,0},{32,16},{48,32},{0,48},{80,64},{96,80},{112,96},{64,112},{1... | collective-permute-start | bytes 442376 | tf_op jit(solution)/shard_map/ppermute | solution.py:34
  149.0 6.4 %collective-permute-start.26 = (f32[24,768]{1,0:T(8,128)S(1)}, f32[24,768]{1,0:T(8,128)S(1)}, u32[]{:S(2)}, u32[]{:S(2)}) collective-permute-start(f32[24,768]{1,0:T(8,128)S(1)} %get-tuple-element.60), channel_id=1, source_target_pairs={{12,0},{13,1},{14,2},{15,3},{0,4},{1,5},{2,6},{3,7},{4,8},{5,9},{6... | collective-permute-start | bytes 221192 | tf_op jit(solution)/shard_map/ppermute | solution.py:30
  149.1 6.3 %collective-permute-start.27 = (f32[24,768]{1,0:T(8,128)S(1)}, f32[24,768]{1,0:T(8,128)S(1)}, u32[]{:S(2)}, u32[]{:S(2)}) collective-permute-start(f32[24,768]{1,0:T(8,128)S(1)} %get-tuple-element.61), channel_id=1, source_target_pairs={{8,0},{9,1},{10,2},{11,3},{12,4},{13,5},{14,6},{15,7},{0,8},{1,9},... | collective-permute-start | bytes 221192 | tf_op jit(solution)/shard_map/ppermute | solution.py:30
  151.4 4.9 %collective-permute-start.28 = (f32[24,768]{1,0:T(8,128)S(1)}, f32[24,768]{1,0:T(8,128)S(1)}, u32[]{:S(2)}, u32[]{:S(2)}) collective-permute-start(f32[24,768]{1,0:T(8,128)S(1)} %get-tuple-element.62), channel_id=1, source_target_pairs={{4,0},{5,1},{6,2},{7,3},{8,4},{9,5},{10,6},{11,7},{12,8},{13,9},{1... | collective-permute-start | bytes 221192 | tf_op jit(solution)/shard_map/ppermute | solution.py:30
  156.4 5.1 %collective-permute-start.29 = (f32[6,768]{1,0:T(8,128)S(1)}, f32[6,768]{1,0:T(8,128)S(1)}, u32[]{:S(2)}, u32[]{:S(2)}) collective-permute-start(f32[6,768]{1,0:T(8,128)S(1)} %get-tuple-element.64), channel_id=1, source_target_pairs={{66,0},{67,1},{64,2},{65,3},{70,4},{71,5},{68,6},{69,7},{74,8},{75... | collective-permute-start | bytes 55304 | tf_op jit(solution)/shard_map/ppermute | solution.py:44
  156.7 5.5 %collective-permute-start.30 = (f32[6,768]{1,0:T(8,128)S(1)}, f32[6,768]{1,0:T(8,128)S(1)}, u32[]{:S(2)}, u32[]{:S(2)}) collective-permute-start(f32[6,768]{1,0:T(8,128)S(1)} %get-tuple-element.65), channel_id=1, source_target_pairs={{2,0},{3,1},{0,2},{1,3},{6,4},{7,5},{4,6},{5,7},{10,8},{11,9},{8,1... | collective-permute-start | bytes 55304 | tf_op jit(solution)/shard_map/ppermute | solution.py:44
  160.1 3.8 %collective-permute-start.31 = (f32[6,768]{1,0:T(8,128)S(1)}, f32[6,768]{1,0:T(8,128)S(1)}, u32[]{:S(2)}, u32[]{:S(2)}) collective-permute-start(f32[6,768]{1,0:T(8,128)S(1)} %get-tuple-element.66), channel_id=1, source_target_pairs={{64,0},{65,1},{66,2},{67,3},{68,4},{69,5},{70,6},{71,7},{72,8},{73... | collective-permute-start | bytes 55304 | tf_op jit(solution)/shard_map/ppermute | solution.py:44
  (1 other events, 0.8 us)
where the time goes:
time: 165 us
  waiting for transfers between devices  53.6 us (32%)
  starting transfers between devices  47.5 us (29%)
  Pallas kernels  36.9 us (22%)
  local copies, waits for them, and re-layouts  14.2 us (9%)
  matrix products  9.86 us (6%)
    pallas_call x2, Pallas kernels, attend(): call(functools.partial(attend_kernel, first), out_shape, in_specs, (here(...  28.1 us
    ppermute x9, waiting for transfers between devices, from_y(): lax.ppermute(value, 'dp', [(d & 4 | d + k & 3, d) for d in range(lax.axis...  23 us
    ppermute x7, waiting for transfers between devices, swap(): lax.ppermute(value, axis, [(i, i ^ bits) for i in range(lax.axis_size(axi...  17.8 us
    ppermute x9, starting transfers between devices, from_x(): lax.ppermute(value, 'ctx', [((c + 4 * k) % size, c) for c in range(size)])  15.6 us
    ppermute x9, waiting for transfers between devices, from_x(): lax.ppermute(value, 'ctx', [((c + 4 * k) % size, c) for c in range(size)])  10.1 us
    unnamed x38, local copies, waits for them, and re-layouts  10.1 us
    ppermute x9, starting transfers between devices, from_y(): lax.ppermute(value, 'dp', [(d & 4 | d + k & 3, d) for d in range(lax.axis...  9.62 us
    ppermute x2, starting transfers between devices, shards(): left = lax.ppermute(part, 'ctx', [(i, i + 1) for i in range(n_ctx - 1)])  9.16 us
  transfers between devices with their start and end apart: 32, of which 24 were waited for; matrix products, arithmetic and copies ran while one was open for 11% of the time, Pallas kernels for 10%

commit v1 on v0

--- a/solution.py
+++ b/solution.py
@@ -145,7 +145,7 @@
     normed[0] = unit.astype(jnp.bfloat16)
     rstd_out[0] = jnp.broadcast_to(rstd, rstd_out.shape[1:])
     keep = start + lax.broadcasted_iota(jnp.int32, (tb, 1), 0) < length
-    pool[0] = jnp.sum(jnp.where(keep, hidden_f, 0.0), axis=0, keepdims=True)
+    pool[0] = jnp.sum(jnp.where(keep, hidden_f, 0.0), axis=0, keepdims=True) / length.astype(jnp.float32)
 
 
 def attend(first, before, me, lengths, tokens, left, right, qk, v_turned, w_qkv, w_v_turned, w_out, gain):
@@ -208,18 +208,29 @@
     out[...] = total
 
 
-def norm_kernel(lengths, mine, other, emb_out, rinv_out, target_out):
-    docs = emb_out.shape[0]
-    both = mine[...] + other[...]
-    row = lax.broadcasted_iota(jnp.int32, (docs, 128), 0)
-    count = jnp.zeros((docs, 128), jnp.float32)
-    for d in range(docs):
-        count = jnp.where(row == d, lengths[d].astype(jnp.float32), count)
-    pooled = both[0:docs] / count[:, 0:1]
+def turn_kernel(me, mixed, out):
+    width = out.shape[0]
+    place = lax.broadcasted_iota(jnp.int32, (width, 1), 0)
+    dp, ctx = me[0], me[1]
+    each = width // 128
+    core = (ctx & 1) ^ (place // (64 * each))
+    y = ((dp & 3) + place // (16 * each) % 4) & 3
+    x = ((ctx >> 2) + place // (4 * each) % 4) & 3
+    z = ((ctx & 2) + (dp >> 2) + place // each % 4) & 3
+    block = ((z & 1) * 4 + y) * 16 + x * 4 + (z >> 1) * 2 + core
+    chosen = block * each + place % each == lax.broadcasted_iota(jnp.int32, (width, width), 1)
+    chosen = jnp.where(chosen, 1.0, 0.0).astype(jnp.bfloat16)
+    out[...] = jnp.dot(chosen, mixed[...], preferred_element_type=jnp.float32).astype(jnp.bfloat16)
+
+
+def norm_kernel(s0, s1, s2, s3, emb_out, rinv_out, target_out):
+    docs = target_out.shape[0]
+    own, other = s0[...] + s2[...], s1[0:docs] + s3[0:docs]
+    pooled = jnp.concatenate([own[0:docs], other], axis=0)
     rinv = lax.rsqrt(jnp.sum(pooled * pooled, axis=1, keepdims=True) + 1e-06)
     emb_out[...] = pooled * rinv
     rinv_out[...] = jnp.broadcast_to(rinv, rinv_out.shape)
-    target_out[...] = both[docs:]
+    target_out[...] = own[docs:]
 
 
 def as_row(column):
@@ -300,13 +311,14 @@
 
 
 def grad_kernel(
-    me, lengths, state, emb, rinv, everyone, target, product, stats, gain, normed, rstd, turned,
+    me, lengths, state, other, emb, rinv, everyone, target, product, stats, gain, normed, rstd, turned,
     keep_out, send_out, loss_out, d_summed,
 ):
-    docs, width = emb.shape
+    docs, width = target.shape
     all_docs = everyone.shape[0]
     y, z_lo = me[0] & 3, me[0] >> 2
-    own, others, now = emb[...], everyone[...], state[...]
+    own, others = emb[0:docs], everyone[...]
+    now = merge(docs, width, [state[...], other[...]])
     total, top, found = (now[docs + k : docs + k + 1, 0:all_docs] for k in range(3))
     batch_top, batch_total = stats[0:1], stats[1:2]
     peak = jnp.maximum(top, batch_top)
@@ -315,12 +327,12 @@
     column = lax.broadcasted_iota(jnp.int32, (docs, all_docs), 1)
     same = column == lax.broadcasted_iota(jnp.int32, (docs, all_docs), 0) + y * 2 * docs + z_lo * docs
     lse = jnp.sum(jnp.where(same, lse_row, 0.0), axis=1, keepdims=True)
-    scores = product[...]
+    scores = product[0:docs]
     g_batch = jnp.where(same, 0.0, jnp.exp(scores - lse) + jnp.exp(scores - lse_row)) / all_docs
     mix = now[0:docs, 0:width] * jnp.exp(now[0:docs, width + 128 : width + 129] - lse)
     from_batch = jnp.dot(g_batch, others, precision=HIGHEST, preferred_element_type=jnp.float32)
     d_emb = ((mix - target[...]) / all_docs + from_batch) / TAU
-    d_pooled = (d_emb - own * jnp.sum(own * d_emb, axis=1, keepdims=True)) * rinv[:, 0:1]
+    d_pooled = (d_emb - own * jnp.sum(own * d_emb, axis=1, keepdims=True)) * rinv[0:docs, 0:1]
     tb = normed.shape[1]
     for doc in range(docs):
         dy = d_pooled[doc : doc + 1] / lengths[doc].astype(jnp.float32) * gain[...]
@@ -357,21 +369,17 @@
 def shards(tokens, w_qkv, w_out, ln_gain, cache, positive, lengths):
     docs, tb, width = tokens.shape
     n_ctx, n_dp = lax.axis_size("ctx"), lax.axis_size("dp")
-    devices = n_dp * n_ctx
     dp, ctx = lax.axis_index("dp"), lax.axis_index("ctx")
     me = jnp.stack([dp, ctx]).astype(jnp.int32)
     all_docs = n_dp * docs
     halos = []
-    for first in range(0, docs, CHUNK):
-        part = tokens[first : first + CHUNK]
-        left = lax.ppermute(part, "ctx", [(i, i + 1) for i in range(n_ctx - 1)])
-        right = lax.ppermute(part, "ctx", [(i + 1, i) for i in range(n_ctx - 1)])
+    parts = [tokens[first : first + CHUNK] for first in range(0, docs, CHUNK)]
+    *parts, cache = lax.optimization_barrier((*parts, cache))
+    for part in parts:
+        left = lax.ppermute(part, "ctx", [(i, (i + 1) % n_ctx) for i in range(n_ctx)])
+        right = lax.ppermute(part, "ctx", [((i + 1) % n_ctx, i) for i in range(n_ctx)])
         halos.append((left, right))
     tables = around(jnp.concatenate([cache, swap(cache, "dp", 4)], axis=0), from_y)
-    target = call(
-        functools.partial(target_kernel, docs), f32(docs, width), [SMEM, SMEM] + [VMEM] * 4, VMEM, name="target"
-    )(me, positive, *tables)
-
     gain = ln_gain.reshape(1, width)
     flat = tokens.reshape(docs * tb, width)
     w_v_turned = w_qkv[:, 2 * width :].T
@@ -380,20 +388,27 @@
     qk = qk.reshape(docs, tb, 2 * width)
     done = None
     for index, (left, right) in enumerate(halos):
+        if index == 1:
+            *done, pool = done
+            pool, after = lax.optimization_barrier((pool, positive))
+            done = [*done, pool]
+            target = call(
+                functools.partial(target_kernel, docs), f32(docs, width), [SMEM, SMEM] + [VMEM] * 4, VMEM, name="target"
+            )(me, after, *tables)
         done = attend(
             index * CHUNK, done, me, lengths, tokens, left, right, qk, v_turned, w_qkv, w_v_turned, w_out, gain
         )
     hidden, mixed, normed, rstd, pool = done
 
-    place = jnp.arange(width, dtype=jnp.int32)
-    each = width // devices
-    core = (ctx & 1) ^ (place // (64 * each))
-    y = ((dp & 3) + place // (16 * each) % 4) & 3
-    x = ((ctx >> 2) + place // (4 * each) % 4) & 3
-    z = ((ctx & 2) + (dp >> 2) + place // each % 4) & 3
-    block = ((z & 1) * 4 + y) * n_ctx + x * 4 + (z >> 1) * 2 + core
-    chosen = ((block * each + place % each)[:, None] == place[None, :]).astype(jnp.bfloat16)
-    turned = jnp.dot(chosen, mixed, preferred_element_type=jnp.float32).astype(jnp.bfloat16)
+    turned = call(
+        turn_kernel,
+        bf16(width, docs * tb),
+        [SMEM, VMEM],
+        VMEM,
+        flops=2 * docs * tb * width * width,
+        moved=4 * 2**20,
+        name="turn",
+    )(me, mixed)
 
     sums = jnp.concatenate([pool.reshape(docs, width), target], axis=0)
     sums = sums + swap(sums, "ctx", 1)
@@ -401,13 +416,13 @@
     sums = (terms[0] + terms[2]) + (terms[1] + terms[3])
     emb, rinv, target = call(
         norm_kernel,
-        (f32(docs, width), f32(docs, 128), f32(docs, width)),
-        [SMEM, VMEM, VMEM],
+        (f32(2 * docs, width), f32(2 * docs, 128), f32(docs, width)),
+        [VMEM] * 4,
         (VMEM,) * 3,
         limit=4,
         name="norm",
-    )(lengths, sums, swap(sums, "ctx", 2))
-    embs = around(jnp.concatenate([emb, swap(emb, "dp", 4)], axis=0), from_y)
+    )(*around(sums, from_z))
+    embs = around(emb, from_y)
     wanted = positive.reshape(2, 4, docs).transpose(1, 0, 2).reshape(all_docs, 1)
     everyone, state = call(
         functools.partial(score_kernel, docs),
@@ -420,7 +435,7 @@
     )(me, wanted, *embs, *tables)
     product, stats = call(
         functools.partial(batch_kernel, docs),
-        (f32(docs, all_docs), f32(8, all_docs)),
+        (f32(2 * docs, all_docs), f32(8, all_docs)),
         [SMEM, VMEM, VMEM],
         (VMEM, VMEM),
         limit=4,
@@ -428,18 +443,19 @@
     )(me, emb, everyone)
     state = merge(docs, width, [state, swap(state, "ctx", 1)])
     state = merge(docs, width, around(state, from_x))
-    state = merge(docs, width, [state, swap(state, "ctx", 2)])
     half = width // 2
     keep, send, loss = call(
         grad_kernel,
         (f32(half, width), f32(half, width), f32(8, 128)),
-        [SMEM, SMEM] + [VMEM] * 11,
+        [SMEM, SMEM] + [VMEM] * 12,
         (VMEM,) * 3,
         flops=2 * docs * tb * width * width,
         moved=8 * 2**20,
         scratch_shapes=[pltpu.VMEM((docs * tb, width), jnp.bfloat16)],
         name="grad",
-    )(me, lengths, state, emb, rinv, everyone, target, product, stats, gain, normed, rstd, turned)
+    )(
+        me, lengths, state, swap(state, "ctx", 2), emb, rinv, everyone, target, product, stats, gain, normed, rstd, turned,
+    )
     keep, *sends = sum_and_split([keep, swap(send, "ctx", 1)], jnp.bfloat16)
     got = [from_y(piece, -(k + 1)) for k, piece in enumerate(sends)]
     keep, *sends = sum_and_split([keep] + got, jnp.float32)

time: 165 us -> 173 us (1.048)
  waiting for transfers between devices: 53.6 us -> 38.6 us
  starting transfers between devices: 47.5 us -> 62 us
  local copies, waits for them, and re-layouts: 14.2 us -> 23.4 us
    ppermute x9, waiting for transfers between devices: 23 us -> 12.5 us  [from_y(): lax.ppermute(value, 'dp', [(d & 4 | d + k & 3, d) for d in range(lax.axis...]
    ppermute x7 -> x5, starting transfers between devices: 6.15 us -> 15.8 us  [swap(): lax.ppermute(value, axis, [(i, i ^ bits) for i in range(lax.axis_size(axi...]
    unnamed x38 -> x54, local copies, waits for them, and re-layouts: 10.1 us -> 19 us
    ppermute x7 -> x5, waiting for transfers between devices: 17.8 us -> 10.8 us  [swap(): lax.ppermute(value, axis, [(i, i ^ bits) for i in range(lax.axis_size(axi...]
    ppermute x3 -> x6, starting transfers between devices: 4.4 us -> 9.53 us  [from_z(): return lax.ppermute(value, ('dp', 'ctx'), pairs)]
    ppermute x3 -> x6, waiting for transfers between devices: 2.7 us -> 5.1 us  [from_z(): return lax.ppermute(value, ('dp', 'ctx'), pairs)]
    ppermute x9, starting transfers between devices: 9.62 us -> 12 us  [from_y(): lax.ppermute(value, 'dp', [(d & 4 | d + k & 3, d) for d in range(lax.axis...]
    pallas_call x2 -> x3, Pallas kernels: 1.48 us -> 3.57 us  [the longest x1 2.62 us: shards(): call(turn_kernel, bf16(width, docs * tb), [SMEM, VMEM], VMEM, flops=2 * d...]
  transfers between devices with their start and end apart: 32 -> 33, of which waited for: 24 -> 20; matrix products, arithmetic and copies ran while one was open for 11% -> 8% of each run, Pallas kernels for 10% -> 18%
where the time goes in v1:
time: 173 us; the launch traced here: 172 us
  starting transfers between devices  62 us (36%)
  waiting for transfers between devices  38.6 us (22%)
  Pallas kernels  37.4 us (22%)
  local copies, waits for them, and re-layouts  23.4 us (14%)
  matrix products  8.33 us (5%)
    pallas_call x2, Pallas kernels, attend(): call(functools.partial(attend_kernel, first), out_shape, in_specs, (here(...  28 us
    unnamed x54, local copies, waits for them, and re-layouts  19 us
    ppermute x5, starting transfers between devices, swap(): lax.ppermute(value, axis, [(i, i ^ bits) for i in range(lax.axis_size(axi...  15.8 us
    ppermute x9, starting transfers between devices, from_x(): lax.ppermute(value, 'ctx', [((c + 4 * k) % size, c) for c in range(size)])  13.8 us
    ppermute x9, waiting for transfers between devices, from_y(): lax.ppermute(value, 'dp', [(d & 4 | d + k & 3, d) for d in range(lax.axis...  12.5 us
    ppermute x9, starting transfers between devices, from_y(): lax.ppermute(value, 'dp', [(d & 4 | d + k & 3, d) for d in range(lax.axis...  12 us
    ppermute x2, starting transfers between devices, shards(): lax.ppermute(part, 'ctx', [((i + 1) % n_ctx, i) for i in range(n_ctx)])  11 us
    ppermute x5, waiting for transfers between devices, swap(): lax.ppermute(value, axis, [(i, i ^ bits) for i in range(lax.axis_size(axi...  10.8 us
  transfers between devices with their start and end apart: 33, of which 20 were waited for; matrix products, arithmetic and copies ran while one was open for 8% of the time, Pallas kernels for 18%

profile of v1, /device:TPU:0, one launch (start us, length us, event | category | flops | bytes accessed | tf_op | source)
XLA Modules:
  0.0 171.9 jit_solution(15281575960182326583)
XLA Ops:
  0.6 2.8 %fusion.7 = (bf16[2,256,768]{2,1,0:T(8,128)(2,1)}, bf16[2,256,768]{2,1,0:T(8,128)(2,1)}) fusion(bf16[4,256,768]{2,1,0:T(8,128)(2,1)} %tok.3), kind=kLoop, calls=%fused_computation.38 | loop fusion | bytes 3145728 | tf_op jit(solution)/shard_map/slice | solution.py:376
  3.5 5.6 %collective-permute-start.3 = (bf16[2,256,768]{2,1,0:T(8,128)(2,1)}, bf16[2,256,768]{2,1,0:T(8,128)(2,1)}, u32[]{:S(2)}, u32[]{:S(2)}) collective-permute-start(bf16[2,256,768]{2,1,0:T(8,128)(2,1)} %get-tuple-element.41), channel_id=1, source_target_pairs={{1,0},{2,1},{3,2},{4,3},{5,4},{6,5},{7,6},{8,7},{9,8},{10,9},{11,1... | collective-permute-start | bytes 2359304 | tf_op jit(solution)/shard_map/ppermute | solution.py:380
  9.1 5.4 %collective-permute-start.1 = (bf16[2,256,768]{2,1,0:T(8,128)(2,1)}, bf16[2,256,768]{2,1,0:T(8,128)(2,1)}, u32[]{:S(2)}, u32[]{:S(2)}) collective-permute-start(bf16[2,256,768]{2,1,0:T(8,128)(2,1)} %get-tuple-element.40), channel_id=1, source_target_pairs={{1,0},{2,1},{3,2},{4,3},{5,4},{6,5},{7,6},{8,7},{9,8},{10,9},{11,1... | collective-permute-start | bytes 2359304 | tf_op jit(solution)/shard_map/ppermute | solution.py:380
  14.4 1.8 %collective-permute-start.4 = (bf16[128,768]{1,0:T(8,128)(2,1)}, bf16[128,768]{1,0:T(8,128)(2,1)}, u32[]{:S(2)}, u32[]{:S(2)}) collective-permute-start(bf16[128,768]{1,0:T(8,128)(2,1)} %param.11), channel_id=1, source_target_pairs={{0,64},{16,80},{32,96},{48,112},{64,0},{80,16},{96,32},{112,48},{1... | collective-permute-start | bytes 589832 | tf_op jit(solution)/shard_map/ppermute | solution.py:25
  16.2 5.8 %convolution_convert_fusion = bf16[1024,1536]{1,0:T(8,128)(2,1)} fusion(bf16[1024,768]{1,0:T(8,128)(2,1)S(1)} %bitcast.20, bf16[768,2304]{1,0:T(8,128)(2,1)} %w_k.3), kind=kOutput, calls=%fused_computation | convolution fusion | flops 2417491968 | bytes 7077888 | tf_op jit(solution)/shard_map/dot_general | solution.py:386
  22.0 2.6 %convolution_convert_fusion.1.v_turned = bf16[768,1024]{1,0:T(8,128)(2,1)} fusion(bf16[1024,768]{1,0:T(8,128)(2,1)S(1)} %bitcast.21, bf16[768,2304]{1,0:T(8,128)(2,1)S(1)} %copy-done), kind=kOutput, calls=%fused_computation.2 | convolution fusion | flops 1208745984 | bytes 4325376 | tf_op jit(solution)/shard_map/dot_general | solution.py:387
  24.6 1.1 slice.54
  25.7 2.4 %copy.22 = bf16[768,768]{0,1:T(8,128)(2,1)} copy(bf16[768,768]{1,0:T(8,128)(2,1)} %slice.54) | data formatting | bytes 2359296
  29.1 4.6 %collective-permute-done.4 = bf16[128,768]{1,0:T(8,128)(2,1)} collective-permute-done((bf16[128,768]{1,0:T(8,128)(2,1)}, bf16[128,768]{1,0:T(8,128)(2,1)}, u32[]{:S(2)}, u32[]{:S(2)}) %collective-permute-start.4) | collective-permute-done | bytes 196640 | tf_op jit(solution)/shard_map/ppermute | solution.py:25
  34.6 3.1 %collective-permute-start.5 = (bf16[256,768]{1,0:T(8,128)(2,1)S(1)}, bf16[256,768]{1,0:T(8,128)(2,1)S(1)}, u32[]{:S(2)}, u32[]{:S(2)}) collective-permute-start(bf16[256,768]{1,0:T(8,128)(2,1)S(1)} %constant_dynamic-update-slice_fusion.refs_0_.t0), channel_id=1, source_target_pairs={{16,0},{32,16},{48,32},{0,48},{80,64},{96,80},{112,96},{64,112},{1... | collective-permute-start | bytes 1179656 | tf_op jit(solution)/shard_map/ppermute | solution.py:34
  39.3 1.4 copy-done.2
  40.7 1.9 %copy-done.3 = bf16[1024,1536]{1,0:T(8,128)(2,1)S(1)} copy-done((bf16[1024,1536]{1,0:T(8,128)(2,1)S(1)}, bf16[1024,1536]{1,0:T(8,128)(2,1)}, u32[]{:S(2)}) %copy-start.3) | copy-done | bytes 3145752
  42.6 1.3 copy-done.5
  43.9 1.4 copy-done.6
  45.3 1.3 copy-done.7
  46.6 14.0 %attend.2 = (bf16[4,256,768]{2,1,0:T(8,128)(2,1)}, bf16[768,1024]{1,0:T(8,128)(2,1)S(1)}, bf16[4,256,768]{2,1,0:T(8,128)(2,1)S(1)}, f32[4,256,128]{2,1,0:T(8,128)S(1)}, f32[4,1,768]{2,1,0:T(1,128)S(1)}) custom-call(s32[2]{0:T(128)S(1)} %pad_add_fusion.me, s32[4]{0:T(128)S(1)} %copy-done.22, bf16[4,256,768]{2,1,0:T(8,128)(2,1)S(1)} %copy-done.2, ...), custom_call_target="tpu_custom_call" | custom-call | flops 3019898880 | bytes 8388608 | tf_op jit(solution)/shard_map/attend/pallas_call | solution.py:169
  60.6 13.9 %attend.3 = (bf16[4,256,768]{2,1,0:T(8,128)(2,1)}, bf16[768,1024]{1,0:T(8,128)(2,1)S(1)}, bf16[4,256,768]{2,1,0:T(8,128)(2,1)S(1)}, f32[4,256,128]{2,1,0:T(8,128)S(1)}, f32[4,1,768]{2,1,0:T(1,128)S(1)}) custom-call(s32[2]{0:T(128)S(1)} %pad_add_fusion.me, ...), custom_call_target="tpu_custom_call", output_to_operand_aliasing={{0}: (11, {}), {1}: (12, {}), {2}: (13, {}), {3}: (14, {}),... | custom-call | flops 3019898880 | bytes 8388608 | tf_op jit(solution)/shard_map/attend/pallas_call | solution.py:169
  74.6 1.1 copy-done.16
  75.7 1.2 copy-done.18
  78.8 13.2 %collective-permute-start.8 = (f32[8,768]{1,0:T(8,128)S(1)}, f32[8,768]{1,0:T(8,128)S(1)}, u32[]{:S(2)}, u32[]{:S(2)}) collective-permute-start(f32[8,768]{1,0:T(8,128)S(1)} %pad_maximum_fusion), channel_id=1, source_target_pairs={{0,1},{1,0},{2,3},{3,2},{4,5},{5,4},{6,7},{7,6},{8,9},{9,8},{10,11... | collective-permute-start | bytes 73736 | tf_op jit(solution)/shard_map/ppermute | solution.py:25
  92.8 3.0 %collective-permute-start.10 = (f32[8,768]{1,0:T(8,128)S(1)}, f32[8,768]{1,0:T(8,128)S(1)}, u32[]{:S(2)}, u32[]{:S(2)}) collective-permute-start(f32[8,768]{1,0:T(8,128)S(1)} %fusion.4), channel_id=1, source_target_pairs={{4,0},{5,1},{6,2},{7,3},{8,4},{9,5},{10,6},{11,7},{12,8},{13,9},{1... | collective-permute-start | bytes 73736 | tf_op jit(solution)/shard_map/ppermute | solution.py:30
  95.9 2.3 %collective-permute-start.9 = (f32[8,768]{1,0:T(8,128)S(1)}, f32[8,768]{1,0:T(8,128)S(1)}, u32[]{:S(2)}, u32[]{:S(2)}) collective-permute-start(f32[8,768]{1,0:T(8,128)S(1)} %fusion.4), channel_id=1, source_target_pairs={{8,0},{9,1},{10,2},{11,3},{12,4},{13,5},{14,6},{15,7},{0,8},{1,9},... | collective-permute-start | bytes 73736 | tf_op jit(solution)/shard_map/ppermute | solution.py:30
  98.2 2.7 %collective-permute-done.11 = f32[8,768]{1,0:T(8,128)S(1)} collective-permute-done((f32[8,768]{1,0:T(8,128)S(1)}, f32[8,768]{1,0:T(8,128)S(1)}, u32[]{:S(2)}, u32[]{:S(2)}) %collective-permute-start.11) | collective-permute-done | bytes 24608 | tf_op jit(solution)/shard_map/ppermute | solution.py:30
  101.2 2.0 %collective-permute-start.12 = (f32[8,768]{1,0:T(8,128)S(1)}, f32[8,768]{1,0:T(8,128)S(1)}, u32[]{:S(2)}, u32[]{:S(2)}) collective-permute-start(f32[8,768]{1,0:T(8,128)S(1)} %add_add_fusion.1.s0), channel_id=1, source_target_pairs={{64,0},{65,1},{66,2},{67,3},{68,4},{69,5},{70,6},{71,7},{72,8},{73... | collective-permute-start | bytes 73736 | tf_op jit(solution)/shard_map/ppermute | solution.py:44
  103.2 1.9 %collective-permute-start.13 = (f32[8,768]{1,0:T(8,128)S(1)}, f32[8,768]{1,0:T(8,128)S(1)}, u32[]{:S(2)}, u32[]{:S(2)}) collective-permute-start(f32[8,768]{1,0:T(8,128)S(1)} %add_add_fusion.1.s0), channel_id=1, source_target_pairs={{2,0},{3,1},{0,2},{1,3},{6,4},{7,5},{4,6},{5,7},{10,8},{11,9},{8,1... | collective-permute-start | bytes 73736 | tf_op jit(solution)/shard_map/ppermute | solution.py:44
  105.1 1.3 collective-permute-start.14
  106.4 2.1 %collective-permute-done.13.s2 = f32[8,768]{1,0:T(8,128)S(1)} collective-permute-done((f32[8,768]{1,0:T(8,128)S(1)}, f32[8,768]{1,0:T(8,128)S(1)}, u32[]{:S(2)}, u32[]{:S(2)}) %collective-permute-start.13) | collective-permute-done | bytes 24608 | tf_op jit(solution)/shard_map/ppermute | solution.py:44
  108.5 1.6 collective-permute-done.14.s3
  110.2 2.3 %collective-permute-start.15 = (f32[8,768]{1,0:T(8,128)S(1)}, f32[8,768]{1,0:T(8,128)S(1)}, u32[]{:S(2)}, u32[]{:S(2)}) collective-permute-start(f32[8,768]{1,0:T(8,128)S(1)} %get-tuple-element.52.e0.emb), channel_id=1, source_target_pairs={{16,0},{32,16},{48,32},{0,48},{80,64},{96,80},{112,96},{64,112},{1... | collective-permute-start | bytes 73736 | tf_op jit(solution)/shard_map/ppermute | solution.py:34
  112.5 1.7 collective-permute-start.16
  114.4 3.5 %collective-permute-done.16.e2 = f32[8,768]{1,0:T(8,128)S(1)} collective-permute-done((f32[8,768]{1,0:T(8,128)S(1)}, f32[8,768]{1,0:T(8,128)S(1)}, u32[]{:S(2)}, u32[]{:S(2)}) %collective-permute-start.16) | collective-permute-done | bytes 24608 | tf_op jit(solution)/shard_map/ppermute | solution.py:34
  117.8 1.4 collective-permute-done.17.e3
  123.2 1.7 %score.1 = (f32[32,768]{1,0:T(8,128)S(1)}, f32[8,1024]{1,0:T(8,128)S(1)}) custom-call(s32[2]{0:T(128)S(1)} %pad_add_fusion.me, s32[32,1]{1,0:T(8,128)S(1)} %reshape.30.positive, f32[8,768]{1,0:T(8,128)S(1)} %get-tuple-element.52.e0.emb, f32[8,768]{1,0:T(8,128)S(1)} %collective-permute-done.15.e1, f32[8,768]{1,0:T(8,128)S(1)} %collective-permute-done.16.e2, ...), custom_call_target="tpu_custom_call" | custom-call | bytes 2097152 | tf_op jit(solution)/shard_map/score/pallas_call | solution.py:427
  125.1 1.2 collective-permute-done.18
  126.5 2.8 %collective-permute-start.19 = (f32[8,1024]{1,0:T(8,128)S(1)}, f32[8,1024]{1,0:T(8,128)S(1)}, u32[]{:S(2)}, u32[]{:S(2)}) collective-permute-start(f32[8,1024]{1,0:T(8,128)S(1)} %fusion.1), channel_id=1, source_target_pairs={{4,0},{5,1},{6,2},{7,3},{8,4},{9,5},{10,6},{11,7},{12,8},{13,9},{1... | collective-permute-start | bytes 98312 | tf_op jit(solution)/shard_map/ppermute | solution.py:30
  130.9 3.9 %collective-permute-done.20 = f32[8,1024]{1,0:T(8,128)S(1)} collective-permute-done((f32[8,1024]{1,0:T(8,128)S(1)}, f32[8,1024]{1,0:T(8,128)S(1)}, u32[]{:S(2)}, u32[]{:S(2)}) %collective-permute-start.20) | collective-permute-done | bytes 32800 | tf_op jit(solution)/shard_map/ppermute | solution.py:30
  135.8 2.6 %turn.1.turned = bf16[768,1024]{1,0:T(8,128)(2,1)S(1)} custom-call(s32[2]{0:T(128)S(1)} %pad_add_fusion.me, bf16[768,1024]{1,0:T(8,128)(2,1)S(1)} %copy-done.17), custom_call_target="tpu_custom_call" | custom-call | flops 1207959552 | bytes 4194304 | tf_op jit(solution)/shard_map/turn/pallas_call | solution.py:403
  139.3 1.4 collective-permute-done.22.other
  140.7 3.0 %grad.1 = (f32[384,768]{1,0:T(8,128)S(1)}, f32[384,768]{1,0:T(8,128)S(1)}, f32[8,128]{1,0:T(8,128)S(1)}) custom-call(s32[2]{0:T(128)S(1)} %pad_add_fusion.me, s32[4]{0:T(128)S(1)} %copy-done.22, f32[8,1024]{1,0:T(8,128)S(1)} %fusion.2.state, f32[8,1024]{1,0:T(8,128)S(1)} %collective-permute-done.22.other, f32[8,768]{1,0:T(8,128)S(1)} %get-tuple-element.52.e0.emb, ...), custom_call_target="tpu_custom_call" | custom-call | flops 1207959552 | bytes 8388608 | tf_op jit(solution)/shard_map/grad/pallas_call | solution.py:447
  143.7 2.8 %collective-permute-done.23.refs_1_ = f32[384,768]{1,0:T(8,128)S(1)} collective-permute-done((f32[384,768]{1,0:T(8,128)S(1)}, f32[384,768]{1,0:T(8,128)S(1)}, u32[]{:S(2)}, u32[]{:S(2)}) %collective-permute-start.23) | collective-permute-done | bytes 1179680 | tf_op jit(solution)/shard_map/ppermute | solution.py:25
  146.8 1.2 collective-permute-start.25
  148.0 2.1 %collective-permute-start.26 = (bf16[96,768]{1,0:T(8,128)(2,1)S(1)}, bf16[96,768]{1,0:T(8,128)(2,1)S(1)}, u32[]{:S(2)}, u32[]{:S(2)}) collective-permute-start(bf16[96,768]{1,0:T(8,128)(2,1)S(1)} %get-tuple-element.68), channel_id=1, source_target_pairs={{16,0},{32,16},{48,32},{0,48},{80,64},{96,80},{112,96},{64,112},{1... | collective-permute-start | bytes 442376 | tf_op jit(solution)/shard_map/ppermute | solution.py:34
  150.1 7.0 %collective-permute-done.24.refs_1_ = bf16[96,768]{1,0:T(8,128)(2,1)S(1)} collective-permute-done((bf16[96,768]{1,0:T(8,128)(2,1)S(1)}, bf16[96,768]{1,0:T(8,128)(2,1)S(1)}, u32[]{:S(2)}, u32[]{:S(2)}) %collective-permute-start.24) | collective-permute-done | bytes 147488 | tf_op jit(solution)/shard_map/ppermute | solution.py:34
  157.8 2.3 %collective-permute-start.28 = (f32[24,768]{1,0:T(8,128)S(1)}, f32[24,768]{1,0:T(8,128)S(1)}, u32[]{:S(2)}, u32[]{:S(2)}) collective-permute-start(f32[24,768]{1,0:T(8,128)S(1)} %get-tuple-element.71), channel_id=1, source_target_pairs={{8,0},{9,1},{10,2},{11,3},{12,4},{13,5},{14,6},{15,7},{0,8},{1,9},... | collective-permute-start | bytes 221192 | tf_op jit(solution)/shard_map/ppermute | solution.py:30
  160.1 2.3 %collective-permute-start.29 = (f32[24,768]{1,0:T(8,128)S(1)}, f32[24,768]{1,0:T(8,128)S(1)}, u32[]{:S(2)}, u32[]{:S(2)}) collective-permute-start(f32[24,768]{1,0:T(8,128)S(1)} %get-tuple-element.72), channel_id=1, source_target_pairs={{4,0},{5,1},{6,2},{7,3},{8,4},{9,5},{10,6},{11,7},{12,8},{13,9},{1... | collective-permute-start | bytes 221192 | tf_op jit(solution)/shard_map/ppermute | solution.py:30
  162.4 1.8 %collective-permute-done.27.refs_1_ = f32[24,768]{1,0:T(8,128)S(1)} collective-permute-done((f32[24,768]{1,0:T(8,128)S(1)}, f32[24,768]{1,0:T(8,128)S(1)}, u32[]{:S(2)}, u32[]{:S(2)}) %collective-permute-start.27) | collective-permute-done | bytes 73760 | tf_op jit(solution)/shard_map/ppermute | solution.py:30
  165.2 2.2 %collective-permute-start.31 = (f32[6,768]{1,0:T(8,128)S(1)}, f32[6,768]{1,0:T(8,128)S(1)}, u32[]{:S(2)}, u32[]{:S(2)}) collective-permute-start(f32[6,768]{1,0:T(8,128)S(1)} %get-tuple-element.75), channel_id=1, source_target_pairs={{2,0},{3,1},{0,2},{1,3},{6,4},{7,5},{4,6},{5,7},{10,8},{11,9},{8,1... | collective-permute-start | bytes 55304 | tf_op jit(solution)/shard_map/ppermute | solution.py:44
  167.5 1.9 %collective-permute-start.32 = (f32[6,768]{1,0:T(8,128)S(1)}, f32[6,768]{1,0:T(8,128)S(1)}, u32[]{:S(2)}, u32[]{:S(2)}) collective-permute-start(f32[6,768]{1,0:T(8,128)S(1)} %get-tuple-element.76), channel_id=1, source_target_pairs={{64,0},{65,1},{66,2},{67,3},{68,4},{69,5},{70,6},{71,7},{72,8},{73... | collective-permute-start | bytes 55304 | tf_op jit(solution)/shard_map/ppermute | solution.py:44
  (108 shorter events, 19.3 us)
Async XLA Ops:
  0.6 15.6 %copy-start.1 = (bf16[4,256,768]{2,1,0:T(8,128)(2,1)S(1)}, bf16[4,256,768]{2,1,0:T(8,128)(2,1)}, u32[]{:S(2)}) copy-start(bf16[4,256,768]{2,1,0:T(8,128)(2,1)} %tok.3) | copy-start | bytes 4718596
  3.5 34.2 %collective-permute-start.2 = (bf16[2,256,768]{2,1,0:T(8,128)(2,1)}, bf16[2,256,768]{2,1,0:T(8,128)(2,1)}, u32[]{:S(2)}, u32[]{:S(2)}) collective-permute-start(bf16[2,256,768]{2,1,0:T(8,128)(2,1)} %get-tuple-element.41), channel_id=1, source_target_pairs={{0,1},{1,2},{2,3},{3,4},{4,5},{5,6},{6,7},{7,8},{8,9},{9,10},{10,1... | collective-permute-start | bytes 2359304 | tf_op jit(solution)/shard_map/ppermute | solution.py:379
  3.5 34.8 %collective-permute-start.3 = (bf16[2,256,768]{2,1,0:T(8,128)(2,1)}, bf16[2,256,768]{2,1,0:T(8,128)(2,1)}, u32[]{:S(2)}, u32[]{:S(2)}) collective-permute-start(bf16[2,256,768]{2,1,0:T(8,128)(2,1)} %get-tuple-element.41), channel_id=1, source_target_pairs={{1,0},{2,1},{3,2},{4,3},{5,4},{6,5},{7,6},{8,7},{9,8},{10,9},{11,1... | collective-permute-start | bytes 2359304 | tf_op jit(solution)/shard_map/ppermute | solution.py:380
  9.1 51.5 %collective-permute-start = (bf16[2,256,768]{2,1,0:T(8,128)(2,1)}, bf16[2,256,768]{2,1,0:T(8,128)(2,1)}, u32[]{:S(2)}, u32[]{:S(2)}) collective-permute-start(bf16[2,256,768]{2,1,0:T(8,128)(2,1)} %get-tuple-element.40), channel_id=1, source_target_pairs={{0,1},{1,2},{2,3},{3,4},{4,5},{5,6},{6,7},{7,8},{8,9},{9,10},{10,1... | collective-permute-start | bytes 2359304 | tf_op jit(solution)/shard_map/ppermute | solution.py:379
  9.1 51.5 %collective-permute-start.1 = (bf16[2,256,768]{2,1,0:T(8,128)(2,1)}, bf16[2,256,768]{2,1,0:T(8,128)(2,1)}, u32[]{:S(2)}, u32[]{:S(2)}) collective-permute-start(bf16[2,256,768]{2,1,0:T(8,128)(2,1)} %get-tuple-element.40), channel_id=1, source_target_pairs={{1,0},{2,1},{3,2},{4,3},{5,4},{6,5},{7,6},{8,7},{9,8},{10,9},{11,1... | collective-permute-start | bytes 2359304 | tf_op jit(solution)/shard_map/ppermute | solution.py:380
  14.4 19.2 %collective-permute-start.4 = (bf16[128,768]{1,0:T(8,128)(2,1)}, bf16[128,768]{1,0:T(8,128)(2,1)}, u32[]{:S(2)}, u32[]{:S(2)}) collective-permute-start(bf16[128,768]{1,0:T(8,128)(2,1)} %param.11), channel_id=1, source_target_pairs={{0,64},{16,80},{32,96},{48,112},{64,0},{80,16},{96,32},{112,48},{1... | collective-permute-start | bytes 589832 | tf_op jit(solution)/shard_map/ppermute | solution.py:25
  16.2 5.8 %copy-start = (bf16[768,2304]{1,0:T(8,128)(2,1)S(1)}, bf16[768,2304]{1,0:T(8,128)(2,1)}, u32[]{:S(2)}) copy-start(bf16[768,2304]{1,0:T(8,128)(2,1)} %w_k.3) | copy-start | bytes 10616836
  25.7 13.6 %copy-start.22 = (s32[4]{0:T(128)S(1)}, s32[4]{0:T(128)}, u32[]{:S(2)}) copy-start(s32[4]{0:T(128)} %lengths.5) | copy-start | bytes 52
  34.6 43.1 %copy-start.8 = (bf16[256,768]{1,0:T(8,128)(2,1)}, bf16[256,768]{1,0:T(8,128)(2,1)S(1)}, u32[]{:S(2)}) copy-start(bf16[256,768]{1,0:T(8,128)(2,1)S(1)} %constant_dynamic-update-slice_fusion.refs_0_.t0) | copy-start | bytes 1179652
  34.6 43.1 %collective-permute-start.5 = (bf16[256,768]{1,0:T(8,128)(2,1)S(1)}, bf16[256,768]{1,0:T(8,128)(2,1)S(1)}, u32[]{:S(2)}, u32[]{:S(2)}) collective-permute-start(bf16[256,768]{1,0:T(8,128)(2,1)S(1)} %constant_dynamic-update-slice_fusion.refs_0_.t0), channel_id=1, source_target_pairs={{16,0},{32,16},{48,32},{0,48},{80,64},{96,80},{112,96},{64,112},{1... | collective-permute-start | bytes 1179656 | tf_op jit(solution)/shard_map/ppermute | solution.py:34
  37.7 40.0 %collective-permute-start.6 = (bf16[256,768]{1,0:T(8,128)(2,1)S(1)}, bf16[256,768]{1,0:T(8,128)(2,1)S(1)}, u32[]{:S(2)}, u32[]{:S(2)}) collective-permute-start(bf16[256,768]{1,0:T(8,128)(2,1)S(1)} %constant_dynamic-update-slice_fusion.refs_0_.t0), channel_id=1, source_target_pairs={{32,0},{48,16},{0,32},{16,48},{96,64},{112,80},{64,96},{80,112},{3... | collective-permute-start | bytes 1179656 | tf_op jit(solution)/shard_map/ppermute | solution.py:34
  38.3 39.4 %collective-permute-start.7 = (bf16[256,768]{1,0:T(8,128)(2,1)S(1)}, bf16[256,768]{1,0:T(8,128)(2,1)S(1)}, u32[]{:S(2)}, u32[]{:S(2)}) collective-permute-start(bf16[256,768]{1,0:T(8,128)(2,1)S(1)} %constant_dynamic-update-slice_fusion.refs_0_.t0), channel_id=1, source_target_pairs={{48,0},{0,16},{16,32},{32,48},{112,64},{64,80},{80,96},{96,112},{4... | collective-permute-start | bytes 1179656 | tf_op jit(solution)/shard_map/ppermute | solution.py:34
  39.3 1.4 copy-start.2
  40.7 1.9 %copy-start.3 = (bf16[1024,1536]{1,0:T(8,128)(2,1)S(1)}, bf16[1024,1536]{1,0:T(8,128)(2,1)}, u32[]{:S(2)}) copy-start(bf16[1024,1536]{1,0:T(8,128)(2,1)} %convolution_convert_fusion) | copy-start | bytes 9437188
  42.6 1.3 copy-start.5
  43.9 1.4 copy-start.6
  45.3 1.3 copy-start.7
  46.5 14.1 %copy-start.4 = (bf16[1024,1536]{1,0:T(8,128)(2,1)S(1)}, bf16[1024,1536]{1,0:T(8,128)(2,1)}, u32[]{:S(2)}) copy-start(bf16[1024,1536]{1,0:T(8,128)(2,1)} %convolution_convert_fusion) | copy-start | bytes 9437188
  60.6 17.1 %copy-start.23 = (s32[32]{0:T(128)S(1)}, s32[32]{0:T(128)}, u32[]{:S(2)}) copy-start(s32[32]{0:T(128)} %positive) | copy-start | bytes 388
  75.7 1.2 copy-start.18
  77.8 58.0 %copy-start.17 = (bf16[768,1024]{1,0:T(8,128)(2,1)S(1)}, bf16[768,1024]{1,0:T(8,128)(2,1)}, u32[]{:S(2)}) copy-start(bf16[768,1024]{1,0:T(8,128)(2,1)} %copy-done.16) | copy-start | bytes 4718596
  78.8 14.0 %collective-permute-start.8 = (f32[8,768]{1,0:T(8,128)S(1)}, f32[8,768]{1,0:T(8,128)S(1)}, u32[]{:S(2)}, u32[]{:S(2)}) collective-permute-start(f32[8,768]{1,0:T(8,128)S(1)} %pad_maximum_fusion), channel_id=1, source_target_pairs={{0,1},{1,0},{2,3},{3,2},{4,5},{5,4},{6,7},{7,6},{8,9},{9,8},{10,11... | collective-permute-start | bytes 73736 | tf_op jit(solution)/shard_map/ppermute | solution.py:25
  92.8 5.3 %collective-permute-start.10 = (f32[8,768]{1,0:T(8,128)S(1)}, f32[8,768]{1,0:T(8,128)S(1)}, u32[]{:S(2)}, u32[]{:S(2)}) collective-permute-start(f32[8,768]{1,0:T(8,128)S(1)} %fusion.4), channel_id=1, source_target_pairs={{4,0},{5,1},{6,2},{7,3},{8,4},{9,5},{10,6},{11,7},{12,8},{13,9},{1... | collective-permute-start | bytes 73736 | tf_op jit(solution)/shard_map/ppermute | solution.py:30
  95.9 5.0 %collective-permute-start.11 = (f32[8,768]{1,0:T(8,128)S(1)}, f32[8,768]{1,0:T(8,128)S(1)}, u32[]{:S(2)}, u32[]{:S(2)}) collective-permute-start(f32[8,768]{1,0:T(8,128)S(1)} %fusion.4), channel_id=1, source_target_pairs={{12,0},{13,1},{14,2},{15,3},{0,4},{1,5},{2,6},{3,7},{4,8},{5,9},{6... | collective-permute-start | bytes 73736 | tf_op jit(solution)/shard_map/ppermute | solution.py:30
  95.9 5.3 %collective-permute-start.9 = (f32[8,768]{1,0:T(8,128)S(1)}, f32[8,768]{1,0:T(8,128)S(1)}, u32[]{:S(2)}, u32[]{:S(2)}) collective-permute-start(f32[8,768]{1,0:T(8,128)S(1)} %fusion.4), channel_id=1, source_target_pairs={{8,0},{9,1},{10,2},{11,3},{12,4},{13,5},{14,6},{15,7},{0,8},{1,9},... | collective-permute-start | bytes 73736 | tf_op jit(solution)/shard_map/ppermute | solution.py:30
  101.2 5.2 %collective-permute-start.12 = (f32[8,768]{1,0:T(8,128)S(1)}, f32[8,768]{1,0:T(8,128)S(1)}, u32[]{:S(2)}, u32[]{:S(2)}) collective-permute-start(f32[8,768]{1,0:T(8,128)S(1)} %add_add_fusion.1.s0), channel_id=1, source_target_pairs={{64,0},{65,1},{66,2},{67,3},{68,4},{69,5},{70,6},{71,7},{72,8},{73... | collective-permute-start | bytes 73736 | tf_op jit(solution)/shard_map/ppermute | solution.py:44
  103.2 5.3 %collective-permute-start.13 = (f32[8,768]{1,0:T(8,128)S(1)}, f32[8,768]{1,0:T(8,128)S(1)}, u32[]{:S(2)}, u32[]{:S(2)}) collective-permute-start(f32[8,768]{1,0:T(8,128)S(1)} %add_add_fusion.1.s0), channel_id=1, source_target_pairs={{2,0},{3,1},{0,2},{1,3},{6,4},{7,5},{4,6},{5,7},{10,8},{11,9},{8,1... | collective-permute-start | bytes 73736 | tf_op jit(solution)/shard_map/ppermute | solution.py:44
  105.1 5.0 %collective-permute-start.14 = (f32[8,768]{1,0:T(8,128)S(1)}, f32[8,768]{1,0:T(8,128)S(1)}, u32[]{:S(2)}, u32[]{:S(2)}) collective-permute-start(f32[8,768]{1,0:T(8,128)S(1)} %add_add_fusion.1.s0), channel_id=1, source_target_pairs={{66,0},{67,1},{64,2},{65,3},{70,4},{71,5},{68,6},{69,7},{74,8},{75... | collective-permute-start | bytes 73736 | tf_op jit(solution)/shard_map/ppermute | solution.py:44
  110.2 4.2 %collective-permute-start.15 = (f32[8,768]{1,0:T(8,128)S(1)}, f32[8,768]{1,0:T(8,128)S(1)}, u32[]{:S(2)}, u32[]{:S(2)}) collective-permute-start(f32[8,768]{1,0:T(8,128)S(1)} %get-tuple-element.52.e0.emb), channel_id=1, source_target_pairs={{16,0},{32,16},{48,32},{0,48},{80,64},{96,80},{112,96},{64,112},{1... | collective-permute-start | bytes 73736 | tf_op jit(solution)/shard_map/ppermute | solution.py:34
  112.5 5.3 %collective-permute-start.16 = (f32[8,768]{1,0:T(8,128)S(1)}, f32[8,768]{1,0:T(8,128)S(1)}, u32[]{:S(2)}, u32[]{:S(2)}) collective-permute-start(f32[8,768]{1,0:T(8,128)S(1)} %get-tuple-element.52.e0.emb), channel_id=1, source_target_pairs={{32,0},{48,16},{0,32},{16,48},{96,64},{112,80},{64,96},{80,112},{3... | collective-permute-start | bytes 73736 | tf_op jit(solution)/shard_map/ppermute | solution.py:34
  114.2 5.0 %collective-permute-start.17 = (f32[8,768]{1,0:T(8,128)S(1)}, f32[8,768]{1,0:T(8,128)S(1)}, u32[]{:S(2)}, u32[]{:S(2)}) collective-permute-start(f32[8,768]{1,0:T(8,128)S(1)} %get-tuple-element.52.e0.emb), channel_id=1, source_target_pairs={{48,0},{0,16},{16,32},{32,48},{112,64},{64,80},{80,96},{96,112},{4... | collective-permute-start | bytes 73736 | tf_op jit(solution)/shard_map/ppermute | solution.py:34
  125.0 1.3 collective-permute-start.18
  126.5 4.4 %collective-permute-start.19 = (f32[8,1024]{1,0:T(8,128)S(1)}, f32[8,1024]{1,0:T(8,128)S(1)}, u32[]{:S(2)}, u32[]{:S(2)}) collective-permute-start(f32[8,1024]{1,0:T(8,128)S(1)} %fusion.1), channel_id=1, source_target_pairs={{4,0},{5,1},{6,2},{7,3},{8,4},{9,5},{10,6},{11,7},{12,8},{13,9},{1... | collective-permute-start | bytes 98312 | tf_op jit(solution)/shard_map/ppermute | solution.py:30
  129.3 5.5 %collective-permute-start.20 = (f32[8,1024]{1,0:T(8,128)S(1)}, f32[8,1024]{1,0:T(8,128)S(1)}, u32[]{:S(2)}, u32[]{:S(2)}) collective-permute-start(f32[8,1024]{1,0:T(8,128)S(1)} %fusion.1), channel_id=1, source_target_pairs={{8,0},{9,1},{10,2},{11,3},{12,4},{13,5},{14,6},{15,7},{0,8},{1,9},... | collective-permute-start | bytes 98312 | tf_op jit(solution)/shard_map/ppermute | solution.py:30
  129.3 5.5 %collective-permute-start.21 = (f32[8,1024]{1,0:T(8,128)S(1)}, f32[8,1024]{1,0:T(8,128)S(1)}, u32[]{:S(2)}, u32[]{:S(2)}) collective-permute-start(f32[8,1024]{1,0:T(8,128)S(1)} %fusion.1), channel_id=1, source_target_pairs={{12,0},{13,1},{14,2},{15,3},{0,4},{1,5},{2,6},{3,7},{4,8},{5,9},{6... | collective-permute-start | bytes 98312 | tf_op jit(solution)/shard_map/ppermute | solution.py:30
  135.1 5.5 %collective-permute-start.22 = (f32[8,1024]{1,0:T(8,128)S(1)}, f32[8,1024]{1,0:T(8,128)S(1)}, u32[]{:S(2)}, u32[]{:S(2)}) collective-permute-start(f32[8,1024]{1,0:T(8,128)S(1)} %fusion.2.state), channel_id=1, source_target_pairs={{0,2},{1,3},{2,0},{3,1},{4,6},{5,7},{6,4},{7,5},{8,10},{9,11},{10,... | collective-permute-start | bytes 98312 | tf_op jit(solution)/shard_map/ppermute | solution.py:25
  135.8 4.9 %copy-start.19 = (bf16[4,256,768]{2,1,0:T(8,128)(2,1)S(1)}, bf16[4,256,768]{2,1,0:T(8,128)(2,1)}, u32[]{:S(2)}) copy-start(bf16[4,256,768]{2,1,0:T(8,128)(2,1)} %copy-done.18) | copy-start | bytes 4718596
  135.8 4.9 %copy-start.21 = (f32[4,256,128]{2,1,0:T(8,128)S(1)}, f32[4,256,128]{2,1,0:T(8,128)}, u32[]{:S(2)}) copy-start(f32[4,256,128]{2,1,0:T(8,128)} %copy-done.20) | copy-start | bytes 1572868
  143.6 2.9 %collective-permute-start.23 = (f32[384,768]{1,0:T(8,128)S(1)}, f32[384,768]{1,0:T(8,128)S(1)}, u32[]{:S(2)}, u32[]{:S(2)}) collective-permute-start(f32[384,768]{1,0:T(8,128)S(1)} %get-tuple-element.64), channel_id=1, source_target_pairs={{0,1},{1,0},{2,3},{3,2},{4,5},{5,4},{6,7},{7,6},{8,9},{9,8},{10,11... | collective-permute-start | bytes 3538952 | tf_op jit(solution)/shard_map/ppermute | solution.py:25
  146.7 10.3 %collective-permute-start.24 = (bf16[96,768]{1,0:T(8,128)(2,1)S(1)}, bf16[96,768]{1,0:T(8,128)(2,1)S(1)}, u32[]{:S(2)}, u32[]{:S(2)}) collective-permute-start(bf16[96,768]{1,0:T(8,128)(2,1)S(1)} %get-tuple-element.66), channel_id=1, source_target_pairs={{48,0},{0,16},{16,32},{32,48},{112,64},{64,80},{80,96},{96,112},{4... | collective-permute-start | bytes 442376 | tf_op jit(solution)/shard_map/ppermute | solution.py:34
  146.8 10.2 %collective-permute-start.25 = (bf16[96,768]{1,0:T(8,128)(2,1)S(1)}, bf16[96,768]{1,0:T(8,128)(2,1)S(1)}, u32[]{:S(2)}, u32[]{:S(2)}) collective-permute-start(bf16[96,768]{1,0:T(8,128)(2,1)S(1)} %get-tuple-element.67), channel_id=1, source_target_pairs={{32,0},{48,16},{0,32},{16,48},{96,64},{112,80},{64,96},{80,112},{3... | collective-permute-start | bytes 442376 | tf_op jit(solution)/shard_map/ppermute | solution.py:34
  148.0 9.7 %collective-permute-start.26 = (bf16[96,768]{1,0:T(8,128)(2,1)S(1)}, bf16[96,768]{1,0:T(8,128)(2,1)S(1)}, u32[]{:S(2)}, u32[]{:S(2)}) collective-permute-start(bf16[96,768]{1,0:T(8,128)(2,1)S(1)} %get-tuple-element.68), channel_id=1, source_target_pairs={{16,0},{32,16},{48,32},{0,48},{80,64},{96,80},{112,96},{64,112},{1... | collective-permute-start | bytes 442376 | tf_op jit(solution)/shard_map/ppermute | solution.py:34
  157.8 6.4 %collective-permute-start.27 = (f32[24,768]{1,0:T(8,128)S(1)}, f32[24,768]{1,0:T(8,128)S(1)}, u32[]{:S(2)}, u32[]{:S(2)}) collective-permute-start(f32[24,768]{1,0:T(8,128)S(1)} %get-tuple-element.70), channel_id=1, source_target_pairs={{12,0},{13,1},{14,2},{15,3},{0,4},{1,5},{2,6},{3,7},{4,8},{5,9},{6... | collective-permute-start | bytes 221192 | tf_op jit(solution)/shard_map/ppermute | solution.py:30
  157.8 6.3 %collective-permute-start.28 = (f32[24,768]{1,0:T(8,128)S(1)}, f32[24,768]{1,0:T(8,128)S(1)}, u32[]{:S(2)}, u32[]{:S(2)}) collective-permute-start(f32[24,768]{1,0:T(8,128)S(1)} %get-tuple-element.71), channel_id=1, source_target_pairs={{8,0},{9,1},{10,2},{11,3},{12,4},{13,5},{14,6},{15,7},{0,8},{1,9},... | collective-permute-start | bytes 221192 | tf_op jit(solution)/shard_map/ppermute | solution.py:30
  160.1 4.9 %collective-permute-start.29 = (f32[24,768]{1,0:T(8,128)S(1)}, f32[24,768]{1,0:T(8,128)S(1)}, u32[]{:S(2)}, u32[]{:S(2)}) collective-permute-start(f32[24,768]{1,0:T(8,128)S(1)} %get-tuple-element.72), channel_id=1, source_target_pairs={{4,0},{5,1},{6,2},{7,3},{8,4},{9,5},{10,6},{11,7},{12,8},{13,9},{1... | collective-permute-start | bytes 221192 | tf_op jit(solution)/shard_map/ppermute | solution.py:30
  165.1 5.1 %collective-permute-start.30 = (f32[6,768]{1,0:T(8,128)S(1)}, f32[6,768]{1,0:T(8,128)S(1)}, u32[]{:S(2)}, u32[]{:S(2)}) collective-permute-start(f32[6,768]{1,0:T(8,128)S(1)} %get-tuple-element.74), channel_id=1, source_target_pairs={{66,0},{67,1},{64,2},{65,3},{70,4},{71,5},{68,6},{69,7},{74,8},{75... | collective-permute-start | bytes 55304 | tf_op jit(solution)/shard_map/ppermute | solution.py:44
  165.2 5.3 %collective-permute-start.31 = (f32[6,768]{1,0:T(8,128)S(1)}, f32[6,768]{1,0:T(8,128)S(1)}, u32[]{:S(2)}, u32[]{:S(2)}) collective-permute-start(f32[6,768]{1,0:T(8,128)S(1)} %get-tuple-element.75), channel_id=1, source_target_pairs={{2,0},{3,1},{0,2},{1,3},{6,4},{7,5},{4,6},{5,7},{10,8},{11,9},{8,1... | collective-permute-start | bytes 55304 | tf_op jit(solution)/shard_map/ppermute | solution.py:44
  167.5 3.8 %collective-permute-start.32 = (f32[6,768]{1,0:T(8,128)S(1)}, f32[6,768]{1,0:T(8,128)S(1)}, u32[]{:S(2)}, u32[]{:S(2)}) collective-permute-start(f32[6,768]{1,0:T(8,128)S(1)} %get-tuple-element.76), channel_id=1, source_target_pairs={{64,0},{65,1},{66,2},{67,3},{68,4},{69,5},{70,6},{71,7},{72,8},{73... | collective-permute-start | bytes 55304 | tf_op jit(solution)/shard_map/ppermute | solution.py:44
  (10 other events, 9.9 us)

commit v2 on v1

--- a/solution.py
+++ b/solution.py
@@ -44,11 +44,30 @@
     return lax.ppermute(value, ("dp", "ctx"), pairs)
 
 
+def from_plane(value, k, last):
+    n_dp, n_ctx = lax.axis_size("dp"), lax.axis_size("ctx")
+    pairs = []
+    for d in range(n_dp):
+        for c in range(n_ctx):
+            along_y = (c & 1 == 1) == last
+            source = ((d & 4) | ((d + k) & 3), c) if along_y else (d, (c + 4 * k) % n_ctx)
+            pairs.append((source[0] * n_ctx + source[1], d * n_ctx + c))
+    return lax.ppermute(value, ("dp", "ctx"), pairs)
+
+
 def around(value, fetch):
     return [value] + [fetch(value, k) for k in (1, 2, 3)]
 
 
-def call(kernel, out_shape, in_specs, out_specs, limit=24, flops=0, moved=0, **keywords):
+def here():
+    return lax.axis_index("dp"), lax.axis_index("ctx")
+
+
+def in_hbm(value):
+    return pltpu.with_memory_space_constraint(value, pltpu.HBM)
+
+
+def call(kernel, out_shape, in_specs, out_specs, limit=16, flops=0, moved=0, **keywords):
     return pl.pallas_call(
         kernel,
         out_shape=out_shape,
@@ -89,12 +108,12 @@
 
 
 def attend_kernel(
-    first, me, lengths, tok, left, right, qk, v_turned, w_k, w_v_turned, w_out, gain, *refs
+    first, lengths, tok, left, right, qk, v_turned, w_k, w_v_turned, w_out, gain, *refs
 ):
     hidden, mixed, normed, rstd_out, pool, keys, values, dist = refs[-8:]
     tb, width = tok.shape[1:]
     ext = tb + 2 * WIN
-    start, length = me[1] * tb, lengths[first + pl.program_id(0)]
+    start, length = lax.axis_index("ctx") * tb, lengths[first + pl.program_id(0)]
     rows = jnp.concatenate([left[0], right[0]], axis=0)
     new = jnp.dot(rows, w_k[...], preferred_element_type=jnp.float32).astype(jnp.bfloat16)
     keys[0:WIN] = new[0:WIN]
@@ -140,7 +159,7 @@
     centred = summed - jnp.mean(summed, axis=1, keepdims=True)
     rstd = lax.rsqrt(jnp.mean(centred * centred, axis=1, keepdims=True) + 1e-05)
     unit = centred * rstd
-    hidden_f = unit * gain[...]
+    hidden_f = unit * gain[...].reshape(1, width)
     hidden[0] = hidden_f.astype(jnp.bfloat16)
     normed[0] = unit.astype(jnp.bfloat16)
     rstd_out[0] = jnp.broadcast_to(rstd, rstd_out.shape[1:])
@@ -148,19 +167,19 @@
     pool[0] = jnp.sum(jnp.where(keep, hidden_f, 0.0), axis=0, keepdims=True) / length.astype(jnp.float32)
 
 
-def attend(first, before, me, lengths, tokens, left, right, qk, v_turned, w_qkv, w_v_turned, w_out, gain):
+def attend(first, before, lengths, tokens, left, right, qk, v_turned, w_qkv, w_v_turned, w_out, gain):
     docs, tb, width = tokens.shape
     ext = tb + 2 * WIN
-    here = lambda *s: pl.BlockSpec((1,) + s, lambda i: (first + i, 0, 0))
+    at = lambda *s: pl.BlockSpec((1,) + s, lambda i: (first + i, 0, 0))
     chunk = lambda *s: pl.BlockSpec((1,) + s, lambda i: (i, 0, 0))
     column = pl.BlockSpec((width, tb), lambda i: (0, first + i))
-    fixed = lambda s, at=(0, 0): pl.BlockSpec(s, lambda i: at, pipeline_mode=pl.Buffered(1))
+    fixed = lambda s, place=(0, 0): pl.BlockSpec(s, lambda i: place, pipeline_mode=pl.Buffered(1))
     out_shape = (bf16(docs, tb, width), bf16(width, docs * tb), bf16(docs, tb, width), f32(docs, tb, 128), f32(docs, 1, width))
     in_specs = [
-        SMEM, SMEM, here(tb, width), chunk(WIN, width), chunk(WIN, width), here(tb, 2 * width), column,
-        fixed((width, width), (0, 1)), fixed((width, width)), fixed((width, width)), fixed((1, width)),
+        SMEM, at(tb, width), chunk(WIN, width), chunk(WIN, width), at(tb, 2 * width), column,
+        fixed((width, width), (0, 1)), fixed((width, width)), fixed((width, width)), VMEM,
     ]
-    operands = [me, lengths, tokens, left, right, qk, v_turned, w_qkv, w_v_turned, w_out, gain]
+    operands = [lengths, tokens, left, right, qk, v_turned, w_qkv, w_v_turned, w_out, gain]
     aliases = {}
     if before is not None:
         aliases = {len(operands) + k: k for k in range(len(out_shape))}
@@ -170,8 +189,8 @@
         functools.partial(attend_kernel, first),
         out_shape,
         in_specs,
-        (here(tb, width), column, here(tb, width), here(tb, 128), here(1, width)),
-        limit=32,
+        (at(tb, width), column, at(tb, width), at(tb, 128), at(1, width)),
+        limit=30,
         flops=CHUNK * 5 * 2 * tb * ext * width,
         moved=8 * 2**20,
         grid=(CHUNK,),
@@ -185,37 +204,99 @@
     )(*operands)
 
 
-def row_ids(me, k, rows, shape, dim):
+def prepare_kernel(tok, w, qk, v_turned, w_v_turned):
+    width = tok.shape[2]
+
+    @pl.when(pl.program_id(0) == 0)
+    def _():
+        w_v_turned[...] = w[:, 2 * width :].T
+
+    rows = tok[0]
+    qk[0] = jnp.dot(rows, w[:, 0 : 2 * width], preferred_element_type=jnp.float32).astype(jnp.bfloat16)
+    v_turned[...] = lax.dot_general(w_v_turned[...], rows, NT, preferred_element_type=jnp.float32).astype(jnp.bfloat16)
+
+
+def prepare(tokens, w_qkv):
+    docs, tb, width = tokens.shape
+    return call(
+        prepare_kernel,
+        (bf16(docs, tb, 2 * width), bf16(width, docs * tb), bf16(width, width)),
+        [
+            pl.BlockSpec((1, tb, width), lambda i: (i, 0, 0)),
+            pl.BlockSpec(w_qkv.shape, lambda i: (0, 0), pipeline_mode=pl.Buffered(1)),
+        ],
+        (
+            pl.BlockSpec((1, tb, 2 * width), lambda i: (i, 0, 0)),
+            pl.BlockSpec((width, tb), lambda i: (0, i)),
+            pl.BlockSpec((width, width), lambda i: (0, 0)),
+        ),
+        flops=2 * docs * tb * width * 3 * width,
+        moved=11 * 2**20,
+        grid=(docs,),
+        name="prepare",
+    )(tokens, w_qkv)
+
+
+def row_ids(k, rows, shape, dim):
     place = lax.broadcasted_iota(jnp.int32, shape, dim)
-    y, z_lo = (me[0] + k) & 3, me[0] >> 2
+    dp, ctx = here()
+    y, z_lo = (dp + k) & 3, dp >> 2
     other = (place >= rows).astype(jnp.int32)
     owner = (z_lo + other - 2 * z_lo * other) * 4 + y
-    return (owner * 16 + me[1]) * rows + place - other * rows
-
-
-def target_kernel(docs, me, positive, *refs):
+    return (owner * 16 + ctx) * rows + place - other * rows
+
+
+def stack_kernel(*refs):
+    low = 0
+    for ref in refs[:-1]:
+        refs[-1][low : low + ref.shape[0], :] = ref[...]
+        low += ref.shape[0]
+
+
+def add_kernel(*refs):
+    terms = [ref[...] for ref in refs[:-1]]
+    if len(terms) == 4:
+        terms = [terms[0] + terms[2], terms[1] + terms[3]]
+    refs[-1][...] = terms[0] + terms[1]
+
+
+def add(terms):
+    return call(add_kernel, f32(*terms[0].shape), [VMEM] * len(terms), VMEM, limit=4, name="add")(*terms)
+
+
+def merge_kernel(docs, width, *refs):
+    refs[-1][...] = merge(docs, width, [ref[...] for ref in refs[:-1]])
+
+
+def merged(docs, width, states):
+    kernel = functools.partial(merge_kernel, docs, width)
+    return call(kernel, f32(*states[0].shape), [VMEM] * len(states), VMEM, limit=4, name="merge")(*states)
+
+
+def target_kernel(docs, positive, *refs):
     pieces, out = refs[:4], refs[4]
     total = jnp.zeros(out.shape, jnp.float32)
     for k, piece in enumerate(pieces):
         rows = piece.shape[0]
-        ids = row_ids(me, k, rows // 2, (8, rows), 1)
+        ids = row_ids(k, rows // 2, (8, rows), 1)
         doc = lax.broadcasted_iota(jnp.int32, (8, rows), 0)
         wanted = jnp.full((8, rows), -1, jnp.int32)
         for d in range(docs):
-            wanted = jnp.where(doc == d, positive[me[0] * docs + d], wanted)
+            wanted = jnp.where(doc == d, positive[lax.axis_index("dp") * docs + d], wanted)
         hit = (ids == wanted).astype(jnp.float32).astype(jnp.bfloat16)
         total = total + jnp.dot(hit, piece[...], preferred_element_type=jnp.float32)[0:docs]
     out[...] = total
 
 
-def turn_kernel(me, mixed, out):
+def turn_kernel(mixed, out):
     width = out.shape[0]
     place = lax.broadcasted_iota(jnp.int32, (width, 1), 0)
-    dp, ctx = me[0], me[1]
+    dp, ctx = here()
     each = width // 128
     core = (ctx & 1) ^ (place // (64 * each))
-    y = ((dp & 3) + place // (16 * each) % 4) & 3
-    x = ((ctx >> 2) + place // (4 * each) % 4) & 3
+    first, second = place // (16 * each) % 4, place // (4 * each) % 4
+    y = ((dp & 3) + jnp.where(core == 0, first, second)) & 3
+    x = ((ctx >> 2) + jnp.where(core == 0, second, first)) & 3
     z = ((ctx & 2) + (dp >> 2) + place // each % 4) & 3
     block = ((z & 1) * 4 + y) * 16 + x * 4 + (z >> 1) * 2 + core
     chosen = block * each + place % each == lax.broadcasted_iota(jnp.int32, (width, width), 1)
@@ -239,9 +320,10 @@
     return jnp.sum(jnp.where(same, column, 0.0), axis=0, keepdims=True)
 
 
-def score_kernel(docs, me, positive, e0, e1, e2, e3, t0, t1, t2, t3, everyone, state, expos):
+def score_kernel(docs, positive, e0, e1, e2, e3, t0, t1, t2, t3, everyone, state, expos):
     all_docs, width = everyone.shape
-    y, z_lo = me[0] & 3, me[0] >> 2
+    dp, _ = here()
+    y, z_lo = dp & 3, dp >> 2
     for k, piece in enumerate((e0, e1, e2, e3)):
         value = piece[...]
         turned = jnp.concatenate([value[docs:], value[0:docs]], axis=0)
@@ -253,13 +335,18 @@
     scores = [folded(lax.dot_general(emb, t[...], NT, preferred_element_type=jnp.float32)) / TAU for t in tables]
     tops = [jnp.max(s, axis=1, keepdims=True) for s in scores]
     top = jnp.maximum(jnp.maximum(tops[0], tops[2]), jnp.maximum(tops[1], tops[3]))
+    row = lax.broadcasted_iota(jnp.int32, (all_docs, 128), 0)
+    wanted = jnp.zeros((all_docs, 128), jnp.int32)
+    for doc in range(all_docs):
+        z, rest = divmod(doc, all_docs // 2)
+        wanted = jnp.where(row == rest // docs * 2 * docs + z * docs + rest % docs, positive[doc], wanted)
     totals, found = [], jnp.zeros((all_docs, 1), jnp.float32)
     for k, s in enumerate(scores):
         expo = jnp.exp(s - top)
         expos[:, k * rows : (k + 1) * rows] = expo
         halves = [jnp.sum(expo[:, h : h + rows // 2], axis=1, keepdims=True) for h in (0, rows // 2)]
         totals.append(halves[0] + halves[1])
-        hit = row_ids(me, k, rows // 2, (all_docs, rows), 1) == positive[...]
+        hit = row_ids(k, rows // 2, (all_docs, rows), 1) == wanted[:, 0:1]
         found = found + jnp.sum(jnp.where(hit, s, 0.0), axis=1, keepdims=True)
     total = (totals[0] + totals[2]) + (totals[1] + totals[3])
     place = pl.multiple_of(y * 2 * docs, 2 * docs)
@@ -296,7 +383,7 @@
     return jnp.where(row == docs + 1, top_lane, joined)
 
 
-def batch_kernel(docs, me, emb, everyone, product_out, stats):
+def batch_kernel(docs, emb, everyone, product_out, stats):
     everything = everyone[...]
     all_docs = everything.shape[0]
     own = lax.dot_general(emb[...], everything, NT, precision=HIGHEST, preferred_element_type=jnp.float32) / TAU
@@ -311,12 +398,13 @@
 
 
 def grad_kernel(
-    me, lengths, state, other, emb, rinv, everyone, target, product, stats, gain, normed, rstd, turned,
+    lengths, state, other, emb, rinv, everyone, target, product, stats, gain, normed, rstd, turned,
     keep_out, send_out, loss_out, d_summed,
 ):
     docs, width = target.shape
     all_docs = everyone.shape[0]
-    y, z_lo = me[0] & 3, me[0] >> 2
+    dp, _ = here()
+    y, z_lo = dp & 3, dp >> 2
     own, others = emb[0:docs], everyone[...]
     now = merge(docs, width, [state[...], other[...]])
     total, top, found = (now[docs + k : docs + k + 1, 0:all_docs] for k in range(3))
@@ -335,11 +423,11 @@
     d_pooled = (d_emb - own * jnp.sum(own * d_emb, axis=1, keepdims=True)) * rinv[0:docs, 0:1]
     tb = normed.shape[1]
     for doc in range(docs):
-        dy = d_pooled[doc : doc + 1] / lengths[doc].astype(jnp.float32) * gain[...]
+        dy = d_pooled[doc : doc + 1] / lengths[doc].astype(jnp.float32) * gain[...].reshape(1, width)
         level = dy - jnp.mean(dy, axis=1, keepdims=True)
         unit = normed[doc].astype(jnp.float32)
         along = jnp.mean(unit * dy, axis=1, keepdims=True)
-        keep = me[1] * tb + lax.broadcasted_iota(jnp.int32, (tb, 1), 0) < lengths[doc]
+        keep = lax.axis_index("ctx") * tb + lax.broadcasted_iota(jnp.int32, (tb, 1), 0) < lengths[doc]
         scale = jnp.where(keep, rstd[doc, :, 0:1], 0.0)
         d_summed[doc * tb : (doc + 1) * tb, :] = (scale * (level - unit * along)).astype(jnp.bfloat16)
     half = width // 2
@@ -369,23 +457,20 @@
 def shards(tokens, w_qkv, w_out, ln_gain, cache, positive, lengths):
     docs, tb, width = tokens.shape
     n_ctx, n_dp = lax.axis_size("ctx"), lax.axis_size("dp")
-    dp, ctx = lax.axis_index("dp"), lax.axis_index("ctx")
-    me = jnp.stack([dp, ctx]).astype(jnp.int32)
     all_docs = n_dp * docs
+    swapped = swap(cache, "dp", 4)
     halos = []
-    parts = [tokens[first : first + CHUNK] for first in range(0, docs, CHUNK)]
-    *parts, cache = lax.optimization_barrier((*parts, cache))
-    for part in parts:
+    for first in range(0, docs, CHUNK):
+        part = tokens[first : first + CHUNK]
         left = lax.ppermute(part, "ctx", [(i, (i + 1) % n_ctx) for i in range(n_ctx)])
         right = lax.ppermute(part, "ctx", [((i + 1) % n_ctx, i) for i in range(n_ctx)])
         halos.append((left, right))
-    tables = around(jnp.concatenate([cache, swap(cache, "dp", 4)], axis=0), from_y)
-    gain = ln_gain.reshape(1, width)
-    flat = tokens.reshape(docs * tb, width)
-    w_v_turned = w_qkv[:, 2 * width :].T
-    qk = jnp.dot(flat, w_qkv[:, : 2 * width], preferred_element_type=jnp.float32).astype(jnp.bfloat16)
-    v_turned = lax.dot_general(w_v_turned, flat, NT, preferred_element_type=jnp.float32).astype(jnp.bfloat16)
-    qk = qk.reshape(docs, tb, 2 * width)
+    gain = ln_gain
+    qk, v_turned, w_v_turned = prepare(in_hbm(tokens), in_hbm(w_qkv))
+    swapped, w_v_turned = lax.optimization_barrier((swapped, w_v_turned))
+    rows = cache.shape[0]
+    table = call(stack_kernel, bf16(2 * rows, width), [VMEM, VMEM], VMEM, limit=4, name="stack")(cache, swapped)
+    tables = around(table, from_y)
     done = None
     for index, (left, right) in enumerate(halos):
         if index == 1:
@@ -393,27 +478,28 @@
             pool, after = lax.optimization_barrier((pool, positive))
             done = [*done, pool]
             target = call(
-                functools.partial(target_kernel, docs), f32(docs, width), [SMEM, SMEM] + [VMEM] * 4, VMEM, name="target"
-            )(me, after, *tables)
+                functools.partial(target_kernel, docs), f32(docs, width), [SMEM] + [VMEM] * 4, VMEM, name="target"
+            )(after, *tables)
         done = attend(
-            index * CHUNK, done, me, lengths, tokens, left, right, qk, v_turned, w_qkv, w_v_turned, w_out, gain
+            index * CHUNK, done, lengths, tokens, left, right, qk, v_turned, w_qkv, w_v_turned, w_out, gain
         )
     hidden, mixed, normed, rstd, pool = done
 
     turned = call(
         turn_kernel,
         bf16(width, docs * tb),
-        [SMEM, VMEM],
+        [VMEM],
         VMEM,
         flops=2 * docs * tb * width * width,
         moved=4 * 2**20,
         name="turn",
-    )(me, mixed)
-
-    sums = jnp.concatenate([pool.reshape(docs, width), target], axis=0)
-    sums = sums + swap(sums, "ctx", 1)
-    terms = around(sums, from_x)
-    sums = (terms[0] + terms[2]) + (terms[1] + terms[3])
+    )(mixed)
+
+    sums = call(stack_kernel, f32(2 * docs, width), [VMEM, VMEM], VMEM, limit=4, name="stack")(
+        pool.reshape(docs, width), target
+    )
+    sums = add([sums, swap(sums, "ctx", 1)])
+    sums = add(around(sums, from_x))
     emb, rinv, target = call(
         norm_kernel,
         (f32(2 * docs, width), f32(2 * docs, 128), f32(docs, width)),
@@ -423,46 +509,45 @@
         name="norm",
     )(*around(sums, from_z))
     embs = around(emb, from_y)
-    wanted = positive.reshape(2, 4, docs).transpose(1, 0, 2).reshape(all_docs, 1)
     everyone, state = call(
         functools.partial(score_kernel, docs),
         (f32(all_docs, width), f32(2 * docs, width + 256)),
-        [SMEM] + [VMEM] * 9,
+        [SMEM] + [VMEM] * 8,
         (VMEM, VMEM),
         moved=2 * 2**20,
         scratch_shapes=[pltpu.VMEM((all_docs, n_dp * cache.shape[0]), jnp.float32)],
         name="score",
-    )(me, wanted, *embs, *tables)
+    )(positive, *embs, *tables)
     product, stats = call(
         functools.partial(batch_kernel, docs),
         (f32(2 * docs, all_docs), f32(8, all_docs)),
-        [SMEM, VMEM, VMEM],
+        [VMEM, VMEM],
         (VMEM, VMEM),
         limit=4,
         name="batch",
-    )(me, emb, everyone)
-    state = merge(docs, width, [state, swap(state, "ctx", 1)])
-    state = merge(docs, width, around(state, from_x))
+    )(emb, everyone)
+    state = merged(docs, width, [state, swap(state, "ctx", 1)])
+    state = merged(docs, width, around(state, from_x))
     half = width // 2
     keep, send, loss = call(
         grad_kernel,
         (f32(half, width), f32(half, width), f32(8, 128)),
-        [SMEM, SMEM] + [VMEM] * 12,
+        [SMEM] + [VMEM] * 12,
         (VMEM,) * 3,
         flops=2 * docs * tb * width * width,
         moved=8 * 2**20,
         scratch_shapes=[pltpu.VMEM((docs * tb, width), jnp.bfloat16)],
         name="grad",
     )(
-        me, lengths, state, swap(state, "ctx", 2), emb, rinv, everyone, target, product, stats, gain, normed, rstd, turned,
+        lengths, state, swap(state, "ctx", 2), emb, rinv, everyone, target, product, stats, gain, normed, rstd, turned,
     )
     keep, *sends = sum_and_split([keep, swap(send, "ctx", 1)], jnp.bfloat16)
-    got = [from_y(piece, -(k + 1)) for k, piece in enumerate(sends)]
+    got = [from_plane(piece, -(k + 1), False) for k, piece in enumerate(sends)]
     keep, *sends = sum_and_split([keep] + got, jnp.float32)
-    got = [from_x(piece, -(k + 1)) for k, piece in enumerate(sends)]
+    got = [from_plane(piece, -(k + 1), True) for k, piece in enumerate(sends)]
     keep, *sends = sum_and_split([keep] + got, jnp.float32)
     got = [from_z(piece, -(k + 1)) for k, piece in enumerate(sends)]
-    return (hidden, loss[0, 0], keep + got[0] + got[1] + got[2])
+    return (hidden, loss[0, 0], add([keep] + got))
 
 
 def solution(mesh):

time: 173 us -> 151 us (0.87)
  local copies, waits for them, and re-layouts: 23.4 us -> 2.05 us
  matrix products: 8.33 us -> 0 us
  Pallas kernels: 37.4 us -> 43.1 us
  waiting for transfers between devices: 38.6 us -> 42.9 us
    unnamed x54 -> x15, local copies, waits for them, and re-layouts: 19 us -> 0.03 us
    dot_general x2 -> x0, matrix products: 8.33 us -> none  [the longest x1 5.75 us: shards(): jnp.dot(flat, w_qkv[:, :2 * width], preferred_element_type=jnp.float32)]
    ppermute x0 -> x6, waiting for transfers between devices: none -> 8.19 us  [from_plane(): return lax.ppermute(value, ('dp', 'ctx'), pairs)]
    ppermute x0 -> x6, starting transfers between devices: none -> 7.97 us  [from_plane(): return lax.ppermute(value, ('dp', 'ctx'), pairs)]
    ppermute x9 -> x6, waiting for transfers between devices: 12.5 us -> 5.04 us  [from_y(): lax.ppermute(value, 'dp', [(d & 4 | d + k & 3, d) for d in range(lax.axis...]
    ppermute x5, waiting for transfers between devices: 10.8 us -> 17.2 us  [swap(): lax.ppermute(value, axis, [(i, i ^ bits) for i in range(lax.axis_size(axi...]
    pallas_call x4 -> x12, Pallas kernels: 31.4 us -> 37.8 us  [the longest x2 26.8 us: attend(): call(functools.partial(attend_kernel, first), out_shape, in_specs, (at(tb...]
    ppermute x9 -> x6, waiting for transfers between devices: 10.2 us -> 6.33 us  [from_x(): lax.ppermute(value, 'ctx', [((c + 4 * k) % size, c) for c in range(size)])]
  transfers between devices with their start and end apart: 33 -> 33, of which waited for: 20 -> 19; matrix products, arithmetic and copies ran while one was open for 8% -> 0% of each run, Pallas kernels for 18% -> 24%
where the time goes in v2:
time: 151 us
  starting transfers between devices  62 us (41%)
  Pallas kernels  43.1 us (29%)
  waiting for transfers between devices  42.9 us (28%)
  local copies, waits for them, and re-layouts  2.05 us (1%)
    pallas_call x2, Pallas kernels, attend(): call(functools.partial(attend_kernel, first), out_shape, in_specs, (at(tb...  26.8 us
    ppermute x5, waiting for transfers between devices, swap(): lax.ppermute(value, axis, [(i, i ^ bits) for i in range(lax.axis_size(axi...  17.2 us
    ppermute x5, starting transfers between devices, swap(): lax.ppermute(value, axis, [(i, i ^ bits) for i in range(lax.axis_size(axi...  15.9 us
    ppermute x2, starting transfers between devices, shards(): lax.ppermute(part, 'ctx', [((i + 1) % n_ctx, i) for i in range(n_ctx)])  11 us
    ppermute x6, starting transfers between devices, from_x(): lax.ppermute(value, 'ctx', [((c + 4 * k) % size, c) for c in range(size)])  10.2 us
    ppermute x6, starting transfers between devices, from_y(): lax.ppermute(value, 'dp', [(d & 4 | d + k & 3, d) for d in range(lax.axis...  8.65 us
    ppermute x6, waiting for transfers between devices, from_plane(): return lax.ppermute(value, ('dp', 'ctx'), pairs)  8.19 us
    ppermute x6, starting transfers between devices, from_z(): return lax.ppermute(value, ('dp', 'ctx'), pairs)  8.19 us
  transfers between devices with their start and end apart: 33, of which 19 were waited for; matrix products, arithmetic and copies ran while one was open for 0% of the time, Pallas kernels for 24%

profile of v2, /device:TPU:0, one launch (start us, length us, event | category | flops | bytes accessed | tf_op | source)
XLA Modules:
  0.0 151.0 jit_solution(1801084803943226084)
XLA Ops:
  0.6 1.5 %fusion = (bf16[2,256,768]{2,1,0:T(8,128)(2,1)S(1)}, bf16[2,256,768]{2,1,0:T(8,128)(2,1)S(1)}) fusion(bf16[4,256,768]{2,1,0:T(8,128)(2,1)} %tok.5), kind=kLoop, calls=%fused_computation.1 | loop fusion | bytes 3145728 | tf_op jit(solution)/shard_map/slice | solution.py:464
  2.2 5.7 %collective-permute-start.4 = (bf16[2,256,768]{2,1,0:T(8,128)(2,1)S(1)}, bf16[2,256,768]{2,1,0:T(8,128)(2,1)S(1)}, u32[]{:S(2)}, u32[]{:S(2)}) collective-permute-start(bf16[2,256,768]{2,1,0:T(8,128)(2,1)S(1)} %get-tuple-element.81), channel_id=1, source_target_pairs={{1,0},{2,1},{3,2},{4,3},{5,4},{6,5},{7,6},{8,7},{9,8},{10,9},{11,1... | collective-permute-start | bytes 2359304 | tf_op jit(solution)/shard_map/ppermute | solution.py:466
  7.9 5.4 %collective-permute-start.1 = (bf16[2,256,768]{2,1,0:T(8,128)(2,1)S(1)}, bf16[2,256,768]{2,1,0:T(8,128)(2,1)S(1)}, u32[]{:S(2)}, u32[]{:S(2)}) collective-permute-start(bf16[2,256,768]{2,1,0:T(8,128)(2,1)S(1)} %get-tuple-element.82), channel_id=1, source_target_pairs={{1,0},{2,1},{3,2},{4,3},{5,4},{6,5},{7,6},{8,7},{9,8},{10,9},{11,1... | collective-permute-start | bytes 2359304 | tf_op jit(solution)/shard_map/ppermute | solution.py:466
  13.3 1.7 %collective-permute-start.2 = (bf16[128,768]{1,0:T(8,128)(2,1)S(1)}, bf16[128,768]{1,0:T(8,128)(2,1)S(1)}, u32[]{:S(2)}, u32[]{:S(2)}) collective-permute-start(bf16[128,768]{1,0:T(8,128)(2,1)S(1)} %copy-done.3), channel_id=1, source_target_pairs={{0,64},{16,80},{32,96},{48,112},{64,0},{80,16},{96,32},{112,48},{1... | collective-permute-start | bytes 589832 | tf_op jit(solution)/shard_map/ppermute | solution.py:25
  15.0 7.2 %prepare.1 = (bf16[4,256,1536]{2,1,0:T(8,128)(2,1)S(1)}, bf16[768,1024]{1,0:T(8,128)(2,1)S(1)}, bf16[768,768]{1,0:T(8,128)(2,1)S(1)}) custom-call(bf16[4,256,768]{2,1,0:T(8,128)(2,1)} %tok.5, bf16[768,2304]{1,0:T(8,128)(2,1)} %w_k.3), custom_call_target="tpu_custom_call" | custom-call | flops 3623878656 | bytes 11534336 | tf_op jit(solution)/shard_map/prepare/pallas_call | solution.py:221
  22.1 9.9 %collective-permute-done.2.refs_1_ = bf16[128,768]{1,0:T(8,128)(2,1)S(1)} collective-permute-done((bf16[128,768]{1,0:T(8,128)(2,1)S(1)}, bf16[128,768]{1,0:T(8,128)(2,1)S(1)}, u32[]{:S(2)}, u32[]{:S(2)}) %collective-permute-start.2) | collective-permute-done | bytes 196640 | tf_op jit(solution)/shard_map/ppermute | solution.py:25
  32.1 3.1 %collective-permute-start.5 = (bf16[256,768]{1,0:T(8,128)(2,1)S(1)}, bf16[256,768]{1,0:T(8,128)(2,1)S(1)}, u32[]{:S(2)}, u32[]{:S(2)}) collective-permute-start(bf16[256,768]{1,0:T(8,128)(2,1)S(1)} %stack.2.refs_0_.t0), channel_id=1, source_target_pairs={{16,0},{32,16},{48,32},{0,48},{80,64},{96,80},{112,96},{64,112},{1... | collective-permute-start | bytes 1179656 | tf_op jit(solution)/shard_map/ppermute | solution.py:34
  35.8 1.0 collective-permute-start.7
  36.8 13.4 %attend.2 = (bf16[4,256,768]{2,1,0:T(8,128)(2,1)}, bf16[768,1024]{1,0:T(8,128)(2,1)S(1)}, bf16[4,256,768]{2,1,0:T(8,128)(2,1)S(1)}, f32[4,256,128]{2,1,0:T(8,128)S(1)}, f32[4,1,768]{2,1,0:T(1,128)S(1)}) custom-call(s32[4]{0:T(128)S(1)} %copy-done.5, bf16[4,256,768]{2,1,0:T(8,128)(2,1)S(1)} %copy-done, bf16[2,256,768]{2,1,0:T(8,128)(2,1)S(1)} %collective-permute-done.3.left, ...), custom_call_target="tpu_custom_call" | custom-call | flops 3019898880 | bytes 8388608 | tf_op jit(solution)/shard_map/attend/pallas_call | solution.py:188
  50.2 13.4 %attend.3 = (bf16[4,256,768]{2,1,0:T(8,128)(2,1)}, bf16[768,1024]{1,0:T(8,128)(2,1)S(1)}, bf16[4,256,768]{2,1,0:T(8,128)(2,1)S(1)}, f32[4,256,128]{2,1,0:T(8,128)S(1)}, f32[4,1,768]{2,1,0:T(1,128)S(1)}) custom-call(s32[4]{0:T(128)S(1)} %copy-done.5, ...), custom_call_target="tpu_custom_call", output_to_operand_aliasing={{0}: (10, {}), {1}: (11, {}), {2}: (12, {}), {3}: (13, {}),... | custom-call | flops 3019898880 | bytes 8388608 | tf_op jit(solution)/shard_map/attend/pallas_call | solution.py:188
  63.7 0.9 target.1.refs_1_
  64.5 13.4 %collective-permute-start.8 = (f32[8,768]{1,0:T(8,128)S(1)}, f32[8,768]{1,0:T(8,128)S(1)}, u32[]{:S(2)}, u32[]{:S(2)}) collective-permute-start(f32[8,768]{1,0:T(8,128)S(1)} %stack.3.refs_0_), channel_id=1, source_target_pairs={{0,1},{1,0},{2,3},{3,2},{4,5},{5,4},{6,7},{7,6},{8,9},{9,8},{10,11... | collective-permute-start | bytes 73736 | tf_op jit(solution)/shard_map/ppermute | solution.py:25
  77.9 0.8 collective-permute-done.8.refs_1_
  78.8 2.8 %collective-permute-start.10 = (f32[8,768]{1,0:T(8,128)S(1)}, f32[8,768]{1,0:T(8,128)S(1)}, u32[]{:S(2)}, u32[]{:S(2)}) collective-permute-start(f32[8,768]{1,0:T(8,128)S(1)} %add.3.refs_0_), channel_id=1, source_target_pairs={{8,0},{9,1},{10,2},{11,3},{12,4},{13,5},{14,6},{15,7},{0,8},{1,9},... | collective-permute-start | bytes 73736 | tf_op jit(solution)/shard_map/ppermute | solution.py:30
  81.5 0.9 collective-permute-start.11
  82.4 2.4 %collective-permute-start.9 = (f32[8,768]{1,0:T(8,128)S(1)}, f32[8,768]{1,0:T(8,128)S(1)}, u32[]{:S(2)}, u32[]{:S(2)}) collective-permute-start(f32[8,768]{1,0:T(8,128)S(1)} %add.3.refs_0_), channel_id=1, source_target_pairs={{4,0},{5,1},{6,2},{7,3},{8,4},{9,5},{10,6},{11,7},{12,8},{13,9},{1... | collective-permute-start | bytes 73736 | tf_op jit(solution)/shard_map/ppermute | solution.py:30
  84.8 1.8 %collective-permute-done.11.refs_3_ = f32[8,768]{1,0:T(8,128)S(1)} collective-permute-done((f32[8,768]{1,0:T(8,128)S(1)}, f32[8,768]{1,0:T(8,128)S(1)}, u32[]{:S(2)}, u32[]{:S(2)}) %collective-permute-start.11) | collective-permute-done | bytes 24608 | tf_op jit(solution)/shard_map/ppermute | solution.py:30
  86.6 1.5 %collective-permute-start.12 = (f32[8,768]{1,0:T(8,128)S(1)}, f32[8,768]{1,0:T(8,128)S(1)}, u32[]{:S(2)}, u32[]{:S(2)}) collective-permute-start(f32[8,768]{1,0:T(8,128)S(1)} %add.4.s0), channel_id=1, source_target_pairs={{64,0},{65,1},{66,2},{67,3},{68,4},{69,5},{70,6},{71,7},{72,8},{73... | collective-permute-start | bytes 73736 | tf_op jit(solution)/shard_map/ppermute | solution.py:44
  88.1 2.0 %collective-permute-start.13 = (f32[8,768]{1,0:T(8,128)S(1)}, f32[8,768]{1,0:T(8,128)S(1)}, u32[]{:S(2)}, u32[]{:S(2)}) collective-permute-start(f32[8,768]{1,0:T(8,128)S(1)} %add.4.s0), channel_id=1, source_target_pairs={{2,0},{3,1},{0,2},{1,3},{6,4},{7,5},{4,6},{5,7},{10,8},{11,9},{8,1... | collective-permute-start | bytes 73736 | tf_op jit(solution)/shard_map/ppermute | solution.py:44
  90.1 1.3 collective-permute-start.14
  91.5 2.0 %collective-permute-done.13.s2 = f32[8,768]{1,0:T(8,128)S(1)} collective-permute-done((f32[8,768]{1,0:T(8,128)S(1)}, f32[8,768]{1,0:T(8,128)S(1)}, u32[]{:S(2)}, u32[]{:S(2)}) %collective-permute-start.13) | collective-permute-done | bytes 24608 | tf_op jit(solution)/shard_map/ppermute | solution.py:44
  93.4 1.7 %collective-permute-done.14.s3 = f32[8,768]{1,0:T(8,128)S(1)} collective-permute-done((f32[8,768]{1,0:T(8,128)S(1)}, f32[8,768]{1,0:T(8,128)S(1)}, u32[]{:S(2)}, u32[]{:S(2)}) %collective-permute-start.14) | collective-permute-done | bytes 24608 | tf_op jit(solution)/shard_map/ppermute | solution.py:44
  95.3 2.3 %collective-permute-start.15 = (f32[8,768]{1,0:T(8,128)S(1)}, f32[8,768]{1,0:T(8,128)S(1)}, u32[]{:S(2)}, u32[]{:S(2)}) collective-permute-start(f32[8,768]{1,0:T(8,128)S(1)} %get-tuple-element.56.e0.emb), channel_id=1, source_target_pairs={{16,0},{32,16},{48,32},{0,48},{80,64},{96,80},{112,96},{64,112},{1... | collective-permute-start | bytes 73736 | tf_op jit(solution)/shard_map/ppermute | solution.py:34
  97.5 1.7 %collective-permute-start.16 = (f32[8,768]{1,0:T(8,128)S(1)}, f32[8,768]{1,0:T(8,128)S(1)}, u32[]{:S(2)}, u32[]{:S(2)}) collective-permute-start(f32[8,768]{1,0:T(8,128)S(1)} %get-tuple-element.56.e0.emb), channel_id=1, source_target_pairs={{32,0},{48,16},{0,32},{16,48},{96,64},{112,80},{64,96},{80,112},{3... | collective-permute-start | bytes 73736 | tf_op jit(solution)/shard_map/ppermute | solution.py:34
  99.2 3.6 %collective-permute-done.16.e2 = f32[8,768]{1,0:T(8,128)S(1)} collective-permute-done((f32[8,768]{1,0:T(8,128)S(1)}, f32[8,768]{1,0:T(8,128)S(1)}, u32[]{:S(2)}, u32[]{:S(2)}) %collective-permute-start.16) | collective-permute-done | bytes 24608 | tf_op jit(solution)/shard_map/ppermute | solution.py:34
  102.9 1.4 collective-permute-done.17.e3
  104.3 1.7 %score.1 = (f32[32,768]{1,0:T(8,128)S(1)}, f32[8,1024]{1,0:T(8,128)S(1)}) custom-call(s32[32]{0:T(128)S(1)} %copy-done.6, f32[8,768]{1,0:T(8,128)S(1)} %get-tuple-element.56.e0.emb, f32[8,768]{1,0:T(8,128)S(1)} %collective-permute-done.15.e1, f32[8,768]{1,0:T(8,128)S(1)} %collective-permute-done.16.e2, f32[8,768]{1,0:T(8,128)S(1)} %collective-permute-done.17.e3, ...), custom_call_target="tpu_custom_call" | custom-call | bytes 2097152 | tf_op jit(solution)/shard_map/score/pallas_call | solution.py:512
  106.1 1.2 collective-permute-done.18.refs_1_
  107.4 3.3 %collective-permute-start.19 = (f32[8,1024]{1,0:T(8,128)S(1)}, f32[8,1024]{1,0:T(8,128)S(1)}, u32[]{:S(2)}, u32[]{:S(2)}) collective-permute-start(f32[8,1024]{1,0:T(8,128)S(1)} %merge.2.refs_0_), channel_id=1, source_target_pairs={{4,0},{5,1},{6,2},{7,3},{8,4},{9,5},{10,6},{11,7},{12,8},{13,9},{1... | collective-permute-start | bytes 98312 | tf_op jit(solution)/shard_map/ppermute | solution.py:30
  110.7 0.9 collective-permute-start.21
  111.6 0.6 collective-permute-done.19.refs_1_
  112.3 3.9 %collective-permute-done.20.refs_2_ = f32[8,1024]{1,0:T(8,128)S(1)} collective-permute-done((f32[8,1024]{1,0:T(8,128)S(1)}, f32[8,1024]{1,0:T(8,128)S(1)}, u32[]{:S(2)}, u32[]{:S(2)}) %collective-permute-start.20) | collective-permute-done | bytes 32800 | tf_op jit(solution)/shard_map/ppermute | solution.py:30
  116.9 2.1 %turn.1.turned = bf16[768,1024]{1,0:T(8,128)(2,1)S(1)} custom-call(bf16[768,1024]{1,0:T(8,128)(2,1)S(1)} %get-tuple-element.65.mixed), custom_call_target="tpu_custom_call" | custom-call | flops 1207959552 | bytes 4194304 | tf_op jit(solution)/shard_map/turn/pallas_call | solution.py:488
  119.3 2.4 %collective-permute-done.22.other = f32[8,1024]{1,0:T(8,128)S(1)} collective-permute-done((f32[8,1024]{1,0:T(8,128)S(1)}, f32[8,1024]{1,0:T(8,128)S(1)}, u32[]{:S(2)}, u32[]{:S(2)}) %collective-permute-start.22) | collective-permute-done | bytes 32800 | tf_op jit(solution)/shard_map/ppermute | solution.py:25
  121.8 2.9 %grad.1 = (f32[384,768]{1,0:T(8,128)S(1)}, f32[384,768]{1,0:T(8,128)S(1)}, f32[8,128]{1,0:T(8,128)S(1)}) custom-call(s32[4]{0:T(128)S(1)} %copy-done.5, f32[8,1024]{1,0:T(8,128)S(1)} %merge.3.state, f32[8,1024]{1,0:T(8,128)S(1)} %collective-permute-done.22.other, f32[8,768]{1,0:T(8,128)S(1)} %get-tuple-element.56.e0.emb, ...), custom_call_target="tpu_custom_call" | custom-call | flops 1207959552 | bytes 8388608 | tf_op jit(solution)/shard_map/grad/pallas_call | solution.py:532
  124.8 2.8 %collective-permute-done.23.refs_1_ = f32[384,768]{1,0:T(8,128)S(1)} collective-permute-done((f32[384,768]{1,0:T(8,128)S(1)}, f32[384,768]{1,0:T(8,128)S(1)}, u32[]{:S(2)}, u32[]{:S(2)}) %collective-permute-start.23) | collective-permute-done | bytes 1179680 | tf_op jit(solution)/shard_map/ppermute | solution.py:25
  127.9 1.2 collective-permute-start.25
  129.1 2.1 %collective-permute-start.26 = (bf16[96,768]{1,0:T(8,128)(2,1)S(1)}, bf16[96,768]{1,0:T(8,128)(2,1)S(1)}, u32[]{:S(2)}, u32[]{:S(2)}) collective-permute-start(bf16[96,768]{1,0:T(8,128)(2,1)S(1)} %get-tuple-element.72), channel_id=1, source_target_pairs={{16,0},{5,1},{18,2},{7,3},{20,4},{9,5},{22,6},{11,7},{24,8},{13,9}... | collective-permute-start | bytes 442376 | tf_op jit(solution)/shard_map/ppermute | solution.py:55
  131.2 4.7 %collective-permute-done.24.refs_1_ = bf16[96,768]{1,0:T(8,128)(2,1)S(1)} collective-permute-done((bf16[96,768]{1,0:T(8,128)(2,1)S(1)}, bf16[96,768]{1,0:T(8,128)(2,1)S(1)}, u32[]{:S(2)}, u32[]{:S(2)}) %collective-permute-start.24) | collective-permute-done | bytes 147488 | tf_op jit(solution)/shard_map/ppermute | solution.py:55
  135.8 0.9 collective-permute-done.26.refs_3_
  136.9 2.3 %collective-permute-start.28 = (f32[24,768]{1,0:T(8,128)S(1)}, f32[24,768]{1,0:T(8,128)S(1)}, u32[]{:S(2)}, u32[]{:S(2)}) collective-permute-start(f32[24,768]{1,0:T(8,128)S(1)} %get-tuple-element.75), channel_id=1, source_target_pairs={{8,0},{33,1},{10,2},{35,3},{12,4},{37,5},{14,6},{39,7},{0,8},{41,9... | collective-permute-start | bytes 221192 | tf_op jit(solution)/shard_map/ppermute | solution.py:55
  139.2 2.3 %collective-permute-start.29 = (f32[24,768]{1,0:T(8,128)S(1)}, f32[24,768]{1,0:T(8,128)S(1)}, u32[]{:S(2)}, u32[]{:S(2)}) collective-permute-start(f32[24,768]{1,0:T(8,128)S(1)} %get-tuple-element.76), channel_id=1, source_target_pairs={{4,0},{17,1},{6,2},{19,3},{8,4},{21,5},{10,6},{23,7},{12,8},{25,9}... | collective-permute-start | bytes 221192 | tf_op jit(solution)/shard_map/ppermute | solution.py:55
  141.5 1.8 %collective-permute-done.27.refs_1_ = f32[24,768]{1,0:T(8,128)S(1)} collective-permute-done((f32[24,768]{1,0:T(8,128)S(1)}, f32[24,768]{1,0:T(8,128)S(1)}, u32[]{:S(2)}, u32[]{:S(2)}) %collective-permute-start.27) | collective-permute-done | bytes 73760 | tf_op jit(solution)/shard_map/ppermute | solution.py:55
  143.2 0.9 collective-permute-done.29.refs_3_
  144.3 2.1 %collective-permute-start.31 = (f32[6,768]{1,0:T(8,128)S(1)}, f32[6,768]{1,0:T(8,128)S(1)}, u32[]{:S(2)}, u32[]{:S(2)}) collective-permute-start(f32[6,768]{1,0:T(8,128)S(1)} %get-tuple-element.79), channel_id=1, source_target_pairs={{2,0},{3,1},{0,2},{1,3},{6,4},{7,5},{4,6},{5,7},{10,8},{11,9},{8,1... | collective-permute-start | bytes 55304 | tf_op jit(solution)/shard_map/ppermute | solution.py:44
  146.4 1.0 collective-permute-start.32
  147.9 1.3 collective-permute-done.30.refs_1_
  149.6 0.7 collective-permute-done.32.refs_3_
  (54 shorter events, 4.4 us)
Async XLA Ops:
  0.6 12.6 %copy-start.3 = (bf16[128,768]{1,0:T(8,128)(2,1)S(1)}, bf16[128,768]{1,0:T(8,128)(2,1)}, u32[]{:S(2)}) copy-start(bf16[128,768]{1,0:T(8,128)(2,1)} %refs_0_.1) | copy-start | bytes 589828
  2.2 33.0 %collective-permute-start.3 = (bf16[2,256,768]{2,1,0:T(8,128)(2,1)S(1)}, bf16[2,256,768]{2,1,0:T(8,128)(2,1)S(1)}, u32[]{:S(2)}, u32[]{:S(2)}) collective-permute-start(bf16[2,256,768]{2,1,0:T(8,128)(2,1)S(1)} %get-tuple-element.81), channel_id=1, source_target_pairs={{0,1},{1,2},{2,3},{3,4},{4,5},{5,6},{6,7},{7,8},{8,9},{9,10},{10,1... | collective-permute-start | bytes 2359304 | tf_op jit(solution)/shard_map/ppermute | solution.py:465
  2.2 33.6 %collective-permute-start.4 = (bf16[2,256,768]{2,1,0:T(8,128)(2,1)S(1)}, bf16[2,256,768]{2,1,0:T(8,128)(2,1)S(1)}, u32[]{:S(2)}, u32[]{:S(2)}) collective-permute-start(bf16[2,256,768]{2,1,0:T(8,128)(2,1)S(1)} %get-tuple-element.81), channel_id=1, source_target_pairs={{1,0},{2,1},{3,2},{4,3},{5,4},{6,5},{7,6},{8,7},{9,8},{10,9},{11,1... | collective-permute-start | bytes 2359304 | tf_op jit(solution)/shard_map/ppermute | solution.py:466
  7.9 28.9 %copy-start.4 = (f32[768]{0:T(1024)S(1)}, f32[768]{0:T(1024)}, u32[]{:S(2)}) copy-start(f32[768]{0:T(1024)} %gain.5) | copy-start | bytes 9220
  7.9 28.9 %copy-start.5 = (s32[4]{0:T(128)S(1)}, s32[4]{0:T(128)}, u32[]{:S(2)}) copy-start(s32[4]{0:T(128)} %lengths.5) | copy-start | bytes 52
  7.9 42.3 %collective-permute-start = (bf16[2,256,768]{2,1,0:T(8,128)(2,1)S(1)}, bf16[2,256,768]{2,1,0:T(8,128)(2,1)S(1)}, u32[]{:S(2)}, u32[]{:S(2)}) collective-permute-start(bf16[2,256,768]{2,1,0:T(8,128)(2,1)S(1)} %get-tuple-element.82), channel_id=1, source_target_pairs={{0,1},{1,2},{2,3},{3,4},{4,5},{5,6},{6,7},{7,8},{8,9},{9,10},{10,1... | collective-permute-start | bytes 2359304 | tf_op jit(solution)/shard_map/ppermute | solution.py:465
  7.9 42.3 %collective-permute-start.1 = (bf16[2,256,768]{2,1,0:T(8,128)(2,1)S(1)}, bf16[2,256,768]{2,1,0:T(8,128)(2,1)S(1)}, u32[]{:S(2)}, u32[]{:S(2)}) collective-permute-start(bf16[2,256,768]{2,1,0:T(8,128)(2,1)S(1)} %get-tuple-element.82), channel_id=1, source_target_pairs={{1,0},{2,1},{3,2},{4,3},{5,4},{6,5},{7,6},{8,7},{9,8},{10,9},{11,1... | collective-permute-start | bytes 2359304 | tf_op jit(solution)/shard_map/ppermute | solution.py:466
  13.3 18.8 %collective-permute-start.2 = (bf16[128,768]{1,0:T(8,128)(2,1)S(1)}, bf16[128,768]{1,0:T(8,128)(2,1)S(1)}, u32[]{:S(2)}, u32[]{:S(2)}) collective-permute-start(bf16[128,768]{1,0:T(8,128)(2,1)S(1)} %copy-done.3), channel_id=1, source_target_pairs={{0,64},{16,80},{32,96},{48,112},{64,0},{80,16},{96,32},{112,48},{1... | collective-permute-start | bytes 589832 | tf_op jit(solution)/shard_map/ppermute | solution.py:25
  15.0 21.8 %copy-start = (bf16[4,256,768]{2,1,0:T(8,128)(2,1)S(1)}, bf16[4,256,768]{2,1,0:T(8,128)(2,1)}, u32[]{:S(2)}) copy-start(bf16[4,256,768]{2,1,0:T(8,128)(2,1)} %tok.5) | copy-start | bytes 4718596
  15.0 21.8 %copy-start.1 = (bf16[768,2304]{1,0:T(8,128)(2,1)S(1)}, bf16[768,2304]{1,0:T(8,128)(2,1)}, u32[]{:S(2)}) copy-start(bf16[768,2304]{1,0:T(8,128)(2,1)} %w_k.3) | copy-start | bytes 10616836
  15.0 21.8 %copy-start.2 = (bf16[768,768]{1,0:T(8,128)(2,1)S(1)}, bf16[768,768]{1,0:T(8,128)(2,1)}, u32[]{:S(2)}) copy-start(bf16[768,768]{1,0:T(8,128)(2,1)} %w_out.3) | copy-start | bytes 3538948
  32.1 31.5 %collective-permute-start.5 = (bf16[256,768]{1,0:T(8,128)(2,1)S(1)}, bf16[256,768]{1,0:T(8,128)(2,1)S(1)}, u32[]{:S(2)}, u32[]{:S(2)}) collective-permute-start(bf16[256,768]{1,0:T(8,128)(2,1)S(1)} %stack.2.refs_0_.t0), channel_id=1, source_target_pairs={{16,0},{32,16},{48,32},{0,48},{80,64},{96,80},{112,96},{64,112},{1... | collective-permute-start | bytes 1179656 | tf_op jit(solution)/shard_map/ppermute | solution.py:34
  35.2 28.4 %collective-permute-start.6 = (bf16[256,768]{1,0:T(8,128)(2,1)S(1)}, bf16[256,768]{1,0:T(8,128)(2,1)S(1)}, u32[]{:S(2)}, u32[]{:S(2)}) collective-permute-start(bf16[256,768]{1,0:T(8,128)(2,1)S(1)} %stack.2.refs_0_.t0), channel_id=1, source_target_pairs={{32,0},{48,16},{0,32},{16,48},{96,64},{112,80},{64,96},{80,112},{3... | collective-permute-start | bytes 1179656 | tf_op jit(solution)/shard_map/ppermute | solution.py:34
  35.8 27.8 %collective-permute-start.7 = (bf16[256,768]{1,0:T(8,128)(2,1)S(1)}, bf16[256,768]{1,0:T(8,128)(2,1)S(1)}, u32[]{:S(2)}, u32[]{:S(2)}) collective-permute-start(bf16[256,768]{1,0:T(8,128)(2,1)S(1)} %stack.2.refs_0_.t0), channel_id=1, source_target_pairs={{48,0},{0,16},{16,32},{32,48},{112,64},{64,80},{80,96},{96,112},{4... | collective-permute-start | bytes 1179656 | tf_op jit(solution)/shard_map/ppermute | solution.py:34
  50.2 13.4 %copy-start.6 = (s32[32]{0:T(128)S(1)}, s32[32]{0:T(128)}, u32[]{:S(2)}) copy-start(s32[32]{0:T(128)} %positive.2) | copy-start | bytes 388
  64.5 14.2 %collective-permute-start.8 = (f32[8,768]{1,0:T(8,128)S(1)}, f32[8,768]{1,0:T(8,128)S(1)}, u32[]{:S(2)}, u32[]{:S(2)}) collective-permute-start(f32[8,768]{1,0:T(8,128)S(1)} %stack.3.refs_0_), channel_id=1, source_target_pairs={{0,1},{1,0},{2,3},{3,2},{4,5},{5,4},{6,7},{7,6},{8,9},{9,8},{10,11... | collective-permute-start | bytes 73736 | tf_op jit(solution)/shard_map/ppermute | solution.py:25
  78.8 6.0 %collective-permute-start.10 = (f32[8,768]{1,0:T(8,128)S(1)}, f32[8,768]{1,0:T(8,128)S(1)}, u32[]{:S(2)}, u32[]{:S(2)}) collective-permute-start(f32[8,768]{1,0:T(8,128)S(1)} %add.3.refs_0_), channel_id=1, source_target_pairs={{8,0},{9,1},{10,2},{11,3},{12,4},{13,5},{14,6},{15,7},{0,8},{1,9},... | collective-permute-start | bytes 73736 | tf_op jit(solution)/shard_map/ppermute | solution.py:30
  81.5 5.0 %collective-permute-start.11 = (f32[8,768]{1,0:T(8,128)S(1)}, f32[8,768]{1,0:T(8,128)S(1)}, u32[]{:S(2)}, u32[]{:S(2)}) collective-permute-start(f32[8,768]{1,0:T(8,128)S(1)} %add.3.refs_0_), channel_id=1, source_target_pairs={{12,0},{13,1},{14,2},{15,3},{0,4},{1,5},{2,6},{3,7},{4,8},{5,9},{6... | collective-permute-start | bytes 73736 | tf_op jit(solution)/shard_map/ppermute | solution.py:30
  82.4 4.2 %collective-permute-start.9 = (f32[8,768]{1,0:T(8,128)S(1)}, f32[8,768]{1,0:T(8,128)S(1)}, u32[]{:S(2)}, u32[]{:S(2)}) collective-permute-start(f32[8,768]{1,0:T(8,128)S(1)} %add.3.refs_0_), channel_id=1, source_target_pairs={{4,0},{5,1},{6,2},{7,3},{8,4},{9,5},{10,6},{11,7},{12,8},{13,9},{1... | collective-permute-start | bytes 73736 | tf_op jit(solution)/shard_map/ppermute | solution.py:30
  86.6 4.9 %collective-permute-start.12 = (f32[8,768]{1,0:T(8,128)S(1)}, f32[8,768]{1,0:T(8,128)S(1)}, u32[]{:S(2)}, u32[]{:S(2)}) collective-permute-start(f32[8,768]{1,0:T(8,128)S(1)} %add.4.s0), channel_id=1, source_target_pairs={{64,0},{65,1},{66,2},{67,3},{68,4},{69,5},{70,6},{71,7},{72,8},{73... | collective-permute-start | bytes 73736 | tf_op jit(solution)/shard_map/ppermute | solution.py:44
  88.1 5.3 %collective-permute-start.13 = (f32[8,768]{1,0:T(8,128)S(1)}, f32[8,768]{1,0:T(8,128)S(1)}, u32[]{:S(2)}, u32[]{:S(2)}) collective-permute-start(f32[8,768]{1,0:T(8,128)S(1)} %add.4.s0), channel_id=1, source_target_pairs={{2,0},{3,1},{0,2},{1,3},{6,4},{7,5},{4,6},{5,7},{10,8},{11,9},{8,1... | collective-permute-start | bytes 73736 | tf_op jit(solution)/shard_map/ppermute | solution.py:44
  90.1 5.0 %collective-permute-start.14 = (f32[8,768]{1,0:T(8,128)S(1)}, f32[8,768]{1,0:T(8,128)S(1)}, u32[]{:S(2)}, u32[]{:S(2)}) collective-permute-start(f32[8,768]{1,0:T(8,128)S(1)} %add.4.s0), channel_id=1, source_target_pairs={{66,0},{67,1},{64,2},{65,3},{70,4},{71,5},{68,6},{69,7},{74,8},{75... | collective-permute-start | bytes 73736 | tf_op jit(solution)/shard_map/ppermute | solution.py:44
  95.3 4.0 %collective-permute-start.15 = (f32[8,768]{1,0:T(8,128)S(1)}, f32[8,768]{1,0:T(8,128)S(1)}, u32[]{:S(2)}, u32[]{:S(2)}) collective-permute-start(f32[8,768]{1,0:T(8,128)S(1)} %get-tuple-element.56.e0.emb), channel_id=1, source_target_pairs={{16,0},{32,16},{48,32},{0,48},{80,64},{96,80},{112,96},{64,112},{1... | collective-permute-start | bytes 73736 | tf_op jit(solution)/shard_map/ppermute | solution.py:34
  97.5 5.3 %collective-permute-start.16 = (f32[8,768]{1,0:T(8,128)S(1)}, f32[8,768]{1,0:T(8,128)S(1)}, u32[]{:S(2)}, u32[]{:S(2)}) collective-permute-start(f32[8,768]{1,0:T(8,128)S(1)} %get-tuple-element.56.e0.emb), channel_id=1, source_target_pairs={{32,0},{48,16},{0,32},{16,48},{96,64},{112,80},{64,96},{80,112},{3... | collective-permute-start | bytes 73736 | tf_op jit(solution)/shard_map/ppermute | solution.py:34
  99.2 5.0 %collective-permute-start.17 = (f32[8,768]{1,0:T(8,128)S(1)}, f32[8,768]{1,0:T(8,128)S(1)}, u32[]{:S(2)}, u32[]{:S(2)}) collective-permute-start(f32[8,768]{1,0:T(8,128)S(1)} %get-tuple-element.56.e0.emb), channel_id=1, source_target_pairs={{48,0},{0,16},{16,32},{32,48},{112,64},{64,80},{80,96},{96,112},{4... | collective-permute-start | bytes 73736 | tf_op jit(solution)/shard_map/ppermute | solution.py:34
  106.0 1.3 collective-permute-start.18
  107.4 4.9 %collective-permute-start.19 = (f32[8,1024]{1,0:T(8,128)S(1)}, f32[8,1024]{1,0:T(8,128)S(1)}, u32[]{:S(2)}, u32[]{:S(2)}) collective-permute-start(f32[8,1024]{1,0:T(8,128)S(1)} %merge.2.refs_0_), channel_id=1, source_target_pairs={{4,0},{5,1},{6,2},{7,3},{8,4},{9,5},{10,6},{11,7},{12,8},{13,9},{1... | collective-permute-start | bytes 98312 | tf_op jit(solution)/shard_map/ppermute | solution.py:30
  110.7 5.5 %collective-permute-start.20 = (f32[8,1024]{1,0:T(8,128)S(1)}, f32[8,1024]{1,0:T(8,128)S(1)}, u32[]{:S(2)}, u32[]{:S(2)}) collective-permute-start(f32[8,1024]{1,0:T(8,128)S(1)} %merge.2.refs_0_), channel_id=1, source_target_pairs={{8,0},{9,1},{10,2},{11,3},{12,4},{13,5},{14,6},{15,7},{0,8},{1,9},... | collective-permute-start | bytes 98312 | tf_op jit(solution)/shard_map/ppermute | solution.py:30
  110.7 5.5 %collective-permute-start.21 = (f32[8,1024]{1,0:T(8,128)S(1)}, f32[8,1024]{1,0:T(8,128)S(1)}, u32[]{:S(2)}, u32[]{:S(2)}) collective-permute-start(f32[8,1024]{1,0:T(8,128)S(1)} %merge.2.refs_0_), channel_id=1, source_target_pairs={{12,0},{13,1},{14,2},{15,3},{0,4},{1,5},{2,6},{3,7},{4,8},{5,9},{6... | collective-permute-start | bytes 98312 | tf_op jit(solution)/shard_map/ppermute | solution.py:30
  116.3 5.5 %collective-permute-start.22 = (f32[8,1024]{1,0:T(8,128)S(1)}, f32[8,1024]{1,0:T(8,128)S(1)}, u32[]{:S(2)}, u32[]{:S(2)}) collective-permute-start(f32[8,1024]{1,0:T(8,128)S(1)} %merge.3.state), channel_id=1, source_target_pairs={{0,2},{1,3},{2,0},{3,1},{4,6},{5,7},{6,4},{7,5},{8,10},{9,11},{10,... | collective-permute-start | bytes 98312 | tf_op jit(solution)/shard_map/ppermute | solution.py:25
  124.7 2.9 %collective-permute-start.23 = (f32[384,768]{1,0:T(8,128)S(1)}, f32[384,768]{1,0:T(8,128)S(1)}, u32[]{:S(2)}, u32[]{:S(2)}) collective-permute-start(f32[384,768]{1,0:T(8,128)S(1)} %get-tuple-element.68), channel_id=1, source_target_pairs={{0,1},{1,0},{2,3},{3,2},{4,5},{5,4},{6,7},{7,6},{8,9},{9,8},{10,11... | collective-permute-start | bytes 3538952 | tf_op jit(solution)/shard_map/ppermute | solution.py:25
  127.8 8.0 %collective-permute-start.24 = (bf16[96,768]{1,0:T(8,128)(2,1)S(1)}, bf16[96,768]{1,0:T(8,128)(2,1)S(1)}, u32[]{:S(2)}, u32[]{:S(2)}) collective-permute-start(bf16[96,768]{1,0:T(8,128)(2,1)S(1)} %get-tuple-element.70), channel_id=1, source_target_pairs={{48,0},{13,1},{50,2},{15,3},{52,4},{1,5},{54,6},{3,7},{56,8},{5,9}... | collective-permute-start | bytes 442376 | tf_op jit(solution)/shard_map/ppermute | solution.py:55
  127.9 7.9 %collective-permute-start.25 = (bf16[96,768]{1,0:T(8,128)(2,1)S(1)}, bf16[96,768]{1,0:T(8,128)(2,1)S(1)}, u32[]{:S(2)}, u32[]{:S(2)}) collective-permute-start(bf16[96,768]{1,0:T(8,128)(2,1)S(1)} %get-tuple-element.71), channel_id=1, source_target_pairs={{32,0},{9,1},{34,2},{11,3},{36,4},{13,5},{38,6},{15,7},{40,8},{1,9... | collective-permute-start | bytes 442376 | tf_op jit(solution)/shard_map/ppermute | solution.py:55
  129.1 7.7 %collective-permute-start.26 = (bf16[96,768]{1,0:T(8,128)(2,1)S(1)}, bf16[96,768]{1,0:T(8,128)(2,1)S(1)}, u32[]{:S(2)}, u32[]{:S(2)}) collective-permute-start(bf16[96,768]{1,0:T(8,128)(2,1)S(1)} %get-tuple-element.72), channel_id=1, source_target_pairs={{16,0},{5,1},{18,2},{7,3},{20,4},{9,5},{22,6},{11,7},{24,8},{13,9}... | collective-permute-start | bytes 442376 | tf_op jit(solution)/shard_map/ppermute | solution.py:55
  136.8 6.4 %collective-permute-start.27 = (f32[24,768]{1,0:T(8,128)S(1)}, f32[24,768]{1,0:T(8,128)S(1)}, u32[]{:S(2)}, u32[]{:S(2)}) collective-permute-start(f32[24,768]{1,0:T(8,128)S(1)} %get-tuple-element.74), channel_id=1, source_target_pairs={{12,0},{49,1},{14,2},{51,3},{0,4},{53,5},{2,6},{55,7},{4,8},{57,9}... | collective-permute-start | bytes 221192 | tf_op jit(solution)/shard_map/ppermute | solution.py:55
  136.9 6.3 %collective-permute-start.28 = (f32[24,768]{1,0:T(8,128)S(1)}, f32[24,768]{1,0:T(8,128)S(1)}, u32[]{:S(2)}, u32[]{:S(2)}) collective-permute-start(f32[24,768]{1,0:T(8,128)S(1)} %get-tuple-element.75), channel_id=1, source_target_pairs={{8,0},{33,1},{10,2},{35,3},{12,4},{37,5},{14,6},{39,7},{0,8},{41,9... | collective-permute-start | bytes 221192 | tf_op jit(solution)/shard_map/ppermute | solution.py:55
  139.2 4.9 %collective-permute-start.29 = (f32[24,768]{1,0:T(8,128)S(1)}, f32[24,768]{1,0:T(8,128)S(1)}, u32[]{:S(2)}, u32[]{:S(2)}) collective-permute-start(f32[24,768]{1,0:T(8,128)S(1)} %get-tuple-element.76), channel_id=1, source_target_pairs={{4,0},{17,1},{6,2},{19,3},{8,4},{21,5},{10,6},{23,7},{12,8},{25,9}... | collective-permute-start | bytes 221192 | tf_op jit(solution)/shard_map/ppermute | solution.py:55
  144.1 5.1 %collective-permute-start.30 = (f32[6,768]{1,0:T(8,128)S(1)}, f32[6,768]{1,0:T(8,128)S(1)}, u32[]{:S(2)}, u32[]{:S(2)}) collective-permute-start(f32[6,768]{1,0:T(8,128)S(1)} %get-tuple-element.78), channel_id=1, source_target_pairs={{66,0},{67,1},{64,2},{65,3},{70,4},{71,5},{68,6},{69,7},{74,8},{75... | collective-permute-start | bytes 55304 | tf_op jit(solution)/shard_map/ppermute | solution.py:44
  144.3 5.3 %collective-permute-start.31 = (f32[6,768]{1,0:T(8,128)S(1)}, f32[6,768]{1,0:T(8,128)S(1)}, u32[]{:S(2)}, u32[]{:S(2)}) collective-permute-start(f32[6,768]{1,0:T(8,128)S(1)} %get-tuple-element.79), channel_id=1, source_target_pairs={{2,0},{3,1},{0,2},{1,3},{6,4},{7,5},{4,6},{5,7},{10,8},{11,9},{8,1... | collective-permute-start | bytes 55304 | tf_op jit(solution)/shard_map/ppermute | solution.py:44
  146.4 3.9 %collective-permute-start.32 = (f32[6,768]{1,0:T(8,128)S(1)}, f32[6,768]{1,0:T(8,128)S(1)}, u32[]{:S(2)}, u32[]{:S(2)}) collective-permute-start(f32[6,768]{1,0:T(8,128)S(1)} %get-tuple-element.80), channel_id=1, source_target_pairs={{64,0},{65,1},{66,2},{67,3},{68,4},{69,5},{70,6},{71,7},{72,8},{73... | collective-permute-start | bytes 55304 | tf_op jit(solution)/shard_map/ppermute | solution.py:44

commit v3 on v2

--- a/solution.py
+++ b/solution.py
@@ -204,8 +204,9 @@
     )(*operands)
 
 
-def prepare_kernel(tok, w, qk, v_turned, w_v_turned):
+def prepare_kernel(tok, w, qk, v_turned, w_v_turned, late):
     width = tok.shape[2]
+    late[...] = tok[...]
 
     @pl.when(pl.program_id(0) == 0)
     def _():
@@ -220,7 +221,7 @@
     docs, tb, width = tokens.shape
     return call(
         prepare_kernel,
-        (bf16(docs, tb, 2 * width), bf16(width, docs * tb), bf16(width, width)),
+        (bf16(docs, tb, 2 * width), bf16(width, docs * tb), bf16(width, width), bf16(docs - CHUNK, tb, width)),
         [
             pl.BlockSpec((1, tb, width), lambda i: (i, 0, 0)),
             pl.BlockSpec(w_qkv.shape, lambda i: (0, 0), pipeline_mode=pl.Buffered(1)),
@@ -229,6 +230,7 @@
             pl.BlockSpec((1, tb, 2 * width), lambda i: (i, 0, 0)),
             pl.BlockSpec((width, tb), lambda i: (0, i)),
             pl.BlockSpec((width, width), lambda i: (0, 0)),
+            pl.BlockSpec((1, tb, width), lambda i: (jnp.maximum(i - CHUNK, 0), 0, 0)),
         ),
         flops=2 * docs * tb * width * 3 * width,
         moved=11 * 2**20,
@@ -399,7 +401,7 @@
 
 def grad_kernel(
     lengths, state, other, emb, rinv, everyone, target, product, stats, gain, normed, rstd, turned,
-    keep_out, send_out, loss_out, d_summed,
+    send_out, d_summed, loss_out,
 ):
     docs, width = target.shape
     all_docs = everyone.shape[0]
@@ -430,9 +432,11 @@
         keep = lax.axis_index("ctx") * tb + lax.broadcasted_iota(jnp.int32, (tb, 1), 0) < lengths[doc]
         scale = jnp.where(keep, rstd[doc, :, 0:1], 0.0)
         d_summed[doc * tb : (doc + 1) * tb, :] = (scale * (level - unit * along)).astype(jnp.bfloat16)
-    half = width // 2
-    send_out[...] = jnp.dot(turned[half:], d_summed[...], preferred_element_type=jnp.float32)
-    keep_out[...] = jnp.dot(turned[0:half], d_summed[...], preferred_element_type=jnp.float32)
+    send_out[...] = jnp.dot(turned[width // 2 :], d_summed[...], preferred_element_type=jnp.float32)
+
+
+def keep_kernel(turned, d_summed, out):
+    out[...] = jnp.dot(turned[0 : out.shape[0]], d_summed[...], preferred_element_type=jnp.float32)
 
 
 def sum_kernel(count, *refs):
@@ -458,16 +462,16 @@
     docs, tb, width = tokens.shape
     n_ctx, n_dp = lax.axis_size("ctx"), lax.axis_size("dp")
     all_docs = n_dp * docs
+    def halo(part):
+        left = lax.ppermute(part, "ctx", [(i, (i + 1) % n_ctx) for i in range(n_ctx)])
+        return left, lax.ppermute(part, "ctx", [((i + 1) % n_ctx, i) for i in range(n_ctx)])
+
+    halos = [halo(tokens[0:CHUNK])]
     swapped = swap(cache, "dp", 4)
-    halos = []
-    for first in range(0, docs, CHUNK):
-        part = tokens[first : first + CHUNK]
-        left = lax.ppermute(part, "ctx", [(i, (i + 1) % n_ctx) for i in range(n_ctx)])
-        right = lax.ppermute(part, "ctx", [((i + 1) % n_ctx, i) for i in range(n_ctx)])
-        halos.append((left, right))
     gain = ln_gain
-    qk, v_turned, w_v_turned = prepare(in_hbm(tokens), in_hbm(w_qkv))
-    swapped, w_v_turned = lax.optimization_barrier((swapped, w_v_turned))
+    qk, v_turned, w_v_turned, late = prepare(in_hbm(tokens), in_hbm(w_qkv))
+    swapped, late = lax.optimization_barrier((swapped, late))
+    halos.append(halo(late))
     rows = cache.shape[0]
     table = call(stack_kernel, bf16(2 * rows, width), [VMEM, VMEM], VMEM, limit=4, name="stack")(cache, swapped)
     tables = around(table, from_y)
@@ -529,18 +533,26 @@
     state = merged(docs, width, [state, swap(state, "ctx", 1)])
     state = merged(docs, width, around(state, from_x))
     half = width // 2
-    keep, send, loss = call(
+    send, d_summed, loss = call(
         grad_kernel,
-        (f32(half, width), f32(half, width), f32(8, 128)),
+        (f32(half, width), bf16(docs * tb, width), f32(8, 128)),
         [SMEM] + [VMEM] * 12,
         (VMEM,) * 3,
-        flops=2 * docs * tb * width * width,
+        flops=docs * tb * width * width,
         moved=8 * 2**20,
-        scratch_shapes=[pltpu.VMEM((docs * tb, width), jnp.bfloat16)],
         name="grad",
     )(
         lengths, state, swap(state, "ctx", 2), emb, rinv, everyone, target, product, stats, gain, normed, rstd, turned,
     )
+    keep = call(
+        keep_kernel,
+        f32(half, width),
+        [VMEM, VMEM],
+        VMEM,
+        flops=docs * tb * width * width,
+        moved=2**20,
+        name="keep",
+    )(turned, d_summed)
     keep, *sends = sum_and_split([keep, swap(send, "ctx", 1)], jnp.bfloat16)
     got = [from_plane(piece, -(k + 1), False) for k, piece in enumerate(sends)]
     keep, *sends = sum_and_split([keep] + got, jnp.float32)

time: 151 us -> 145 us (0.960)
  waiting for transfers between devices: 42.9 us -> 37.5 us
    ppermute x5, waiting for transfers between devices: 17.2 us -> 13.3 us  [swap(): lax.ppermute(value, axis, [(i, i ^ bits) for i in range(lax.axis_size(axi...]
    ppermute x6, starting transfers between devices: 8.19 us -> 12 us  [from_z(): return lax.ppermute(value, ('dp', 'ctx'), pairs)]
    ppermute x5, starting transfers between devices: 15.9 us -> 12.5 us  [swap(): lax.ppermute(value, axis, [(i, i ^ bits) for i in range(lax.axis_size(axi...]
    ppermute x6, starting transfers between devices: 8.65 us -> 6.74 us  [from_y(): lax.ppermute(value, 'dp', [(d & 4 | d + k & 3, d) for d in range(lax.axis...]
    pallas_call x1 -> x2, Pallas kernels: 2.94 us -> 3.4 us  [the longest x1 2.61 us: shards(): call(grad_kernel, (f32(half, width), bf16(docs * tb, width), f32(8, 128))...]
  transfers between devices with their start and end apart: 33 -> 33, of which waited for: 19 -> 21; matrix products, arithmetic and copies ran while one was open for 0% -> 0% of each run, Pallas kernels for 24% -> 17%
where the time goes in v3:
time: 145 us
  starting transfers between devices  61.5 us (42%)
  Pallas kernels  43.7 us (30%)
  waiting for transfers between devices  37.5 us (26%)
  local copies, waits for them, and re-layouts  1.77 us (1%)
    pallas_call x2, Pallas kernels, attend(): call(functools.partial(attend_kernel, first), out_shape, in_specs, (at(tb...  26.8 us
    ppermute x5, waiting for transfers between devices, swap(): lax.ppermute(value, axis, [(i, i ^ bits) for i in range(lax.axis_size(axi...  13.3 us
    ppermute x5, starting transfers between devices, swap(): lax.ppermute(value, axis, [(i, i ^ bits) for i in range(lax.axis_size(axi...  12.5 us
    ppermute x6, starting transfers between devices, from_z(): return lax.ppermute(value, ('dp', 'ctx'), pairs)  12 us
    ppermute x6, starting transfers between devices, from_x(): lax.ppermute(value, 'ctx', [((c + 4 * k) % size, c) for c in range(size)])  10.2 us
    ppermute x6, starting transfers between devices, from_plane(): return lax.ppermute(value, ('dp', 'ctx'), pairs)  8.82 us
    ppermute x6, waiting for transfers between devices, from_plane(): return lax.ppermute(value, ('dp', 'ctx'), pairs)  7.31 us
    pallas_call x1, Pallas kernels, prepare(): call(prepare_kernel, (bf16(docs, tb, 2 * width), bf16(width, docs * tb),...  7.27 us
  transfers between devices with their start and end apart: 33, of which 21 were waited for; matrix products, arithmetic and copies ran while one was open for 0% of the time, Pallas kernels for 17%

profile of v3, /device:TPU:0, one launch (start us, length us, event | category | flops | bytes accessed | tf_op | source)
XLA Modules:
  0.0 145.3 jit_solution(10884800139854776444)
XLA Ops:
  0.6 1.2 slice.6
  2.0 5.7 %collective-permute-start.4 = (bf16[2,256,768]{2,1,0:T(8,128)(2,1)S(1)}, bf16[2,256,768]{2,1,0:T(8,128)(2,1)S(1)}, u32[]{:S(2)}, u32[]{:S(2)}) collective-permute-start(bf16[2,256,768]{2,1,0:T(8,128)(2,1)S(1)} %slice.6), channel_id=1, source_target_pairs={{1,0},{2,1},{3,2},{4,3},{5,4},{6,5},{7,6},{8,7},{9,8},{10,9},{11,1... | collective-permute-start | bytes 2359304 | tf_op jit(solution)/shard_map/ppermute | solution.py:467
  7.6 1.7 %collective-permute-start = (bf16[128,768]{1,0:T(8,128)(2,1)S(1)}, bf16[128,768]{1,0:T(8,128)(2,1)S(1)}, u32[]{:S(2)}, u32[]{:S(2)}) collective-permute-start(bf16[128,768]{1,0:T(8,128)(2,1)S(1)} %copy-done.3), channel_id=1, source_target_pairs={{0,64},{16,80},{32,96},{48,112},{64,0},{80,16},{96,32},{112,48},{1... | collective-permute-start | bytes 589832 | tf_op jit(solution)/shard_map/ppermute | solution.py:25
  9.3 7.3 %prepare.1 = (bf16[4,256,1536]{2,1,0:T(8,128)(2,1)S(1)}, bf16[768,1024]{1,0:T(8,128)(2,1)S(1)}, bf16[768,768]{1,0:T(8,128)(2,1)S(1)}, bf16[2,256,768]{2,1,0:T(8,128)(2,1)S(1)}) custom-call(bf16[4,256,768]{2,1,0:T(8,128)(2,1)} %tok.5, bf16[768,2304]{1,0:T(8,128)(2,1)} %w_k.3), custom_call_target="tpu_custom_call" | custom-call | flops 3623878656 | bytes 11534336 | tf_op jit(solution)/shard_map/prepare/pallas_call | solution.py:222
  16.6 6.8 %collective-permute-done.refs_1_ = bf16[128,768]{1,0:T(8,128)(2,1)S(1)} collective-permute-done((bf16[128,768]{1,0:T(8,128)(2,1)S(1)}, bf16[128,768]{1,0:T(8,128)(2,1)S(1)}, u32[]{:S(2)}, u32[]{:S(2)}) %collective-permute-start) | collective-permute-done | bytes 196640 | tf_op jit(solution)/shard_map/ppermute | solution.py:25
  23.4 5.4 %collective-permute-start.1 = (bf16[2,256,768]{2,1,0:T(8,128)(2,1)S(1)}, bf16[2,256,768]{2,1,0:T(8,128)(2,1)S(1)}, u32[]{:S(2)}, u32[]{:S(2)}) collective-permute-start(bf16[2,256,768]{2,1,0:T(8,128)(2,1)S(1)} %get-tuple-element.44), channel_id=1, source_target_pairs={{0,1},{1,2},{2,3},{3,4},{4,5},{5,6},{6,7},{7,8},{8,9},{9,10},{10,1... | collective-permute-start | bytes 2359304 | tf_op jit(solution)/shard_map/ppermute | solution.py:466
  28.8 3.1 %collective-permute-start.5 = (bf16[256,768]{1,0:T(8,128)(2,1)S(1)}, bf16[256,768]{1,0:T(8,128)(2,1)S(1)}, u32[]{:S(2)}, u32[]{:S(2)}) collective-permute-start(bf16[256,768]{1,0:T(8,128)(2,1)S(1)} %stack.2.refs_0_.t0), channel_id=1, source_target_pairs={{16,0},{32,16},{48,32},{0,48},{80,64},{96,80},{112,96},{64,112},{1... | collective-permute-start | bytes 1179656 | tf_op jit(solution)/shard_map/ppermute | solution.py:34
  32.5 1.0 collective-permute-start.7
  33.6 13.4 %attend.2 = (bf16[4,256,768]{2,1,0:T(8,128)(2,1)}, bf16[768,1024]{1,0:T(8,128)(2,1)S(1)}, bf16[4,256,768]{2,1,0:T(8,128)(2,1)S(1)}, f32[4,256,128]{2,1,0:T(8,128)S(1)}, f32[4,1,768]{2,1,0:T(1,128)S(1)}) custom-call(s32[4]{0:T(128)S(1)} %copy-done.5, bf16[4,256,768]{2,1,0:T(8,128)(2,1)S(1)} %copy-done.1, ...), custom_call_target="tpu_custom_call" | custom-call | flops 3019898880 | bytes 8388608 | tf_op jit(solution)/shard_map/attend/pallas_call | solution.py:188
  47.0 0.9 target.1.refs_1_
  47.8 13.4 %attend.3 = (bf16[4,256,768]{2,1,0:T(8,128)(2,1)}, bf16[768,1024]{1,0:T(8,128)(2,1)S(1)}, bf16[4,256,768]{2,1,0:T(8,128)(2,1)S(1)}, f32[4,256,128]{2,1,0:T(8,128)S(1)}, f32[4,1,768]{2,1,0:T(1,128)S(1)}) custom-call(s32[4]{0:T(128)S(1)} %copy-done.5, ...), custom_call_target="tpu_custom_call", output_to_operand_aliasing={{0}: (10, {}), {1}: (11, {}), {2}: (12, {}), {3}: (13, {}),... | custom-call | flops 3019898880 | bytes 8388608 | tf_op jit(solution)/shard_map/attend/pallas_call | solution.py:188
  61.3 10.1 %collective-permute-start.8 = (f32[8,768]{1,0:T(8,128)S(1)}, f32[8,768]{1,0:T(8,128)S(1)}, u32[]{:S(2)}, u32[]{:S(2)}) collective-permute-start(f32[8,768]{1,0:T(8,128)S(1)} %stack.3.refs_0_), channel_id=1, source_target_pairs={{0,1},{1,0},{2,3},{3,2},{4,5},{5,4},{6,7},{7,6},{8,9},{9,8},{10,11... | collective-permute-start | bytes 73736 | tf_op jit(solution)/shard_map/ppermute | solution.py:25
  71.3 0.8 collective-permute-done.8.refs_1_
  72.2 2.7 %collective-permute-start.10 = (f32[8,768]{1,0:T(8,128)S(1)}, f32[8,768]{1,0:T(8,128)S(1)}, u32[]{:S(2)}, u32[]{:S(2)}) collective-permute-start(f32[8,768]{1,0:T(8,128)S(1)} %add.3.refs_0_), channel_id=1, source_target_pairs={{8,0},{9,1},{10,2},{11,3},{12,4},{13,5},{14,6},{15,7},{0,8},{1,9},... | collective-permute-start | bytes 73736 | tf_op jit(solution)/shard_map/ppermute | solution.py:30
  74.9 3.2 %collective-permute-start.9 = (f32[8,768]{1,0:T(8,128)S(1)}, f32[8,768]{1,0:T(8,128)S(1)}, u32[]{:S(2)}, u32[]{:S(2)}) collective-permute-start(f32[8,768]{1,0:T(8,128)S(1)} %add.3.refs_0_), channel_id=1, source_target_pairs={{4,0},{5,1},{6,2},{7,3},{8,4},{9,5},{10,6},{11,7},{12,8},{13,9},{1... | collective-permute-start | bytes 73736 | tf_op jit(solution)/shard_map/ppermute | solution.py:30
  78.1 1.8 %collective-permute-done.11.refs_3_ = f32[8,768]{1,0:T(8,128)S(1)} collective-permute-done((f32[8,768]{1,0:T(8,128)S(1)}, f32[8,768]{1,0:T(8,128)S(1)}, u32[]{:S(2)}, u32[]{:S(2)}) %collective-permute-start.11) | collective-permute-done | bytes 24608 | tf_op jit(solution)/shard_map/ppermute | solution.py:30
  79.9 5.6 %collective-permute-start.12 = (f32[8,768]{1,0:T(8,128)S(1)}, f32[8,768]{1,0:T(8,128)S(1)}, u32[]{:S(2)}, u32[]{:S(2)}) collective-permute-start(f32[8,768]{1,0:T(8,128)S(1)} %add.4.s0), channel_id=1, source_target_pairs={{64,0},{65,1},{66,2},{67,3},{68,4},{69,5},{70,6},{71,7},{72,8},{73... | collective-permute-start | bytes 73736 | tf_op jit(solution)/shard_map/ppermute | solution.py:44
  85.5 1.8 %collective-permute-start.13 = (f32[8,768]{1,0:T(8,128)S(1)}, f32[8,768]{1,0:T(8,128)S(1)}, u32[]{:S(2)}, u32[]{:S(2)}) collective-permute-start(f32[8,768]{1,0:T(8,128)S(1)} %add.4.s0), channel_id=1, source_target_pairs={{2,0},{3,1},{0,2},{1,3},{6,4},{7,5},{4,6},{5,7},{10,8},{11,9},{8,1... | collective-permute-start | bytes 73736 | tf_op jit(solution)/shard_map/ppermute | solution.py:44
  87.3 1.3 collective-permute-start.14
  88.6 2.2 %collective-permute-done.13.s2 = f32[8,768]{1,0:T(8,128)S(1)} collective-permute-done((f32[8,768]{1,0:T(8,128)S(1)}, f32[8,768]{1,0:T(8,128)S(1)}, u32[]{:S(2)}, u32[]{:S(2)}) %collective-permute-start.13) | collective-permute-done | bytes 24608 | tf_op jit(solution)/shard_map/ppermute | solution.py:44
  90.8 1.5 %collective-permute-done.14.s3 = f32[8,768]{1,0:T(8,128)S(1)} collective-permute-done((f32[8,768]{1,0:T(8,128)S(1)}, f32[8,768]{1,0:T(8,128)S(1)}, u32[]{:S(2)}, u32[]{:S(2)}) %collective-permute-start.14) | collective-permute-done | bytes 24608 | tf_op jit(solution)/shard_map/ppermute | solution.py:44
  93.7 0.8 collective-permute-start.17
  94.5 1.8 %collective-permute-done.15.e1 = f32[8,768]{1,0:T(8,128)S(1)} collective-permute-done((f32[8,768]{1,0:T(8,128)S(1)}, f32[8,768]{1,0:T(8,128)S(1)}, u32[]{:S(2)}, u32[]{:S(2)}) %collective-permute-start.15) | collective-permute-done | bytes 24608 | tf_op jit(solution)/shard_map/ppermute | solution.py:34
  96.3 2.1 %collective-permute-done.16.e2 = f32[8,768]{1,0:T(8,128)S(1)} collective-permute-done((f32[8,768]{1,0:T(8,128)S(1)}, f32[8,768]{1,0:T(8,128)S(1)}, u32[]{:S(2)}, u32[]{:S(2)}) %collective-permute-start.16) | collective-permute-done | bytes 24608 | tf_op jit(solution)/shard_map/ppermute | solution.py:34
  99.0 1.7 %score.1 = (f32[32,768]{1,0:T(8,128)S(1)}, f32[8,1024]{1,0:T(8,128)S(1)}) custom-call(s32[32]{0:T(128)S(1)} %copy-done.6, f32[8,768]{1,0:T(8,128)S(1)} %get-tuple-element.58.e0.emb, f32[8,768]{1,0:T(8,128)S(1)} %collective-permute-done.15.e1, f32[8,768]{1,0:T(8,128)S(1)} %collective-permute-done.16.e2, f32[8,768]{1,0:T(8,128)S(1)} %collective-permute-done.17.e3, ...), custom_call_target="tpu_custom_call" | custom-call | bytes 2097152 | tf_op jit(solution)/shard_map/score/pallas_call | solution.py:516
  100.8 1.2 collective-permute-done.18.refs_1_
  102.1 3.3 %collective-permute-start.19 = (f32[8,1024]{1,0:T(8,128)S(1)}, f32[8,1024]{1,0:T(8,128)S(1)}, u32[]{:S(2)}, u32[]{:S(2)}) collective-permute-start(f32[8,1024]{1,0:T(8,128)S(1)} %merge.2.refs_0_), channel_id=1, source_target_pairs={{4,0},{5,1},{6,2},{7,3},{8,4},{9,5},{10,6},{11,7},{12,8},{13,9},{1... | collective-permute-start | bytes 98312 | tf_op jit(solution)/shard_map/ppermute | solution.py:30
  105.4 0.9 collective-permute-start.21
  106.3 0.6 collective-permute-done.19.refs_1_
  107.0 3.9 %collective-permute-done.20.refs_2_ = f32[8,1024]{1,0:T(8,128)S(1)} collective-permute-done((f32[8,1024]{1,0:T(8,128)S(1)}, f32[8,1024]{1,0:T(8,128)S(1)}, u32[]{:S(2)}, u32[]{:S(2)}) %collective-permute-start.20) | collective-permute-done | bytes 32800 | tf_op jit(solution)/shard_map/ppermute | solution.py:30
  111.0 0.6 collective-permute-start.22
  111.6 2.1 %turn.1.turned = bf16[768,1024]{1,0:T(8,128)(2,1)S(1)} custom-call(bf16[768,1024]{1,0:T(8,128)(2,1)S(1)} %get-tuple-element.67.mixed), custom_call_target="tpu_custom_call" | custom-call | flops 1207959552 | bytes 4194304 | tf_op jit(solution)/shard_map/turn/pallas_call | solution.py:492
  114.0 2.4 %collective-permute-done.22.other = f32[8,1024]{1,0:T(8,128)S(1)} collective-permute-done((f32[8,1024]{1,0:T(8,128)S(1)}, f32[8,1024]{1,0:T(8,128)S(1)}, u32[]{:S(2)}, u32[]{:S(2)}) %collective-permute-start.22) | collective-permute-done | bytes 32800 | tf_op jit(solution)/shard_map/ppermute | solution.py:25
  116.5 2.6 %grad.1 = (f32[384,768]{1,0:T(8,128)S(1)}, bf16[1024,768]{1,0:T(8,128)(2,1)S(1)}, f32[8,128]{1,0:T(8,128)S(1)}) custom-call(s32[4]{0:T(128)S(1)} %copy-done.5, f32[8,1024]{1,0:T(8,128)S(1)} %merge.3.state, f32[8,1024]{1,0:T(8,128)S(1)} %collective-permute-done.22.other, f32[8,768]{1,0:T(8,128)S(1)} %get-tuple-element.58.e0.emb, ...), custom_call_target="tpu_custom_call" | custom-call | flops 603979776 | bytes 8388608 | tf_op jit(solution)/shard_map/grad/pallas_call | solution.py:536
  119.2 0.8 keep.1.refs_0_
  119.9 2.0 %collective-permute-done.23.refs_1_ = f32[384,768]{1,0:T(8,128)S(1)} collective-permute-done((f32[384,768]{1,0:T(8,128)S(1)}, f32[384,768]{1,0:T(8,128)S(1)}, u32[]{:S(2)}, u32[]{:S(2)}) %collective-permute-start.23) | collective-permute-done | bytes 1179680 | tf_op jit(solution)/shard_map/ppermute | solution.py:25
  122.2 0.9 collective-permute-start.24
  123.1 2.6 %collective-permute-start.25 = (bf16[96,768]{1,0:T(8,128)(2,1)S(1)}, bf16[96,768]{1,0:T(8,128)(2,1)S(1)}, u32[]{:S(2)}, u32[]{:S(2)}) collective-permute-start(bf16[96,768]{1,0:T(8,128)(2,1)S(1)} %get-tuple-element.73), channel_id=1, source_target_pairs={{32,0},{9,1},{34,2},{11,3},{36,4},{13,5},{38,6},{15,7},{40,8},{1,9... | collective-permute-start | bytes 442376 | tf_op jit(solution)/shard_map/ppermute | solution.py:55
  126.3 2.3 %collective-permute-done.24.refs_1_ = bf16[96,768]{1,0:T(8,128)(2,1)S(1)} collective-permute-done((bf16[96,768]{1,0:T(8,128)(2,1)S(1)}, bf16[96,768]{1,0:T(8,128)(2,1)S(1)}, u32[]{:S(2)}, u32[]{:S(2)}) %collective-permute-start.24) | collective-permute-done | bytes 147488 | tf_op jit(solution)/shard_map/ppermute | solution.py:55
  128.6 1.8 %collective-permute-done.25.refs_2_ = bf16[96,768]{1,0:T(8,128)(2,1)S(1)} collective-permute-done((bf16[96,768]{1,0:T(8,128)(2,1)S(1)}, bf16[96,768]{1,0:T(8,128)(2,1)S(1)}, u32[]{:S(2)}, u32[]{:S(2)}) %collective-permute-start.25) | collective-permute-done | bytes 147488 | tf_op jit(solution)/shard_map/ppermute | solution.py:55
  131.2 2.3 %collective-permute-start.28 = (f32[24,768]{1,0:T(8,128)S(1)}, f32[24,768]{1,0:T(8,128)S(1)}, u32[]{:S(2)}, u32[]{:S(2)}) collective-permute-start(f32[24,768]{1,0:T(8,128)S(1)} %get-tuple-element.77), channel_id=1, source_target_pairs={{8,0},{33,1},{10,2},{35,3},{12,4},{37,5},{14,6},{39,7},{0,8},{41,9... | collective-permute-start | bytes 221192 | tf_op jit(solution)/shard_map/ppermute | solution.py:55
  133.5 2.3 %collective-permute-start.29 = (f32[24,768]{1,0:T(8,128)S(1)}, f32[24,768]{1,0:T(8,128)S(1)}, u32[]{:S(2)}, u32[]{:S(2)}) collective-permute-start(f32[24,768]{1,0:T(8,128)S(1)} %get-tuple-element.78), channel_id=1, source_target_pairs={{4,0},{17,1},{6,2},{19,3},{8,4},{21,5},{10,6},{23,7},{12,8},{25,9}... | collective-permute-start | bytes 221192 | tf_op jit(solution)/shard_map/ppermute | solution.py:55
  135.8 1.8 %collective-permute-done.27.refs_1_ = f32[24,768]{1,0:T(8,128)S(1)} collective-permute-done((f32[24,768]{1,0:T(8,128)S(1)}, f32[24,768]{1,0:T(8,128)S(1)}, u32[]{:S(2)}, u32[]{:S(2)}) %collective-permute-start.27) | collective-permute-done | bytes 73760 | tf_op jit(solution)/shard_map/ppermute | solution.py:55
  137.5 0.9 collective-permute-done.29.refs_3_
  138.6 2.1 %collective-permute-start.31 = (f32[6,768]{1,0:T(8,128)S(1)}, f32[6,768]{1,0:T(8,128)S(1)}, u32[]{:S(2)}, u32[]{:S(2)}) collective-permute-start(f32[6,768]{1,0:T(8,128)S(1)} %get-tuple-element.81), channel_id=1, source_target_pairs={{2,0},{3,1},{0,2},{1,3},{6,4},{7,5},{4,6},{5,7},{10,8},{11,9},{8,1... | collective-permute-start | bytes 55304 | tf_op jit(solution)/shard_map/ppermute | solution.py:44
  140.7 1.0 collective-permute-start.32
  142.2 1.3 collective-permute-done.30.refs_1_
  143.9 0.7 collective-permute-done.32.refs_3_
  (55 shorter events, 6.7 us)
Async XLA Ops:
  0.6 7.0 %copy-start.3 = (bf16[128,768]{1,0:T(8,128)(2,1)S(1)}, bf16[128,768]{1,0:T(8,128)(2,1)}, u32[]{:S(2)}) copy-start(bf16[128,768]{1,0:T(8,128)(2,1)} %refs_0_.1) | copy-start | bytes 589828
  1.9 31.6 %copy-start.4 = (f32[768]{0:T(1024)S(1)}, f32[768]{0:T(1024)}, u32[]{:S(2)}) copy-start(f32[768]{0:T(1024)} %gain.5) | copy-start | bytes 9220
  1.9 31.6 %copy-start.5 = (s32[4]{0:T(128)S(1)}, s32[4]{0:T(128)}, u32[]{:S(2)}) copy-start(s32[4]{0:T(128)} %lengths.5) | copy-start | bytes 52
  1.9 30.0 %collective-permute-start.3 = (bf16[2,256,768]{2,1,0:T(8,128)(2,1)S(1)}, bf16[2,256,768]{2,1,0:T(8,128)(2,1)S(1)}, u32[]{:S(2)}, u32[]{:S(2)}) collective-permute-start(bf16[2,256,768]{2,1,0:T(8,128)(2,1)S(1)} %slice.6), channel_id=1, source_target_pairs={{0,1},{1,2},{2,3},{3,4},{4,5},{5,6},{6,7},{7,8},{8,9},{9,10},{10,1... | collective-permute-start | bytes 2359304 | tf_op jit(solution)/shard_map/ppermute | solution.py:466
  2.0 30.6 %collective-permute-start.4 = (bf16[2,256,768]{2,1,0:T(8,128)(2,1)S(1)}, bf16[2,256,768]{2,1,0:T(8,128)(2,1)S(1)}, u32[]{:S(2)}, u32[]{:S(2)}) collective-permute-start(bf16[2,256,768]{2,1,0:T(8,128)(2,1)S(1)} %slice.6), channel_id=1, source_target_pairs={{1,0},{2,1},{3,2},{4,3},{5,4},{6,5},{7,6},{8,7},{9,8},{10,9},{11,1... | collective-permute-start | bytes 2359304 | tf_op jit(solution)/shard_map/ppermute | solution.py:467
  7.6 15.7 %collective-permute-start = (bf16[128,768]{1,0:T(8,128)(2,1)S(1)}, bf16[128,768]{1,0:T(8,128)(2,1)S(1)}, u32[]{:S(2)}, u32[]{:S(2)}) collective-permute-start(bf16[128,768]{1,0:T(8,128)(2,1)S(1)} %copy-done.3), channel_id=1, source_target_pairs={{0,64},{16,80},{32,96},{48,112},{64,0},{80,16},{96,32},{112,48},{1... | collective-permute-start | bytes 589832 | tf_op jit(solution)/shard_map/ppermute | solution.py:25
  9.3 24.2 %copy-start = (bf16[768,2304]{1,0:T(8,128)(2,1)S(1)}, bf16[768,2304]{1,0:T(8,128)(2,1)}, u32[]{:S(2)}) copy-start(bf16[768,2304]{1,0:T(8,128)(2,1)} %w_k.3) | copy-start | bytes 10616836
  9.3 24.2 %copy-start.1 = (bf16[4,256,768]{2,1,0:T(8,128)(2,1)S(1)}, bf16[4,256,768]{2,1,0:T(8,128)(2,1)}, u32[]{:S(2)}) copy-start(bf16[4,256,768]{2,1,0:T(8,128)(2,1)} %tok.5) | copy-start | bytes 4718596
  9.3 24.2 %copy-start.2 = (bf16[768,768]{1,0:T(8,128)(2,1)S(1)}, bf16[768,768]{1,0:T(8,128)(2,1)}, u32[]{:S(2)}) copy-start(bf16[768,768]{1,0:T(8,128)(2,1)} %w_out.3) | copy-start | bytes 3538948
  23.4 24.4 %collective-permute-start.1 = (bf16[2,256,768]{2,1,0:T(8,128)(2,1)S(1)}, bf16[2,256,768]{2,1,0:T(8,128)(2,1)S(1)}, u32[]{:S(2)}, u32[]{:S(2)}) collective-permute-start(bf16[2,256,768]{2,1,0:T(8,128)(2,1)S(1)} %get-tuple-element.44), channel_id=1, source_target_pairs={{0,1},{1,2},{2,3},{3,4},{4,5},{5,6},{6,7},{7,8},{8,9},{9,10},{10,1... | collective-permute-start | bytes 2359304 | tf_op jit(solution)/shard_map/ppermute | solution.py:466
  28.8 19.1 %collective-permute-start.2 = (bf16[2,256,768]{2,1,0:T(8,128)(2,1)S(1)}, bf16[2,256,768]{2,1,0:T(8,128)(2,1)S(1)}, u32[]{:S(2)}, u32[]{:S(2)}) collective-permute-start(bf16[2,256,768]{2,1,0:T(8,128)(2,1)S(1)} %get-tuple-element.44), channel_id=1, source_target_pairs={{1,0},{2,1},{3,2},{4,3},{5,4},{6,5},{7,6},{8,7},{9,8},{10,9},{11,1... | collective-permute-start | bytes 2359304 | tf_op jit(solution)/shard_map/ppermute | solution.py:467
  28.8 18.1 %collective-permute-start.5 = (bf16[256,768]{1,0:T(8,128)(2,1)S(1)}, bf16[256,768]{1,0:T(8,128)(2,1)S(1)}, u32[]{:S(2)}, u32[]{:S(2)}) collective-permute-start(bf16[256,768]{1,0:T(8,128)(2,1)S(1)} %stack.2.refs_0_.t0), channel_id=1, source_target_pairs={{16,0},{32,16},{48,32},{0,48},{80,64},{96,80},{112,96},{64,112},{1... | collective-permute-start | bytes 1179656 | tf_op jit(solution)/shard_map/ppermute | solution.py:34
  31.9 15.0 %collective-permute-start.6 = (bf16[256,768]{1,0:T(8,128)(2,1)S(1)}, bf16[256,768]{1,0:T(8,128)(2,1)S(1)}, u32[]{:S(2)}, u32[]{:S(2)}) collective-permute-start(bf16[256,768]{1,0:T(8,128)(2,1)S(1)} %stack.2.refs_0_.t0), channel_id=1, source_target_pairs={{32,0},{48,16},{0,32},{16,48},{96,64},{112,80},{64,96},{80,112},{3... | collective-permute-start | bytes 1179656 | tf_op jit(solution)/shard_map/ppermute | solution.py:34
  32.5 14.4 %collective-permute-start.7 = (bf16[256,768]{1,0:T(8,128)(2,1)S(1)}, bf16[256,768]{1,0:T(8,128)(2,1)S(1)}, u32[]{:S(2)}, u32[]{:S(2)}) collective-permute-start(bf16[256,768]{1,0:T(8,128)(2,1)S(1)} %stack.2.refs_0_.t0), channel_id=1, source_target_pairs={{48,0},{0,16},{16,32},{32,48},{112,64},{64,80},{80,96},{96,112},{4... | collective-permute-start | bytes 1179656 | tf_op jit(solution)/shard_map/ppermute | solution.py:34
  33.5 13.4 %copy-start.6 = (s32[32]{0:T(128)S(1)}, s32[32]{0:T(128)}, u32[]{:S(2)}) copy-start(s32[32]{0:T(128)} %positive.2) | copy-start | bytes 388
  61.3 10.9 %collective-permute-start.8 = (f32[8,768]{1,0:T(8,128)S(1)}, f32[8,768]{1,0:T(8,128)S(1)}, u32[]{:S(2)}, u32[]{:S(2)}) collective-permute-start(f32[8,768]{1,0:T(8,128)S(1)} %stack.3.refs_0_), channel_id=1, source_target_pairs={{0,1},{1,0},{2,3},{3,2},{4,5},{5,4},{6,7},{7,6},{8,9},{9,8},{10,11... | collective-permute-start | bytes 73736 | tf_op jit(solution)/shard_map/ppermute | solution.py:25
  72.2 6.0 %collective-permute-start.10 = (f32[8,768]{1,0:T(8,128)S(1)}, f32[8,768]{1,0:T(8,128)S(1)}, u32[]{:S(2)}, u32[]{:S(2)}) collective-permute-start(f32[8,768]{1,0:T(8,128)S(1)} %add.3.refs_0_), channel_id=1, source_target_pairs={{8,0},{9,1},{10,2},{11,3},{12,4},{13,5},{14,6},{15,7},{0,8},{1,9},... | collective-permute-start | bytes 73736 | tf_op jit(solution)/shard_map/ppermute | solution.py:30
  74.9 5.0 %collective-permute-start.11 = (f32[8,768]{1,0:T(8,128)S(1)}, f32[8,768]{1,0:T(8,128)S(1)}, u32[]{:S(2)}, u32[]{:S(2)}) collective-permute-start(f32[8,768]{1,0:T(8,128)S(1)} %add.3.refs_0_), channel_id=1, source_target_pairs={{12,0},{13,1},{14,2},{15,3},{0,4},{1,5},{2,6},{3,7},{4,8},{5,9},{6... | collective-permute-start | bytes 73736 | tf_op jit(solution)/shard_map/ppermute | solution.py:30
  74.9 5.0 %collective-permute-start.9 = (f32[8,768]{1,0:T(8,128)S(1)}, f32[8,768]{1,0:T(8,128)S(1)}, u32[]{:S(2)}, u32[]{:S(2)}) collective-permute-start(f32[8,768]{1,0:T(8,128)S(1)} %add.3.refs_0_), channel_id=1, source_target_pairs={{4,0},{5,1},{6,2},{7,3},{8,4},{9,5},{10,6},{11,7},{12,8},{13,9},{1... | collective-permute-start | bytes 73736 | tf_op jit(solution)/shard_map/ppermute | solution.py:30
  79.9 8.7 %collective-permute-start.12 = (f32[8,768]{1,0:T(8,128)S(1)}, f32[8,768]{1,0:T(8,128)S(1)}, u32[]{:S(2)}, u32[]{:S(2)}) collective-permute-start(f32[8,768]{1,0:T(8,128)S(1)} %add.4.s0), channel_id=1, source_target_pairs={{64,0},{65,1},{66,2},{67,3},{68,4},{69,5},{70,6},{71,7},{72,8},{73... | collective-permute-start | bytes 73736 | tf_op jit(solution)/shard_map/ppermute | solution.py:44
  85.5 5.3 %collective-permute-start.13 = (f32[8,768]{1,0:T(8,128)S(1)}, f32[8,768]{1,0:T(8,128)S(1)}, u32[]{:S(2)}, u32[]{:S(2)}) collective-permute-start(f32[8,768]{1,0:T(8,128)S(1)} %add.4.s0), channel_id=1, source_target_pairs={{2,0},{3,1},{0,2},{1,3},{6,4},{7,5},{4,6},{5,7},{10,8},{11,9},{8,1... | collective-permute-start | bytes 73736 | tf_op jit(solution)/shard_map/ppermute | solution.py:44
  87.3 5.0 %collective-permute-start.14 = (f32[8,768]{1,0:T(8,128)S(1)}, f32[8,768]{1,0:T(8,128)S(1)}, u32[]{:S(2)}, u32[]{:S(2)}) collective-permute-start(f32[8,768]{1,0:T(8,128)S(1)} %add.4.s0), channel_id=1, source_target_pairs={{66,0},{67,1},{64,2},{65,3},{70,4},{71,5},{68,6},{69,7},{74,8},{75... | collective-permute-start | bytes 73736 | tf_op jit(solution)/shard_map/ppermute | solution.py:44
  92.4 3.8 %collective-permute-start.15 = (f32[8,768]{1,0:T(8,128)S(1)}, f32[8,768]{1,0:T(8,128)S(1)}, u32[]{:S(2)}, u32[]{:S(2)}) collective-permute-start(f32[8,768]{1,0:T(8,128)S(1)} %get-tuple-element.58.e0.emb), channel_id=1, source_target_pairs={{16,0},{32,16},{48,32},{0,48},{80,64},{96,80},{112,96},{64,112},{1... | collective-permute-start | bytes 73736 | tf_op jit(solution)/shard_map/ppermute | solution.py:34
  93.1 5.3 %collective-permute-start.16 = (f32[8,768]{1,0:T(8,128)S(1)}, f32[8,768]{1,0:T(8,128)S(1)}, u32[]{:S(2)}, u32[]{:S(2)}) collective-permute-start(f32[8,768]{1,0:T(8,128)S(1)} %get-tuple-element.58.e0.emb), channel_id=1, source_target_pairs={{32,0},{48,16},{0,32},{16,48},{96,64},{112,80},{64,96},{80,112},{3... | collective-permute-start | bytes 73736 | tf_op jit(solution)/shard_map/ppermute | solution.py:34
  93.7 5.3 %collective-permute-start.17 = (f32[8,768]{1,0:T(8,128)S(1)}, f32[8,768]{1,0:T(8,128)S(1)}, u32[]{:S(2)}, u32[]{:S(2)}) collective-permute-start(f32[8,768]{1,0:T(8,128)S(1)} %get-tuple-element.58.e0.emb), channel_id=1, source_target_pairs={{48,0},{0,16},{16,32},{32,48},{112,64},{64,80},{80,96},{96,112},{4... | collective-permute-start | bytes 73736 | tf_op jit(solution)/shard_map/ppermute | solution.py:34
  100.7 1.3 collective-permute-start.18
  102.1 4.9 %collective-permute-start.19 = (f32[8,1024]{1,0:T(8,128)S(1)}, f32[8,1024]{1,0:T(8,128)S(1)}, u32[]{:S(2)}, u32[]{:S(2)}) collective-permute-start(f32[8,1024]{1,0:T(8,128)S(1)} %merge.2.refs_0_), channel_id=1, source_target_pairs={{4,0},{5,1},{6,2},{7,3},{8,4},{9,5},{10,6},{11,7},{12,8},{13,9},{1... | collective-permute-start | bytes 98312 | tf_op jit(solution)/shard_map/ppermute | solution.py:30
  105.4 5.5 %collective-permute-start.20 = (f32[8,1024]{1,0:T(8,128)S(1)}, f32[8,1024]{1,0:T(8,128)S(1)}, u32[]{:S(2)}, u32[]{:S(2)}) collective-permute-start(f32[8,1024]{1,0:T(8,128)S(1)} %merge.2.refs_0_), channel_id=1, source_target_pairs={{8,0},{9,1},{10,2},{11,3},{12,4},{13,5},{14,6},{15,7},{0,8},{1,9},... | collective-permute-start | bytes 98312 | tf_op jit(solution)/shard_map/ppermute | solution.py:30
  105.4 5.5 %collective-permute-start.21 = (f32[8,1024]{1,0:T(8,128)S(1)}, f32[8,1024]{1,0:T(8,128)S(1)}, u32[]{:S(2)}, u32[]{:S(2)}) collective-permute-start(f32[8,1024]{1,0:T(8,128)S(1)} %merge.2.refs_0_), channel_id=1, source_target_pairs={{12,0},{13,1},{14,2},{15,3},{0,4},{1,5},{2,6},{3,7},{4,8},{5,9},{6... | collective-permute-start | bytes 98312 | tf_op jit(solution)/shard_map/ppermute | solution.py:30
  111.0 5.5 %collective-permute-start.22 = (f32[8,1024]{1,0:T(8,128)S(1)}, f32[8,1024]{1,0:T(8,128)S(1)}, u32[]{:S(2)}, u32[]{:S(2)}) collective-permute-start(f32[8,1024]{1,0:T(8,128)S(1)} %merge.3.state), channel_id=1, source_target_pairs={{0,2},{1,3},{2,0},{3,1},{4,6},{5,7},{6,4},{7,5},{8,10},{9,11},{10,... | collective-permute-start | bytes 98312 | tf_op jit(solution)/shard_map/ppermute | solution.py:25
  119.1 2.9 %collective-permute-start.23 = (f32[384,768]{1,0:T(8,128)S(1)}, f32[384,768]{1,0:T(8,128)S(1)}, u32[]{:S(2)}, u32[]{:S(2)}) collective-permute-start(f32[384,768]{1,0:T(8,128)S(1)} %get-tuple-element.70), channel_id=1, source_target_pairs={{0,1},{1,0},{2,3},{3,2},{4,5},{5,4},{6,7},{7,6},{8,9},{9,8},{10,11... | collective-permute-start | bytes 3538952 | tf_op jit(solution)/shard_map/ppermute | solution.py:25
  122.2 6.4 %collective-permute-start.24 = (bf16[96,768]{1,0:T(8,128)(2,1)S(1)}, bf16[96,768]{1,0:T(8,128)(2,1)S(1)}, u32[]{:S(2)}, u32[]{:S(2)}) collective-permute-start(bf16[96,768]{1,0:T(8,128)(2,1)S(1)} %get-tuple-element.72), channel_id=1, source_target_pairs={{48,0},{13,1},{50,2},{15,3},{52,4},{1,5},{54,6},{3,7},{56,8},{5,9}... | collective-permute-start | bytes 442376 | tf_op jit(solution)/shard_map/ppermute | solution.py:55
  123.1 7.3 %collective-permute-start.25 = (bf16[96,768]{1,0:T(8,128)(2,1)S(1)}, bf16[96,768]{1,0:T(8,128)(2,1)S(1)}, u32[]{:S(2)}, u32[]{:S(2)}) collective-permute-start(bf16[96,768]{1,0:T(8,128)(2,1)S(1)} %get-tuple-element.73), channel_id=1, source_target_pairs={{32,0},{9,1},{34,2},{11,3},{36,4},{13,5},{38,6},{15,7},{40,8},{1,9... | collective-permute-start | bytes 442376 | tf_op jit(solution)/shard_map/ppermute | solution.py:55
  125.7 5.3 %collective-permute-start.26 = (bf16[96,768]{1,0:T(8,128)(2,1)S(1)}, bf16[96,768]{1,0:T(8,128)(2,1)S(1)}, u32[]{:S(2)}, u32[]{:S(2)}) collective-permute-start(bf16[96,768]{1,0:T(8,128)(2,1)S(1)} %get-tuple-element.74), channel_id=1, source_target_pairs={{16,0},{5,1},{18,2},{7,3},{20,4},{9,5},{22,6},{11,7},{24,8},{13,9}... | collective-permute-start | bytes 442376 | tf_op jit(solution)/shard_map/ppermute | solution.py:55
  131.1 6.4 %collective-permute-start.27 = (f32[24,768]{1,0:T(8,128)S(1)}, f32[24,768]{1,0:T(8,128)S(1)}, u32[]{:S(2)}, u32[]{:S(2)}) collective-permute-start(f32[24,768]{1,0:T(8,128)S(1)} %get-tuple-element.76), channel_id=1, source_target_pairs={{12,0},{49,1},{14,2},{51,3},{0,4},{53,5},{2,6},{55,7},{4,8},{57,9}... | collective-permute-start | bytes 221192 | tf_op jit(solution)/shard_map/ppermute | solution.py:55
  131.2 6.3 %collective-permute-start.28 = (f32[24,768]{1,0:T(8,128)S(1)}, f32[24,768]{1,0:T(8,128)S(1)}, u32[]{:S(2)}, u32[]{:S(2)}) collective-permute-start(f32[24,768]{1,0:T(8,128)S(1)} %get-tuple-element.77), channel_id=1, source_target_pairs={{8,0},{33,1},{10,2},{35,3},{12,4},{37,5},{14,6},{39,7},{0,8},{41,9... | collective-permute-start | bytes 221192 | tf_op jit(solution)/shard_map/ppermute | solution.py:55
  133.5 4.9 %collective-permute-start.29 = (f32[24,768]{1,0:T(8,128)S(1)}, f32[24,768]{1,0:T(8,128)S(1)}, u32[]{:S(2)}, u32[]{:S(2)}) collective-permute-start(f32[24,768]{1,0:T(8,128)S(1)} %get-tuple-element.78), channel_id=1, source_target_pairs={{4,0},{17,1},{6,2},{19,3},{8,4},{21,5},{10,6},{23,7},{12,8},{25,9}... | collective-permute-start | bytes 221192 | tf_op jit(solution)/shard_map/ppermute | solution.py:55
  138.4 5.1 %collective-permute-start.30 = (f32[6,768]{1,0:T(8,128)S(1)}, f32[6,768]{1,0:T(8,128)S(1)}, u32[]{:S(2)}, u32[]{:S(2)}) collective-permute-start(f32[6,768]{1,0:T(8,128)S(1)} %get-tuple-element.80), channel_id=1, source_target_pairs={{66,0},{67,1},{64,2},{65,3},{70,4},{71,5},{68,6},{69,7},{74,8},{75... | collective-permute-start | bytes 55304 | tf_op jit(solution)/shard_map/ppermute | solution.py:44
  138.6 5.3 %collective-permute-start.31 = (f32[6,768]{1,0:T(8,128)S(1)}, f32[6,768]{1,0:T(8,128)S(1)}, u32[]{:S(2)}, u32[]{:S(2)}) collective-permute-start(f32[6,768]{1,0:T(8,128)S(1)} %get-tuple-element.81), channel_id=1, source_target_pairs={{2,0},{3,1},{0,2},{1,3},{6,4},{7,5},{4,6},{5,7},{10,8},{11,9},{8,1... | collective-permute-start | bytes 55304 | tf_op jit(solution)/shard_map/ppermute | solution.py:44
  140.7 3.9 %collective-permute-start.32 = (f32[6,768]{1,0:T(8,128)S(1)}, f32[6,768]{1,0:T(8,128)S(1)}, u32[]{:S(2)}, u32[]{:S(2)}) collective-permute-start(f32[6,768]{1,0:T(8,128)S(1)} %get-tuple-element.82), channel_id=1, source_target_pairs={{64,0},{65,1},{66,2},{67,3},{68,4},{69,5},{70,6},{71,7},{72,8},{73... | collective-permute-start | bytes 55304 | tf_op jit(solution)/shard_map/ppermute | solution.py:44

commit v4 on v3

--- a/solution.py
+++ b/solution.py
@@ -239,20 +239,17 @@
     )(tokens, w_qkv)
 
 
-def row_ids(k, rows, shape, dim):
+def row_ids(k, shape, dim):
+    dp, ctx = here()
     place = lax.broadcasted_iota(jnp.int32, shape, dim)
-    dp, ctx = here()
-    y, z_lo = (dp + k) & 3, dp >> 2
-    other = (place >= rows).astype(jnp.int32)
-    owner = (z_lo + other - 2 * z_lo * other) * 4 + y
-    return (owner * 16 + ctx) * rows + place - other * rows
-
-
-def stack_kernel(*refs):
-    low = 0
-    for ref in refs[:-1]:
-        refs[-1][low : low + ref.shape[0], :] = ref[...]
-        low += ref.shape[0]
+    return (((dp & 4) | ((dp + k) & 3)) * 16 + ctx) * shape[dim] + place
+
+
+def stack_kernel(pool, target, out):
+    docs = pool.shape[0]
+    for doc in range(docs):
+        out[doc : doc + 1, :] = pool[doc]
+    out[docs:, :] = target[...]
 
 
 def add_kernel(*refs):
@@ -277,16 +274,16 @@
 
 def target_kernel(docs, positive, *refs):
     pieces, out = refs[:4], refs[4]
+    dp, _ = here()
     total = jnp.zeros(out.shape, jnp.float32)
     for k, piece in enumerate(pieces):
-        rows = piece.shape[0]
-        ids = row_ids(k, rows // 2, (8, rows), 1)
-        doc = lax.broadcasted_iota(jnp.int32, (8, rows), 0)
-        wanted = jnp.full((8, rows), -1, jnp.int32)
-        for d in range(docs):
-            wanted = jnp.where(doc == d, positive[lax.axis_index("dp") * docs + d], wanted)
-        hit = (ids == wanted).astype(jnp.float32).astype(jnp.bfloat16)
-        total = total + jnp.dot(hit, piece[...], preferred_element_type=jnp.float32)[0:docs]
+        shape = (out.shape[0], piece.shape[0])
+        doc = lax.broadcasted_iota(jnp.int32, shape, 0)
+        wanted = jnp.zeros(shape, jnp.int32)
+        for d in range(2 * docs):
+            wanted = jnp.where(doc == d, positive[(d // docs * 4 + (dp & 3)) * docs + d % docs], wanted)
+        hit = (row_ids(k, shape, 1) == wanted).astype(jnp.float32).astype(jnp.bfloat16)
+        total = total + jnp.dot(hit, piece[...], preferred_element_type=jnp.float32)
     out[...] = total
 
 
@@ -307,13 +304,15 @@
 
 
 def norm_kernel(s0, s1, s2, s3, emb_out, rinv_out, target_out):
-    docs = target_out.shape[0]
-    own, other = s0[...] + s2[...], s1[0:docs] + s3[0:docs]
-    pooled = jnp.concatenate([own[0:docs], other], axis=0)
+    docs = s0.shape[0] // 3
+    dp, _ = here()
+    own, other = s0[0:docs] + s2[0:docs], s1[0:docs] + s3[0:docs]
+    second = dp >= 4
+    pooled = jnp.concatenate([jnp.where(second, other, own), jnp.where(second, own, other)], axis=0)
     rinv = lax.rsqrt(jnp.sum(pooled * pooled, axis=1, keepdims=True) + 1e-06)
     emb_out[...] = pooled * rinv
     rinv_out[...] = jnp.broadcast_to(rinv, rinv_out.shape)
-    target_out[...] = own[docs:]
+    target_out[...] = (s0[docs:] + s2[docs:]) + (s1[docs:] + s3[docs:])
 
 
 def as_row(column):
@@ -325,47 +324,43 @@
 def score_kernel(docs, positive, e0, e1, e2, e3, t0, t1, t2, t3, everyone, state, expos):
     all_docs, width = everyone.shape
     dp, _ = here()
-    y, z_lo = dp & 3, dp >> 2
+    y = dp & 3
+    group = e0.shape[0]
     for k, piece in enumerate((e0, e1, e2, e3)):
-        value = piece[...]
-        turned = jnp.concatenate([value[docs:], value[0:docs]], axis=0)
-        place = pl.multiple_of(((y + k) & 3) * 2 * docs, 2 * docs)
-        everyone[pl.ds(place, 2 * docs), :] = jnp.where(z_lo == 1, turned, value)
+        everyone[pl.ds(pl.multiple_of(((y + k) & 3) * group, group), group), :] = piece[...]
     tables = (t0, t1, t2, t3)
     rows = t0.shape[0]
     emb = thirds(everyone[...])
     scores = [folded(lax.dot_general(emb, t[...], NT, preferred_element_type=jnp.float32)) / TAU for t in tables]
     tops = [jnp.max(s, axis=1, keepdims=True) for s in scores]
     top = jnp.maximum(jnp.maximum(tops[0], tops[2]), jnp.maximum(tops[1], tops[3]))
-    row = lax.broadcasted_iota(jnp.int32, (all_docs, 128), 0)
-    wanted = jnp.zeros((all_docs, 128), jnp.int32)
+    row = lax.broadcasted_iota(jnp.int32, (all_docs, rows), 0)
+    wanted = jnp.zeros((all_docs, rows), jnp.int32)
     for doc in range(all_docs):
         z, rest = divmod(doc, all_docs // 2)
-        wanted = jnp.where(row == rest // docs * 2 * docs + z * docs + rest % docs, positive[doc], wanted)
+        wanted = jnp.where(row == rest // docs * group + z * docs + rest % docs, positive[doc], wanted)
     totals, found = [], jnp.zeros((all_docs, 1), jnp.float32)
     for k, s in enumerate(scores):
         expo = jnp.exp(s - top)
         expos[:, k * rows : (k + 1) * rows] = expo
-        halves = [jnp.sum(expo[:, h : h + rows // 2], axis=1, keepdims=True) for h in (0, rows // 2)]
-        totals.append(halves[0] + halves[1])
-        hit = row_ids(k, rows // 2, (all_docs, rows), 1) == wanted[:, 0:1]
+        totals.append(jnp.sum(expo, axis=1, keepdims=True))
+        hit = row_ids(k, (all_docs, rows), 1) == wanted
         found = found + jnp.sum(jnp.where(hit, s, 0.0), axis=1, keepdims=True)
     total = (totals[0] + totals[2]) + (totals[1] + totals[3])
-    place = pl.multiple_of(y * 2 * docs, 2 * docs)
-    mine = thirds(expos[pl.ds(place, 2 * docs), :])
-    mix = jnp.zeros((2 * docs, width), jnp.float32)
+    mine = thirds(expos[pl.ds(pl.multiple_of(y * group, group), group), :])
+    mix = jnp.zeros((group, width), jnp.float32)
     for k, t in enumerate(tables):
         mix = mix + folded(jnp.dot(mine[:, k * rows : (k + 1) * rows], t[...], preferred_element_type=jnp.float32))
-    column = lax.broadcasted_iota(jnp.int32, (docs, all_docs), 1)
-    own = column == lax.broadcasted_iota(jnp.int32, (docs, all_docs), 0) + y * 2 * docs + z_lo * docs
+    column = lax.broadcasted_iota(jnp.int32, (group, all_docs), 1)
+    own = column == lax.broadcasted_iota(jnp.int32, (group, all_docs), 0) + y * group
     total_row, top_row, found_row = as_row(total), as_row(top), as_row(found)
     state[...] = jnp.zeros_like(state)
-    state[0:docs, 0:width] = jnp.where(z_lo == 1, mix[docs:], mix[0:docs])
-    for place, row in ((width, total_row), (width + 128, top_row)):
-        value = jnp.sum(jnp.where(own, row, 0.0), axis=1, keepdims=True)
-        state[0:docs, place : place + 128] = jnp.broadcast_to(value, (docs, 128))
-    for index, row in enumerate((total_row, top_row, found_row)):
-        state[docs + index : docs + index + 1, 0:all_docs] = row
+    state[0:group, 0:width] = mix
+    for place, values in ((width, total_row), (width + 128, top_row)):
+        value = jnp.sum(jnp.where(own, values, 0.0), axis=1, keepdims=True)
+        state[0:group, place : place + 128] = jnp.broadcast_to(value, (group, 128))
+    for index, values in enumerate((total_row, top_row, found_row)):
+        state[group + index : group + index + 1, 0:all_docs] = values
 
 
 def merge(docs, width, states):
@@ -385,7 +380,7 @@
     return jnp.where(row == docs + 1, top_lane, joined)
 
 
-def batch_kernel(docs, emb, everyone, product_out, stats):
+def batch_kernel(emb, everyone, product_out, stats):
     everything = everyone[...]
     all_docs = everything.shape[0]
     own = lax.dot_general(emb[...], everything, NT, precision=HIGHEST, preferred_element_type=jnp.float32) / TAU
@@ -400,30 +395,31 @@
 
 
 def grad_kernel(
-    lengths, state, other, emb, rinv, everyone, target, product, stats, gain, normed, rstd, turned,
+    lengths, s0, s1, s2, s3, emb, rinv, everyone, target, product, stats, gain, normed, rstd, turned,
     send_out, d_summed, loss_out,
 ):
-    docs, width = target.shape
-    all_docs = everyone.shape[0]
+    docs, tb, width = normed.shape
+    all_docs, group = everyone.shape[0], emb.shape[0]
     dp, _ = here()
-    y, z_lo = dp & 3, dp >> 2
-    own, others = emb[0:docs], everyone[...]
-    now = merge(docs, width, [state[...], other[...]])
-    total, top, found = (now[docs + k : docs + k + 1, 0:all_docs] for k in range(3))
+    mine = lambda a: jnp.where(dp >= 4, a[docs:group], a[0:docs])
+    own, others = mine(emb), everyone[...]
+    now = merge(group, width, [s[...] for s in (s0, s1, s2, s3)])
+    total, top, found = (now[group + k : group + k + 1, 0:all_docs] for k in range(3))
     batch_top, batch_total = stats[0:1], stats[1:2]
     peak = jnp.maximum(top, batch_top)
     lse_row = peak + jnp.log(total * jnp.exp(top - peak) + batch_total * jnp.exp(batch_top - peak))
     loss_out[...] = jnp.broadcast_to(jnp.sum(lse_row - found, axis=1, keepdims=True) / all_docs, loss_out.shape)
     column = lax.broadcasted_iota(jnp.int32, (docs, all_docs), 1)
-    same = column == lax.broadcasted_iota(jnp.int32, (docs, all_docs), 0) + y * 2 * docs + z_lo * docs
+    first = (dp & 3) * group + (dp >> 2) * docs
+    same = column == lax.broadcasted_iota(jnp.int32, (docs, all_docs), 0) + first
     lse = jnp.sum(jnp.where(same, lse_row, 0.0), axis=1, keepdims=True)
-    scores = product[0:docs]
+    scores = mine(product)
     g_batch = jnp.where(same, 0.0, jnp.exp(scores - lse) + jnp.exp(scores - lse_row)) / all_docs
-    mix = now[0:docs, 0:width] * jnp.exp(now[0:docs, width + 128 : width + 129] - lse)
+    shares = mine(now)
+    mix = shares[:, 0:width] * jnp.exp(shares[:, width + 128 : width + 129] - lse)
     from_batch = jnp.dot(g_batch, others, precision=HIGHEST, preferred_element_type=jnp.float32)
-    d_emb = ((mix - target[...]) / all_docs + from_batch) / TAU
-    d_pooled = (d_emb - own * jnp.sum(own * d_emb, axis=1, keepdims=True)) * rinv[0:docs, 0:1]
-    tb = normed.shape[1]
+    d_emb = ((mix - mine(target)) / all_docs + from_batch) / TAU
+    d_pooled = (d_emb - own * jnp.sum(own * d_emb, axis=1, keepdims=True)) * mine(rinv)[:, 0:1]
     for doc in range(docs):
         dy = d_pooled[doc : doc + 1] / lengths[doc].astype(jnp.float32) * gain[...].reshape(1, width)
         level = dy - jnp.mean(dy, axis=1, keepdims=True)
@@ -467,14 +463,10 @@
         return left, lax.ppermute(part, "ctx", [((i + 1) % n_ctx, i) for i in range(n_ctx)])
 
     halos = [halo(tokens[0:CHUNK])]
-    swapped = swap(cache, "dp", 4)
+    tables = around(cache, from_y)
     gain = ln_gain
     qk, v_turned, w_v_turned, late = prepare(in_hbm(tokens), in_hbm(w_qkv))
-    swapped, late = lax.optimization_barrier((swapped, late))
     halos.append(halo(late))
-    rows = cache.shape[0]
-    table = call(stack_kernel, bf16(2 * rows, width), [VMEM, VMEM], VMEM, limit=4, name="stack")(cache, swapped)
-    tables = around(table, from_y)
     done = None
     for index, (left, right) in enumerate(halos):
         if index == 1:
@@ -482,8 +474,9 @@
             pool, after = lax.optimization_barrier((pool, positive))
             done = [*done, pool]
             target = call(
-                functools.partial(target_kernel, docs), f32(docs, width), [SMEM] + [VMEM] * 4, VMEM, name="target"
+                functools.partial(target_kernel, docs), f32(2 * docs, width), [SMEM] + [VMEM] * 4, VMEM, name="target"
             )(after, *tables)
+            left, target = lax.optimization_barrier((left, target))
         done = attend(
             index * CHUNK, done, lengths, tokens, left, right, qk, v_turned, w_qkv, w_v_turned, w_out, gain
         )
@@ -499,14 +492,15 @@
         name="turn",
     )(mixed)
 
-    sums = call(stack_kernel, f32(2 * docs, width), [VMEM, VMEM], VMEM, limit=4, name="stack")(
-        pool.reshape(docs, width), target
+    group = 2 * docs
+    sums = call(stack_kernel, f32(docs + group, width), [VMEM, VMEM], VMEM, limit=4, name="stack")(
+        pool, target
     )
     sums = add([sums, swap(sums, "ctx", 1)])
     sums = add(around(sums, from_x))
     emb, rinv, target = call(
         norm_kernel,
-        (f32(2 * docs, width), f32(2 * docs, 128), f32(docs, width)),
+        (f32(group, width), f32(group, 128), f32(group, width)),
         [VMEM] * 4,
         (VMEM,) * 3,
         limit=4,
@@ -515,7 +509,7 @@
     embs = around(emb, from_y)
     everyone, state = call(
         functools.partial(score_kernel, docs),
-        (f32(all_docs, width), f32(2 * docs, width + 256)),
+        (f32(all_docs, width), f32(2 * group, width + 256)),
         [SMEM] + [VMEM] * 8,
         (VMEM, VMEM),
         moved=2 * 2**20,
@@ -523,26 +517,26 @@
         name="score",
     )(positive, *embs, *tables)
     product, stats = call(
-        functools.partial(batch_kernel, docs),
-        (f32(2 * docs, all_docs), f32(8, all_docs)),
+        batch_kernel,
+        (f32(group, all_docs), f32(8, all_docs)),
         [VMEM, VMEM],
         (VMEM, VMEM),
         limit=4,
         name="batch",
     )(emb, everyone)
-    state = merged(docs, width, [state, swap(state, "ctx", 1)])
-    state = merged(docs, width, around(state, from_x))
+    state = merged(group, width, [state, swap(state, "ctx", 1)])
+    state = merged(group, width, around(state, from_x))
     half = width // 2
     send, d_summed, loss = call(
         grad_kernel,
         (f32(half, width), bf16(docs * tb, width), f32(8, 128)),
-        [SMEM] + [VMEM] * 12,
+        [SMEM] + [VMEM] * 14,
         (VMEM,) * 3,
         flops=docs * tb * width * width,
         moved=8 * 2**20,
         name="grad",
     )(
-        lengths, state, swap(state, "ctx", 2), emb, rinv, everyone, target, product, stats, gain, normed, rstd, turned,
+        lengths, *around(state, from_z), emb, rinv, everyone, target, product, stats, gain, normed, rstd, turned,
     )
     keep = call(
         keep_kernel,

time: 145 us -> 138 us (0.952)
  waiting for transfers between devices: 37.5 us -> 28.9 us
  starting transfers between devices: 61.5 us -> 63.3 us
    ppermute x5 -> x3, waiting for transfers between devices: 13.3 us -> 4.17 us  [swap(): lax.ppermute(value, axis, [(i, i ^ bits) for i in range(lax.axis_size(axi...]
    ppermute x2, starting transfers between devices: 5.67 us -> 11.1 us  [halo(): lax.ppermute(part, 'ctx', [((i + 1) % n_ctx, i) for i in range(n_ctx)])]
    ppermute x2, starting transfers between devices: 5.49 us -> 0.08 us  [halo(): lax.ppermute(part, 'ctx', [(i, (i + 1) % n_ctx) for i in range(n_ctx)])]
    ppermute x6, starting transfers between devices: 6.74 us -> 9.09 us  [from_y(): lax.ppermute(value, 'dp', [(d & 4 | d + k & 3, d) for d in range(lax.axis...]
    ppermute x5 -> x3, starting transfers between devices: 12.5 us -> 10.3 us  [swap(): lax.ppermute(value, axis, [(i, i ^ bits) for i in range(lax.axis_size(axi...]
    ppermute x6 -> x9, starting transfers between devices: 12 us -> 14.1 us  [from_z(): return lax.ppermute(value, ('dp', 'ctx'), pairs)]
    ppermute x6, waiting for transfers between devices: 4.46 us -> 2.9 us  [from_y(): lax.ppermute(value, 'dp', [(d & 4 | d + k & 3, d) for d in range(lax.axis...]
    ppermute x6 -> x9, waiting for transfers between devices: 6.11 us -> 7.11 us  [from_z(): return lax.ppermute(value, ('dp', 'ctx'), pairs)]
  transfers between devices with their start and end apart: 33 -> 34, of which waited for: 21 -> 22; matrix products, arithmetic and copies ran while one was open for 0% -> 0% of each run, Pallas kernels for 17% -> 18%
where the time goes in v4:
time: 138 us
  starting transfers between devices  63.3 us (46%)
  Pallas kernels  43.1 us (31%)
  waiting for transfers between devices  28.9 us (21%)
  local copies, waits for them, and re-layouts  1.74 us (1%)
    pallas_call x2, Pallas kernels, attend(): call(functools.partial(attend_kernel, first), out_shape, in_specs, (at(tb...  26.8 us
    ppermute x9, starting transfers between devices, from_z(): return lax.ppermute(value, ('dp', 'ctx'), pairs)  14.1 us
    ppermute x2, starting transfers between devices, halo(): lax.ppermute(part, 'ctx', [((i + 1) % n_ctx, i) for i in range(n_ctx)])  11.1 us
    ppermute x3, starting transfers between devices, swap(): lax.ppermute(value, axis, [(i, i ^ bits) for i in range(lax.axis_size(axi...  10.3 us
    ppermute x6, starting transfers between devices, from_x(): lax.ppermute(value, 'ctx', [((c + 4 * k) % size, c) for c in range(size)])  9.87 us
    ppermute x6, starting transfers between devices, from_y(): lax.ppermute(value, 'dp', [(d & 4 | d + k & 3, d) for d in range(lax.axis...  9.09 us
    ppermute x6, starting transfers between devices, from_plane(): return lax.ppermute(value, ('dp', 'ctx'), pairs)  8.8 us
    ppermute x6, waiting for transfers between devices, from_plane(): return lax.ppermute(value, ('dp', 'ctx'), pairs)  7.82 us
  transfers between devices with their start and end apart: 34, of which 22 were waited for; matrix products, arithmetic and copies ran while one was open for 0% of the time, Pallas kernels for 18%

profile of v4, /device:TPU:0, one launch (start us, length us, event | category | flops | bytes accessed | tf_op | source)
XLA Modules:
  0.0 137.9 jit_solution(9347043277557015316)
XLA Ops:
  0.6 1.2 slice.6
  1.9 5.7 %collective-permute-start.2 = (bf16[2,256,768]{2,1,0:T(8,128)(2,1)S(1)}, bf16[2,256,768]{2,1,0:T(8,128)(2,1)S(1)}, u32[]{:S(2)}, u32[]{:S(2)}) collective-permute-start(bf16[2,256,768]{2,1,0:T(8,128)(2,1)S(1)} %slice.6), channel_id=1, source_target_pairs={{1,0},{2,1},{3,2},{4,3},{5,4},{6,5},{7,6},{8,7},{9,8},{10,9},{11,1... | collective-permute-start | bytes 2359304 | tf_op jit(solution)/shard_map/ppermute | solution.py:463
  7.5 7.3 %prepare.1 = (bf16[4,256,1536]{2,1,0:T(8,128)(2,1)S(1)}, bf16[768,1024]{1,0:T(8,128)(2,1)S(1)}, bf16[768,768]{1,0:T(8,128)(2,1)S(1)}, bf16[2,256,768]{2,1,0:T(8,128)(2,1)S(1)}) custom-call(bf16[4,256,768]{2,1,0:T(8,128)(2,1)} %tok.5, bf16[768,2304]{1,0:T(8,128)(2,1)} %w_k.3), custom_call_target="tpu_custom_call" | custom-call | flops 3623878656 | bytes 11534336 | tf_op jit(solution)/shard_map/prepare/pallas_call | solution.py:222
  14.9 5.4 %collective-permute-start.6 = (bf16[2,256,768]{2,1,0:T(8,128)(2,1)S(1)}, bf16[2,256,768]{2,1,0:T(8,128)(2,1)S(1)}, u32[]{:S(2)}, u32[]{:S(2)}) collective-permute-start(bf16[2,256,768]{2,1,0:T(8,128)(2,1)S(1)} %get-tuple-element.43), channel_id=1, source_target_pairs={{1,0},{2,1},{3,2},{4,3},{5,4},{6,5},{7,6},{8,7},{9,8},{10,9},{11,1... | collective-permute-start | bytes 2359304 | tf_op jit(solution)/shard_map/ppermute | solution.py:463
  20.3 1.6 %collective-permute-start.5 = (bf16[128,768]{1,0:T(8,128)(2,1)S(1)}, bf16[128,768]{1,0:T(8,128)(2,1)S(1)}, u32[]{:S(2)}, u32[]{:S(2)}) collective-permute-start(bf16[128,768]{1,0:T(8,128)(2,1)S(1)} %copy-done.3), channel_id=1, source_target_pairs={{48,0},{0,16},{16,32},{32,48},{112,64},{64,80},{80,96},{96,112},{4... | collective-permute-start | bytes 589832 | tf_op jit(solution)/shard_map/ppermute | solution.py:34
  21.9 2.9 %collective-permute-start.4 = (bf16[128,768]{1,0:T(8,128)(2,1)S(1)}, bf16[128,768]{1,0:T(8,128)(2,1)S(1)}, u32[]{:S(2)}, u32[]{:S(2)}) collective-permute-start(bf16[128,768]{1,0:T(8,128)(2,1)S(1)} %copy-done.3), channel_id=1, source_target_pairs={{32,0},{48,16},{0,32},{16,48},{96,64},{112,80},{64,96},{80,112},{3... | collective-permute-start | bytes 589832 | tf_op jit(solution)/shard_map/ppermute | solution.py:34
  24.8 1.3 collective-permute-start.3
  26.2 13.4 %attend.2 = (bf16[4,256,768]{2,1,0:T(8,128)(2,1)}, bf16[768,1024]{1,0:T(8,128)(2,1)S(1)}, bf16[4,256,768]{2,1,0:T(8,128)(2,1)S(1)}, f32[4,256,128]{2,1,0:T(8,128)S(1)}, f32[4,1,768]{2,1,0:T(1,128)S(1)}) custom-call(s32[4]{0:T(128)S(1)} %copy-done.5, bf16[4,256,768]{2,1,0:T(8,128)(2,1)S(1)} %copy-done.1, ...), custom_call_target="tpu_custom_call" | custom-call | flops 3019898880 | bytes 8388608 | tf_op jit(solution)/shard_map/attend/pallas_call | solution.py:188
  40.4 13.4 %attend.3 = (bf16[4,256,768]{2,1,0:T(8,128)(2,1)}, bf16[768,1024]{1,0:T(8,128)(2,1)S(1)}, bf16[4,256,768]{2,1,0:T(8,128)(2,1)S(1)}, f32[4,256,128]{2,1,0:T(8,128)S(1)}, f32[4,1,768]{2,1,0:T(1,128)S(1)}) custom-call(s32[4]{0:T(128)S(1)} %copy-done.5, ...), custom_call_target="tpu_custom_call", output_to_operand_aliasing={{0}: (10, {}), {1}: (11, {}), {2}: (12, {}), {3}: (13, {}),... | custom-call | flops 3019898880 | bytes 8388608 | tf_op jit(solution)/shard_map/attend/pallas_call | solution.py:188
  53.8 10.2 %collective-permute-start.7 = (f32[12,768]{1,0:T(8,128)S(1)}, f32[12,768]{1,0:T(8,128)S(1)}, u32[]{:S(2)}, u32[]{:S(2)}) collective-permute-start(f32[12,768]{1,0:T(8,128)S(1)} %stack.1.refs_0_), channel_id=1, source_target_pairs={{0,1},{1,0},{2,3},{3,2},{4,5},{5,4},{6,7},{7,6},{8,9},{9,8},{10,11... | collective-permute-start | bytes 110600 | tf_op jit(solution)/shard_map/ppermute | solution.py:25
  63.9 0.9 collective-permute-done.7.refs_1_
  64.8 1.5 %collective-permute-start.10 = (f32[12,768]{1,0:T(8,128)S(1)}, f32[12,768]{1,0:T(8,128)S(1)}, u32[]{:S(2)}, u32[]{:S(2)}) collective-permute-start(f32[12,768]{1,0:T(8,128)S(1)} %add.3.refs_0_), channel_id=1, source_target_pairs={{12,0},{13,1},{14,2},{15,3},{0,4},{1,5},{2,6},{3,7},{4,8},{5,9},{6... | collective-permute-start | bytes 110600 | tf_op jit(solution)/shard_map/ppermute | solution.py:30
  66.3 2.7 %collective-permute-start.9 = (f32[12,768]{1,0:T(8,128)S(1)}, f32[12,768]{1,0:T(8,128)S(1)}, u32[]{:S(2)}, u32[]{:S(2)}) collective-permute-start(f32[12,768]{1,0:T(8,128)S(1)} %add.3.refs_0_), channel_id=1, source_target_pairs={{8,0},{9,1},{10,2},{11,3},{12,4},{13,5},{14,6},{15,7},{0,8},{1,9},... | collective-permute-start | bytes 110600 | tf_op jit(solution)/shard_map/ppermute | solution.py:30
  69.1 1.4 %collective-permute-start.8 = (f32[12,768]{1,0:T(8,128)S(1)}, f32[12,768]{1,0:T(8,128)S(1)}, u32[]{:S(2)}, u32[]{:S(2)}) collective-permute-start(f32[12,768]{1,0:T(8,128)S(1)} %add.3.refs_0_), channel_id=1, source_target_pairs={{4,0},{5,1},{6,2},{7,3},{8,4},{9,5},{10,6},{11,7},{12,8},{13,9},{1... | collective-permute-start | bytes 110600 | tf_op jit(solution)/shard_map/ppermute | solution.py:30
  70.5 1.7 %collective-permute-done.9.refs_2_ = f32[12,768]{1,0:T(8,128)S(1)} collective-permute-done((f32[12,768]{1,0:T(8,128)S(1)}, f32[12,768]{1,0:T(8,128)S(1)}, u32[]{:S(2)}, u32[]{:S(2)}) %collective-permute-start.9) | collective-permute-done | bytes 36896 | tf_op jit(solution)/shard_map/ppermute | solution.py:30
  72.2 1.0 collective-permute-done.8.refs_1_
  73.2 1.1 collective-permute-start.13
  74.3 3.5 %collective-permute-start.12 = (f32[12,768]{1,0:T(8,128)S(1)}, f32[12,768]{1,0:T(8,128)S(1)}, u32[]{:S(2)}, u32[]{:S(2)}) collective-permute-start(f32[12,768]{1,0:T(8,128)S(1)} %add.4.s0), channel_id=1, source_target_pairs={{2,0},{3,1},{0,2},{1,3},{6,4},{7,5},{4,6},{5,7},{10,8},{11,9},{8,1... | collective-permute-start | bytes 110600 | tf_op jit(solution)/shard_map/ppermute | solution.py:44
  77.8 1.0 collective-permute-start.11
  78.8 1.6 %collective-permute-done.12.s2 = f32[12,768]{1,0:T(8,128)S(1)} collective-permute-done((f32[12,768]{1,0:T(8,128)S(1)}, f32[12,768]{1,0:T(8,128)S(1)}, u32[]{:S(2)}, u32[]{:S(2)}) %collective-permute-start.12) | collective-permute-done | bytes 36896 | tf_op jit(solution)/shard_map/ppermute | solution.py:44
  80.4 1.5 %collective-permute-done.11.s1 = f32[12,768]{1,0:T(8,128)S(1)} collective-permute-done((f32[12,768]{1,0:T(8,128)S(1)}, f32[12,768]{1,0:T(8,128)S(1)}, u32[]{:S(2)}, u32[]{:S(2)}) %collective-permute-start.11) | collective-permute-done | bytes 36896 | tf_op jit(solution)/shard_map/ppermute | solution.py:44
  82.0 2.2 %collective-permute-start.15 = (f32[8,768]{1,0:T(8,128)S(1)}, f32[8,768]{1,0:T(8,128)S(1)}, u32[]{:S(2)}, u32[]{:S(2)}) collective-permute-start(f32[8,768]{1,0:T(8,128)S(1)} %get-tuple-element.58.e0.emb), channel_id=1, source_target_pairs={{32,0},{48,16},{0,32},{16,48},{96,64},{112,80},{64,96},{80,112},{3... | collective-permute-start | bytes 73736 | tf_op jit(solution)/shard_map/ppermute | solution.py:34
  84.2 1.1 collective-permute-start.14
  85.3 1.8 %collective-permute-done.16.e3 = f32[8,768]{1,0:T(8,128)S(1)} collective-permute-done((f32[8,768]{1,0:T(8,128)S(1)}, f32[8,768]{1,0:T(8,128)S(1)}, u32[]{:S(2)}, u32[]{:S(2)}) %collective-permute-start.16) | collective-permute-done | bytes 24608 | tf_op jit(solution)/shard_map/ppermute | solution.py:34
  87.4 0.7 collective-permute-done.14.e1
  88.2 1.3 score.1
  89.5 1.2 collective-permute-done.17.refs_1_
  91.4 3.7 %collective-permute-start.19 = (f32[16,1024]{1,0:T(8,128)S(1)}, f32[16,1024]{1,0:T(8,128)S(1)}, u32[]{:S(2)}, u32[]{:S(2)}) collective-permute-start(f32[16,1024]{1,0:T(8,128)S(1)} %merge.2.refs_0_), channel_id=1, source_target_pairs={{8,0},{9,1},{10,2},{11,3},{12,4},{13,5},{14,6},{15,7},{0,8},{1,9},... | collective-permute-start | bytes 196616 | tf_op jit(solution)/shard_map/ppermute | solution.py:30
  95.1 1.3 collective-permute-done.20.refs_3_
  96.4 2.2 %collective-permute-done.19.refs_2_ = f32[16,1024]{1,0:T(8,128)S(1)} collective-permute-done((f32[16,1024]{1,0:T(8,128)S(1)}, f32[16,1024]{1,0:T(8,128)S(1)}, u32[]{:S(2)}, u32[]{:S(2)}) %collective-permute-start.19) | collective-permute-done | bytes 65568 | tf_op jit(solution)/shard_map/ppermute | solution.py:30
  98.6 0.7 collective-permute-done.18.refs_1_
  99.6 3.6 %collective-permute-start.22 = (f32[16,1024]{1,0:T(8,128)S(1)}, f32[16,1024]{1,0:T(8,128)S(1)}, u32[]{:S(2)}, u32[]{:S(2)}) collective-permute-start(f32[16,1024]{1,0:T(8,128)S(1)} %merge.3.s0), channel_id=1, source_target_pairs={{2,0},{3,1},{0,2},{1,3},{6,4},{7,5},{4,6},{5,7},{10,8},{11,9},{8,1... | collective-permute-start | bytes 196616 | tf_op jit(solution)/shard_map/ppermute | solution.py:44
  103.7 2.1 %turn.1.turned = bf16[768,1024]{1,0:T(8,128)(2,1)S(1)} custom-call(bf16[768,1024]{1,0:T(8,128)(2,1)S(1)} %get-tuple-element.67.mixed), custom_call_target="tpu_custom_call" | custom-call | flops 1207959552 | bytes 4194304 | tf_op jit(solution)/shard_map/turn/pallas_call | solution.py:485
  106.1 1.3 collective-permute-done.21.s1
  107.5 2.6 %grad.1 = (f32[384,768]{1,0:T(8,128)S(1)}, bf16[1024,768]{1,0:T(8,128)(2,1)S(1)}, f32[8,128]{1,0:T(8,128)S(1)}) custom-call(s32[4]{0:T(128)S(1)} %copy-done.5, f32[16,1024]{1,0:T(8,128)S(1)} %merge.3.s0, f32[16,1024]{1,0:T(8,128)S(1)} %collective-permute-done.21.s1, f32[16,1024]{1,0:T(8,128)S(1)} %collective-permute-done.22.s2, ...), custom_call_target="tpu_custom_call" | custom-call | flops 603979776 | bytes 8388608 | tf_op jit(solution)/shard_map/grad/pallas_call | solution.py:530
  110.2 0.8 keep.1.refs_0_
  110.9 2.0 %collective-permute-done.24.refs_1_ = f32[384,768]{1,0:T(8,128)S(1)} collective-permute-done((f32[384,768]{1,0:T(8,128)S(1)}, f32[384,768]{1,0:T(8,128)S(1)}, u32[]{:S(2)}, u32[]{:S(2)}) %collective-permute-start.24) | collective-permute-done | bytes 1179680 | tf_op jit(solution)/shard_map/ppermute | solution.py:25
  113.2 1.8 %collective-permute-start.25 = (bf16[96,768]{1,0:T(8,128)(2,1)S(1)}, bf16[96,768]{1,0:T(8,128)(2,1)S(1)}, u32[]{:S(2)}, u32[]{:S(2)}) collective-permute-start(bf16[96,768]{1,0:T(8,128)(2,1)S(1)} %get-tuple-element.72), channel_id=1, source_target_pairs={{48,0},{13,1},{50,2},{15,3},{52,4},{1,5},{54,6},{3,7},{56,8},{5,9}... | collective-permute-start | bytes 442376 | tf_op jit(solution)/shard_map/ppermute | solution.py:55
  115.0 2.1 %collective-permute-start.26 = (bf16[96,768]{1,0:T(8,128)(2,1)S(1)}, bf16[96,768]{1,0:T(8,128)(2,1)S(1)}, u32[]{:S(2)}, u32[]{:S(2)}) collective-permute-start(bf16[96,768]{1,0:T(8,128)(2,1)S(1)} %get-tuple-element.73), channel_id=1, source_target_pairs={{32,0},{9,1},{34,2},{11,3},{36,4},{13,5},{38,6},{15,7},{40,8},{1,9... | collective-permute-start | bytes 442376 | tf_op jit(solution)/shard_map/ppermute | solution.py:55
  117.8 1.8 %collective-permute-done.25.refs_1_ = bf16[96,768]{1,0:T(8,128)(2,1)S(1)} collective-permute-done((bf16[96,768]{1,0:T(8,128)(2,1)S(1)}, bf16[96,768]{1,0:T(8,128)(2,1)S(1)}, u32[]{:S(2)}, u32[]{:S(2)}) %collective-permute-start.25) | collective-permute-done | bytes 147488 | tf_op jit(solution)/shard_map/ppermute | solution.py:55
  119.6 2.2 %collective-permute-done.26.refs_2_ = bf16[96,768]{1,0:T(8,128)(2,1)S(1)} collective-permute-done((bf16[96,768]{1,0:T(8,128)(2,1)S(1)}, bf16[96,768]{1,0:T(8,128)(2,1)S(1)}, u32[]{:S(2)}, u32[]{:S(2)}) %collective-permute-start.26) | collective-permute-done | bytes 147488 | tf_op jit(solution)/shard_map/ppermute | solution.py:55
  122.4 3.1 %collective-permute-start.29 = (f32[24,768]{1,0:T(8,128)S(1)}, f32[24,768]{1,0:T(8,128)S(1)}, u32[]{:S(2)}, u32[]{:S(2)}) collective-permute-start(f32[24,768]{1,0:T(8,128)S(1)} %get-tuple-element.77), channel_id=1, source_target_pairs={{8,0},{33,1},{10,2},{35,3},{12,4},{37,5},{14,6},{39,7},{0,8},{41,9... | collective-permute-start | bytes 221192 | tf_op jit(solution)/shard_map/ppermute | solution.py:55
  125.5 1.0 collective-permute-start.30
  126.5 2.2 %collective-permute-done.28.refs_1_ = f32[24,768]{1,0:T(8,128)S(1)} collective-permute-done((f32[24,768]{1,0:T(8,128)S(1)}, f32[24,768]{1,0:T(8,128)S(1)}, u32[]{:S(2)}, u32[]{:S(2)}) %collective-permute-start.28) | collective-permute-done | bytes 73760 | tf_op jit(solution)/shard_map/ppermute | solution.py:55
  128.8 1.1 collective-permute-done.30.refs_3_
  130.4 3.1 %collective-permute-start.32 = (f32[6,768]{1,0:T(8,128)S(1)}, f32[6,768]{1,0:T(8,128)S(1)}, u32[]{:S(2)}, u32[]{:S(2)}) collective-permute-start(f32[6,768]{1,0:T(8,128)S(1)} %get-tuple-element.81), channel_id=1, source_target_pairs={{2,0},{3,1},{0,2},{1,3},{6,4},{7,5},{4,6},{5,7},{10,8},{11,9},{8,1... | collective-permute-start | bytes 55304 | tf_op jit(solution)/shard_map/ppermute | solution.py:44
  135.0 0.7 collective-permute-done.32.refs_2_
  135.7 1.6 %collective-permute-done.33.refs_3_ = f32[6,768]{1,0:T(8,128)S(1)} collective-permute-done((f32[6,768]{1,0:T(8,128)S(1)}, f32[6,768]{1,0:T(8,128)S(1)}, u32[]{:S(2)}, u32[]{:S(2)}) %collective-permute-start.33) | collective-permute-done | bytes 18464 | tf_op jit(solution)/shard_map/ppermute | solution.py:44
  (55 shorter events, 7.3 us)
Async XLA Ops:
  1.8 18.5 %copy-start.3 = (bf16[128,768]{1,0:T(8,128)(2,1)S(1)}, bf16[128,768]{1,0:T(8,128)(2,1)}, u32[]{:S(2)}) copy-start(bf16[128,768]{1,0:T(8,128)(2,1)} %t0.1) | copy-start | bytes 589828
  1.8 24.3 %copy-start.1 = (bf16[4,256,768]{2,1,0:T(8,128)(2,1)S(1)}, bf16[4,256,768]{2,1,0:T(8,128)(2,1)}, u32[]{:S(2)}) copy-start(bf16[4,256,768]{2,1,0:T(8,128)(2,1)} %tok.5) | copy-start | bytes 4718596
  1.8 24.3 %copy-start.2 = (bf16[768,768]{1,0:T(8,128)(2,1)S(1)}, bf16[768,768]{1,0:T(8,128)(2,1)}, u32[]{:S(2)}) copy-start(bf16[768,768]{1,0:T(8,128)(2,1)} %w_out.3) | copy-start | bytes 3538948
  1.9 24.3 %copy-start.4 = (f32[768]{0:T(1024)S(1)}, f32[768]{0:T(1024)}, u32[]{:S(2)}) copy-start(f32[768]{0:T(1024)} %gain.5) | copy-start | bytes 9220
  1.9 24.3 %copy-start.5 = (s32[4]{0:T(128)S(1)}, s32[4]{0:T(128)}, u32[]{:S(2)}) copy-start(s32[4]{0:T(128)} %lengths.5) | copy-start | bytes 52
  1.9 20.0 %collective-permute-start.2 = (bf16[2,256,768]{2,1,0:T(8,128)(2,1)S(1)}, bf16[2,256,768]{2,1,0:T(8,128)(2,1)S(1)}, u32[]{:S(2)}, u32[]{:S(2)}) collective-permute-start(bf16[2,256,768]{2,1,0:T(8,128)(2,1)S(1)} %slice.6), channel_id=1, source_target_pairs={{1,0},{2,1},{3,2},{4,3},{5,4},{6,5},{7,6},{8,7},{9,8},{10,9},{11,1... | collective-permute-start | bytes 2359304 | tf_op jit(solution)/shard_map/ppermute | solution.py:463
  7.5 17.3 %collective-permute-start.1 = (bf16[2,256,768]{2,1,0:T(8,128)(2,1)S(1)}, bf16[2,256,768]{2,1,0:T(8,128)(2,1)S(1)}, u32[]{:S(2)}, u32[]{:S(2)}) collective-permute-start(bf16[2,256,768]{2,1,0:T(8,128)(2,1)S(1)} %slice.6), channel_id=1, source_target_pairs={{0,1},{1,2},{2,3},{3,4},{4,5},{5,6},{6,7},{7,8},{8,9},{9,10},{10,1... | collective-permute-start | bytes 2359304 | tf_op jit(solution)/shard_map/ppermute | solution.py:462
  7.5 18.6 %copy-start = (bf16[768,2304]{1,0:T(8,128)(2,1)S(1)}, bf16[768,2304]{1,0:T(8,128)(2,1)}, u32[]{:S(2)}) copy-start(bf16[768,2304]{1,0:T(8,128)(2,1)} %w_k.3) | copy-start | bytes 10616836
  14.8 25.5 %collective-permute-start = (bf16[2,256,768]{2,1,0:T(8,128)(2,1)S(1)}, bf16[2,256,768]{2,1,0:T(8,128)(2,1)S(1)}, u32[]{:S(2)}, u32[]{:S(2)}) collective-permute-start(bf16[2,256,768]{2,1,0:T(8,128)(2,1)S(1)} %get-tuple-element.43), channel_id=1, source_target_pairs={{0,1},{1,2},{2,3},{3,4},{4,5},{5,6},{6,7},{7,8},{8,9},{9,10},{10,1... | collective-permute-start | bytes 2359304 | tf_op jit(solution)/shard_map/ppermute | solution.py:462
  14.9 25.5 %collective-permute-start.6 = (bf16[2,256,768]{2,1,0:T(8,128)(2,1)S(1)}, bf16[2,256,768]{2,1,0:T(8,128)(2,1)S(1)}, u32[]{:S(2)}, u32[]{:S(2)}) collective-permute-start(bf16[2,256,768]{2,1,0:T(8,128)(2,1)S(1)} %get-tuple-element.43), channel_id=1, source_target_pairs={{1,0},{2,1},{3,2},{4,3},{5,4},{6,5},{7,6},{8,7},{9,8},{10,9},{11,1... | collective-permute-start | bytes 2359304 | tf_op jit(solution)/shard_map/ppermute | solution.py:463
  20.3 19.3 %collective-permute-start.5 = (bf16[128,768]{1,0:T(8,128)(2,1)S(1)}, bf16[128,768]{1,0:T(8,128)(2,1)S(1)}, u32[]{:S(2)}, u32[]{:S(2)}) collective-permute-start(bf16[128,768]{1,0:T(8,128)(2,1)S(1)} %copy-done.3), channel_id=1, source_target_pairs={{48,0},{0,16},{16,32},{32,48},{112,64},{64,80},{80,96},{96,112},{4... | collective-permute-start | bytes 589832 | tf_op jit(solution)/shard_map/ppermute | solution.py:34
  21.9 17.7 %collective-permute-start.4 = (bf16[128,768]{1,0:T(8,128)(2,1)S(1)}, bf16[128,768]{1,0:T(8,128)(2,1)S(1)}, u32[]{:S(2)}, u32[]{:S(2)}) collective-permute-start(bf16[128,768]{1,0:T(8,128)(2,1)S(1)} %copy-done.3), channel_id=1, source_target_pairs={{32,0},{48,16},{0,32},{16,48},{96,64},{112,80},{64,96},{80,112},{3... | collective-permute-start | bytes 589832 | tf_op jit(solution)/shard_map/ppermute | solution.py:34
  24.8 14.8 %collective-permute-start.3 = (bf16[128,768]{1,0:T(8,128)(2,1)S(1)}, bf16[128,768]{1,0:T(8,128)(2,1)S(1)}, u32[]{:S(2)}, u32[]{:S(2)}) collective-permute-start(bf16[128,768]{1,0:T(8,128)(2,1)S(1)} %copy-done.3), channel_id=1, source_target_pairs={{16,0},{32,16},{48,32},{0,48},{80,64},{96,80},{112,96},{64,112},{1... | collective-permute-start | bytes 589832 | tf_op jit(solution)/shard_map/ppermute | solution.py:34
  26.2 13.4 %copy-start.6 = (s32[32]{0:T(128)S(1)}, s32[32]{0:T(128)}, u32[]{:S(2)}) copy-start(s32[32]{0:T(128)} %positive.2) | copy-start | bytes 388
  53.8 11.0 %collective-permute-start.7 = (f32[12,768]{1,0:T(8,128)S(1)}, f32[12,768]{1,0:T(8,128)S(1)}, u32[]{:S(2)}, u32[]{:S(2)}) collective-permute-start(f32[12,768]{1,0:T(8,128)S(1)} %stack.1.refs_0_), channel_id=1, source_target_pairs={{0,1},{1,0},{2,3},{3,2},{4,5},{5,4},{6,7},{7,6},{8,9},{9,8},{10,11... | collective-permute-start | bytes 110600 | tf_op jit(solution)/shard_map/ppermute | solution.py:25
  64.8 5.7 %collective-permute-start.10 = (f32[12,768]{1,0:T(8,128)S(1)}, f32[12,768]{1,0:T(8,128)S(1)}, u32[]{:S(2)}, u32[]{:S(2)}) collective-permute-start(f32[12,768]{1,0:T(8,128)S(1)} %add.3.refs_0_), channel_id=1, source_target_pairs={{12,0},{13,1},{14,2},{15,3},{0,4},{1,5},{2,6},{3,7},{4,8},{5,9},{6... | collective-permute-start | bytes 110600 | tf_op jit(solution)/shard_map/ppermute | solution.py:30
  66.3 5.8 %collective-permute-start.9 = (f32[12,768]{1,0:T(8,128)S(1)}, f32[12,768]{1,0:T(8,128)S(1)}, u32[]{:S(2)}, u32[]{:S(2)}) collective-permute-start(f32[12,768]{1,0:T(8,128)S(1)} %add.3.refs_0_), channel_id=1, source_target_pairs={{8,0},{9,1},{10,2},{11,3},{12,4},{13,5},{14,6},{15,7},{0,8},{1,9},... | collective-permute-start | bytes 110600 | tf_op jit(solution)/shard_map/ppermute | solution.py:30
  69.1 4.1 %collective-permute-start.8 = (f32[12,768]{1,0:T(8,128)S(1)}, f32[12,768]{1,0:T(8,128)S(1)}, u32[]{:S(2)}, u32[]{:S(2)}) collective-permute-start(f32[12,768]{1,0:T(8,128)S(1)} %add.3.refs_0_), channel_id=1, source_target_pairs={{4,0},{5,1},{6,2},{7,3},{8,4},{9,5},{10,6},{11,7},{12,8},{13,9},{1... | collective-permute-start | bytes 110600 | tf_op jit(solution)/shard_map/ppermute | solution.py:30
  73.2 5.7 %collective-permute-start.13 = (f32[12,768]{1,0:T(8,128)S(1)}, f32[12,768]{1,0:T(8,128)S(1)}, u32[]{:S(2)}, u32[]{:S(2)}) collective-permute-start(f32[12,768]{1,0:T(8,128)S(1)} %add.4.s0), channel_id=1, source_target_pairs={{66,0},{67,1},{64,2},{65,3},{70,4},{71,5},{68,6},{69,7},{74,8},{75... | collective-permute-start | bytes 110600 | tf_op jit(solution)/shard_map/ppermute | solution.py:44
  74.3 6.1 %collective-permute-start.12 = (f32[12,768]{1,0:T(8,128)S(1)}, f32[12,768]{1,0:T(8,128)S(1)}, u32[]{:S(2)}, u32[]{:S(2)}) collective-permute-start(f32[12,768]{1,0:T(8,128)S(1)} %add.4.s0), channel_id=1, source_target_pairs={{2,0},{3,1},{0,2},{1,3},{6,4},{7,5},{4,6},{5,7},{10,8},{11,9},{8,1... | collective-permute-start | bytes 110600 | tf_op jit(solution)/shard_map/ppermute | solution.py:44
  77.8 4.1 %collective-permute-start.11 = (f32[12,768]{1,0:T(8,128)S(1)}, f32[12,768]{1,0:T(8,128)S(1)}, u32[]{:S(2)}, u32[]{:S(2)}) collective-permute-start(f32[12,768]{1,0:T(8,128)S(1)} %add.4.s0), channel_id=1, source_target_pairs={{64,0},{65,1},{66,2},{67,3},{68,4},{69,5},{70,6},{71,7},{72,8},{73... | collective-permute-start | bytes 110600 | tf_op jit(solution)/shard_map/ppermute | solution.py:44
  82.0 5.0 %collective-permute-start.16 = (f32[8,768]{1,0:T(8,128)S(1)}, f32[8,768]{1,0:T(8,128)S(1)}, u32[]{:S(2)}, u32[]{:S(2)}) collective-permute-start(f32[8,768]{1,0:T(8,128)S(1)} %get-tuple-element.58.e0.emb), channel_id=1, source_target_pairs={{48,0},{0,16},{16,32},{32,48},{112,64},{64,80},{80,96},{96,112},{4... | collective-permute-start | bytes 73736 | tf_op jit(solution)/shard_map/ppermute | solution.py:34
  82.0 5.4 %collective-permute-start.15 = (f32[8,768]{1,0:T(8,128)S(1)}, f32[8,768]{1,0:T(8,128)S(1)}, u32[]{:S(2)}, u32[]{:S(2)}) collective-permute-start(f32[8,768]{1,0:T(8,128)S(1)} %get-tuple-element.58.e0.emb), channel_id=1, source_target_pairs={{32,0},{48,16},{0,32},{16,48},{96,64},{112,80},{64,96},{80,112},{3... | collective-permute-start | bytes 73736 | tf_op jit(solution)/shard_map/ppermute | solution.py:34
  84.2 4.0 %collective-permute-start.14 = (f32[8,768]{1,0:T(8,128)S(1)}, f32[8,768]{1,0:T(8,128)S(1)}, u32[]{:S(2)}, u32[]{:S(2)}) collective-permute-start(f32[8,768]{1,0:T(8,128)S(1)} %get-tuple-element.58.e0.emb), channel_id=1, source_target_pairs={{16,0},{32,16},{48,32},{0,48},{80,64},{96,80},{112,96},{64,112},{1... | collective-permute-start | bytes 73736 | tf_op jit(solution)/shard_map/ppermute | solution.py:34
  89.5 1.3 collective-permute-start.17
  90.9 5.5 %collective-permute-start.20 = (f32[16,1024]{1,0:T(8,128)S(1)}, f32[16,1024]{1,0:T(8,128)S(1)}, u32[]{:S(2)}, u32[]{:S(2)}) collective-permute-start(f32[16,1024]{1,0:T(8,128)S(1)} %merge.2.refs_0_), channel_id=1, source_target_pairs={{12,0},{13,1},{14,2},{15,3},{0,4},{1,5},{2,6},{3,7},{4,8},{5,9},{6... | collective-permute-start | bytes 196616 | tf_op jit(solution)/shard_map/ppermute | solution.py:30
  91.4 7.2 %collective-permute-start.19 = (f32[16,1024]{1,0:T(8,128)S(1)}, f32[16,1024]{1,0:T(8,128)S(1)}, u32[]{:S(2)}, u32[]{:S(2)}) collective-permute-start(f32[16,1024]{1,0:T(8,128)S(1)} %merge.2.refs_0_), channel_id=1, source_target_pairs={{8,0},{9,1},{10,2},{11,3},{12,4},{13,5},{14,6},{15,7},{0,8},{1,9},... | collective-permute-start | bytes 196616 | tf_op jit(solution)/shard_map/ppermute | solution.py:30
  95.1 4.3 %collective-permute-start.18 = (f32[16,1024]{1,0:T(8,128)S(1)}, f32[16,1024]{1,0:T(8,128)S(1)}, u32[]{:S(2)}, u32[]{:S(2)}) collective-permute-start(f32[16,1024]{1,0:T(8,128)S(1)} %merge.2.refs_0_), channel_id=1, source_target_pairs={{4,0},{5,1},{6,2},{7,3},{8,4},{9,5},{10,6},{11,7},{12,8},{13,9},{1... | collective-permute-start | bytes 196616 | tf_op jit(solution)/shard_map/ppermute | solution.py:30
  99.4 6.7 %collective-permute-start.23 = (f32[16,1024]{1,0:T(8,128)S(1)}, f32[16,1024]{1,0:T(8,128)S(1)}, u32[]{:S(2)}, u32[]{:S(2)}) collective-permute-start(f32[16,1024]{1,0:T(8,128)S(1)} %merge.3.s0), channel_id=1, source_target_pairs={{66,0},{67,1},{64,2},{65,3},{70,4},{71,5},{68,6},{69,7},{74,8},{75... | collective-permute-start | bytes 196616 | tf_op jit(solution)/shard_map/ppermute | solution.py:44
  99.6 6.6 %collective-permute-start.22 = (f32[16,1024]{1,0:T(8,128)S(1)}, f32[16,1024]{1,0:T(8,128)S(1)}, u32[]{:S(2)}, u32[]{:S(2)}) collective-permute-start(f32[16,1024]{1,0:T(8,128)S(1)} %merge.3.s0), channel_id=1, source_target_pairs={{2,0},{3,1},{0,2},{1,3},{6,4},{7,5},{4,6},{5,7},{10,8},{11,9},{8,1... | collective-permute-start | bytes 196616 | tf_op jit(solution)/shard_map/ppermute | solution.py:44
  103.2 4.3 %collective-permute-start.21 = (f32[16,1024]{1,0:T(8,128)S(1)}, f32[16,1024]{1,0:T(8,128)S(1)}, u32[]{:S(2)}, u32[]{:S(2)}) collective-permute-start(f32[16,1024]{1,0:T(8,128)S(1)} %merge.3.s0), channel_id=1, source_target_pairs={{64,0},{65,1},{66,2},{67,3},{68,4},{69,5},{70,6},{71,7},{72,8},{73... | collective-permute-start | bytes 196616 | tf_op jit(solution)/shard_map/ppermute | solution.py:44
  110.1 2.9 %collective-permute-start.24 = (f32[384,768]{1,0:T(8,128)S(1)}, f32[384,768]{1,0:T(8,128)S(1)}, u32[]{:S(2)}, u32[]{:S(2)}) collective-permute-start(f32[384,768]{1,0:T(8,128)S(1)} %get-tuple-element.70), channel_id=1, source_target_pairs={{0,1},{1,0},{2,3},{3,2},{4,5},{5,4},{6,7},{7,6},{8,9},{9,8},{10,11... | collective-permute-start | bytes 3538952 | tf_op jit(solution)/shard_map/ppermute | solution.py:25
  113.2 6.4 %collective-permute-start.25 = (bf16[96,768]{1,0:T(8,128)(2,1)S(1)}, bf16[96,768]{1,0:T(8,128)(2,1)S(1)}, u32[]{:S(2)}, u32[]{:S(2)}) collective-permute-start(bf16[96,768]{1,0:T(8,128)(2,1)S(1)} %get-tuple-element.72), channel_id=1, source_target_pairs={{48,0},{13,1},{50,2},{15,3},{52,4},{1,5},{54,6},{3,7},{56,8},{5,9}... | collective-permute-start | bytes 442376 | tf_op jit(solution)/shard_map/ppermute | solution.py:55
  115.0 6.8 %collective-permute-start.26 = (bf16[96,768]{1,0:T(8,128)(2,1)S(1)}, bf16[96,768]{1,0:T(8,128)(2,1)S(1)}, u32[]{:S(2)}, u32[]{:S(2)}) collective-permute-start(bf16[96,768]{1,0:T(8,128)(2,1)S(1)} %get-tuple-element.73), channel_id=1, source_target_pairs={{32,0},{9,1},{34,2},{11,3},{36,4},{13,5},{38,6},{15,7},{40,8},{1,9... | collective-permute-start | bytes 442376 | tf_op jit(solution)/shard_map/ppermute | solution.py:55
  117.1 5.1 %collective-permute-start.27 = (bf16[96,768]{1,0:T(8,128)(2,1)S(1)}, bf16[96,768]{1,0:T(8,128)(2,1)S(1)}, u32[]{:S(2)}, u32[]{:S(2)}) collective-permute-start(bf16[96,768]{1,0:T(8,128)(2,1)S(1)} %get-tuple-element.74), channel_id=1, source_target_pairs={{16,0},{5,1},{18,2},{7,3},{20,4},{9,5},{22,6},{11,7},{24,8},{13,9}... | collective-permute-start | bytes 442376 | tf_op jit(solution)/shard_map/ppermute | solution.py:55
  122.3 6.4 %collective-permute-start.28 = (f32[24,768]{1,0:T(8,128)S(1)}, f32[24,768]{1,0:T(8,128)S(1)}, u32[]{:S(2)}, u32[]{:S(2)}) collective-permute-start(f32[24,768]{1,0:T(8,128)S(1)} %get-tuple-element.76), channel_id=1, source_target_pairs={{12,0},{49,1},{14,2},{51,3},{0,4},{53,5},{2,6},{55,7},{4,8},{57,9}... | collective-permute-start | bytes 221192 | tf_op jit(solution)/shard_map/ppermute | solution.py:55
  122.4 6.3 %collective-permute-start.29 = (f32[24,768]{1,0:T(8,128)S(1)}, f32[24,768]{1,0:T(8,128)S(1)}, u32[]{:S(2)}, u32[]{:S(2)}) collective-permute-start(f32[24,768]{1,0:T(8,128)S(1)} %get-tuple-element.77), channel_id=1, source_target_pairs={{8,0},{33,1},{10,2},{35,3},{12,4},{37,5},{14,6},{39,7},{0,8},{41,9... | collective-permute-start | bytes 221192 | tf_op jit(solution)/shard_map/ppermute | solution.py:55
  125.5 4.4 %collective-permute-start.30 = (f32[24,768]{1,0:T(8,128)S(1)}, f32[24,768]{1,0:T(8,128)S(1)}, u32[]{:S(2)}, u32[]{:S(2)}) collective-permute-start(f32[24,768]{1,0:T(8,128)S(1)} %get-tuple-element.78), channel_id=1, source_target_pairs={{4,0},{17,1},{6,2},{19,3},{8,4},{21,5},{10,6},{23,7},{12,8},{25,9}... | collective-permute-start | bytes 221192 | tf_op jit(solution)/shard_map/ppermute | solution.py:55
  129.9 5.1 %collective-permute-start.31 = (f32[6,768]{1,0:T(8,128)S(1)}, f32[6,768]{1,0:T(8,128)S(1)}, u32[]{:S(2)}, u32[]{:S(2)}) collective-permute-start(f32[6,768]{1,0:T(8,128)S(1)} %get-tuple-element.80), channel_id=1, source_target_pairs={{66,0},{67,1},{64,2},{65,3},{70,4},{71,5},{68,6},{69,7},{74,8},{75... | collective-permute-start | bytes 55304 | tf_op jit(solution)/shard_map/ppermute | solution.py:44
  130.4 5.3 %collective-permute-start.32 = (f32[6,768]{1,0:T(8,128)S(1)}, f32[6,768]{1,0:T(8,128)S(1)}, u32[]{:S(2)}, u32[]{:S(2)}) collective-permute-start(f32[6,768]{1,0:T(8,128)S(1)} %get-tuple-element.81), channel_id=1, source_target_pairs={{2,0},{3,1},{0,2},{1,3},{6,4},{7,5},{4,6},{5,7},{10,8},{11,9},{8,1... | collective-permute-start | bytes 55304 | tf_op jit(solution)/shard_map/ppermute | solution.py:44
  133.5 3.8 %collective-permute-start.33 = (f32[6,768]{1,0:T(8,128)S(1)}, f32[6,768]{1,0:T(8,128)S(1)}, u32[]{:S(2)}, u32[]{:S(2)}) collective-permute-start(f32[6,768]{1,0:T(8,128)S(1)} %get-tuple-element.82), channel_id=1, source_target_pairs={{64,0},{65,1},{66,2},{67,3},{68,4},{69,5},{70,6},{71,7},{72,8},{73... | collective-permute-start | bytes 55304 | tf_op jit(solution)/shard_map/ppermute | solution.py:44
